TPU v7x, 256 devices: a whole 4x4x8 slice. The times are simulated.
256 devices in a mesh: leaf: 128 (over y, z, x), sub: 2 (over core).
Axes of the slice: x: 4, y: 4, z: 8, core: 2. Of those that a mesh axis runs over, the one named last changes fastest.
Arguments:
- coords: float32 [3, 2097152], P(None, ('leaf', 'sub')), may hold values from 0 to 1
- vectors: bfloat16 [2097152, 64], P(('leaf', 'sub')), may hold values from -6 to 6
- bases: bfloat16 [32768, 64, 64], P(('leaf', 'sub')), may hold values from -0.75 to 0.75
- transfer: bfloat16 [256, 254, 64, 64], P(('leaf', 'sub')), may hold values from -0.5234375 to 0.5234375
- coupling: bfloat16 [256, 31, 64, 64], P(('leaf', 'sub')), may hold values from -0.75 to 0.75
- top_transfer: bfloat16 [508, 64, 64], replicated, may hold values from -0.5234375 to 0.5234375
- top_coupling: bfloat16 [255, 64, 64], replicated, may hold values from -0.75 to 0.75
Outputs:
- product: float32 [2097152, 64], P(('leaf', 'sub'))
All inputs are finite; a program needn't handle non-finite values.
Results may differ from a plain program's by a relative error of at most 0.0029.
Values sent between devices are 32-bit elements; how exact they have to be, the bound alone decides.
No kernel may reach another device: no remote copies, remote signals or barrier semaphores. Data moves between devices by JAX's collectives and lax.ppermute only.
A program may use at most 128 MiB of HBM per device.

v0:
```python
import functools

import jax
import jax.numpy as jnp
from jax import lax
from jax.experimental import pallas as pl
from jax.experimental.pallas import tpu as pltpu
from jax.sharding import PartitionSpec as P

F32 = jnp.float32
BF16 = jnp.bfloat16
VMEM = pltpu.VMEM
AXES = ("leaf", "sub")
HIGH = lax.Precision.HIGHEST

STEP = 136
NN = (((1,), (0,)), ((), ()))
NT = (((1,), (1,)), ((), ()))
TN = (((0,), (0,)), ((), ()))
LEVEL_AT = (None, 0, 4096, 6144, 7168, 7680, 7936)
NODE_AT = (0, 128, 192, 224, 240, 248, 252)
NUGGET_DIAG = 1.5
CHORD = 2.0 * 1.4426950408889634


def mxu(a, b, dims):
    return lax.dot_general(a, b, dims, preferred_element_type=F32)


def split(c):
    hi = c.astype(BF16)
    lo = (c - hi.astype(F32)).astype(BF16)
    return jnp.concatenate([hi, lo], 0)


def fold(t):
    half = t.shape[0] // 2
    return t[:half] + t[half:]


def picker(bit):
    row = lax.broadcasted_iota(jnp.int32, (128, 256), 0)
    col = lax.broadcasted_iota(jnp.int32, (128, 256), 1)
    return jnp.where(col == row + 128 * ((row >> bit) & 1), 1.0, 0.0).astype(BF16)


def spread(src, width, lane0, pick, slab):
    for i in range(32):
        parts = []
        for u in range(2):
            w = src[2 * i + u, :, lane0 : lane0 + width]
            if width < 128:
                w = jnp.concatenate([w, jnp.zeros((64, 128 - width), BF16)], 1)
            z = jnp.zeros_like(w)
            parts += [jnp.concatenate([w, z], 1), jnp.concatenate([z, w], 1)]
        out = mxu(pick, jnp.concatenate(parts, 0), NT)
        for u in range(2):
            slab[pl.ds((2 * i + u) * STEP, 128), :] = out[:, 128 * u : 128 * u + 128]


def box_matrix(slab, box):
    return slab[pl.ds(box, 64, stride=STEP), :]


def up_kernel(
    bases_h, vectors_h, transfer_h, own_out, levels_h, pairs_h, quads_h,
    bases, vectors, transfer, slab0, slab1, leaf_coef, levels, pairs, quads, sems,
):
    loads = [
        pltpu.make_async_copy(a, b, sems.at[i])
        for i, (a, b) in enumerate(
            [(bases_h, bases), (vectors_h, vectors), (transfer_h, transfer)]
        )
    ]
    for copy in loads:
        copy.start()
    pick_pair = picker(0)
    pick_quad = picker(1)
    loads[0].wait()
    spread(bases, 128, 0, pick_pair, slab0)
    loads[1].wait()
    for j in range(64):
        pair = jnp.concatenate(
            [box_matrix(slab0, 2 * j), box_matrix(slab0, 2 * j + 1)], 0
        ).astype(BF16)
        pairs[j] = pair
        leaf_coef[:, 128 * j : 128 * j + 128] = mxu(
            vectors[:, 128 * j : 128 * j + 128], pair, NN
        )
    store_pairs = pltpu.make_async_copy(pairs, pairs_h, sems.at[3])
    store_pairs.start()
    loads[2].wait()
    spread(transfer, 128, 0, pick_quad, slab1)
    spread(transfer, 126, 128, pick_quad, slab0)
    for level in range(6):
        count = 128 >> level
        for q in range(count // 4):
            first = NODE_AT[level] + 4 * q
            slab = slab1 if first < 128 else slab0
            quad = jnp.concatenate(
                [box_matrix(slab, (first + u) % 128) for u in range(4)], 0
            ).astype(BF16)
            quads[first // 4] = quad
            if level == 0:
                coef = leaf_coef[:, 256 * q : 256 * q + 256]
            else:
                at = LEVEL_AT[level] + 256 * q
                coef = levels[:, at : at + 256]
            at = LEVEL_AT[level + 1] + 128 * q
            levels[:, at : at + 128] = fold(mxu(split(coef), quad, NN))
    last = jnp.concatenate([box_matrix(slab0, 124), box_matrix(slab0, 125)], 0).astype(BF16)
    quads[63, :128, :] = last
    quads[63, 128:, :] = jnp.zeros((128, 128), BF16)
    store_levels = pltpu.make_async_copy(levels, levels_h, sems.at[4])
    store_quads = pltpu.make_async_copy(quads, quads_h, sems.at[5])
    store_levels.start()
    store_quads.start()
    at = LEVEL_AT[6]
    own_out[...] = fold(mxu(split(levels[:, at : at + 128]), last, NN))[:, :64]
    store_pairs.wait()
    store_levels.wait()
    store_quads.wait()


def upward(bases, vectors, transfer):
    return pl.pallas_call(
        up_kernel,
        out_shape=[
            jax.ShapeDtypeStruct((64, 64), F32),
            jax.ShapeDtypeStruct((64, 8064), F32),
            jax.ShapeDtypeStruct((64, 128, 128), BF16),
            jax.ShapeDtypeStruct((64, 256, 128), BF16),
        ],
        in_specs=[pl.BlockSpec(memory_space=pl.ANY)] * 3,
        out_specs=[pl.BlockSpec(memory_space=VMEM)] + [pl.BlockSpec(memory_space=pl.ANY)] * 3,
        scratch_shapes=[
            VMEM((64, 64, 128), BF16),
            VMEM((64, 8192), BF16),
            VMEM((64, 64, 254), BF16),
            VMEM((64 * STEP, 128), F32),
            VMEM((64 * STEP, 128), F32),
            VMEM((64, 8192), F32),
            VMEM((64, 8064), F32),
            VMEM((64, 128, 128), BF16),
            VMEM((64, 256, 128), BF16),
            pltpu.SemaphoreType.DMA((6,)),
        ],
        compiler_params=pltpu.CompilerParams(vmem_limit_bytes=58 * 2**20),
        cost_estimate=pl.CostEstimate(flops=10**9, bytes_accessed=8 * 2**20, transcendentals=0),
        name="upward",
    )(bases, vectors, transfer)


def top_kernel(device, transfer, coupling, own_out, sib_out, fields_out, slab, slab2):
    dev = device[0]
    row = lax.broadcasted_iota(jnp.int32, (16, 508), 0)
    col = lax.broadcasted_iota(jnp.int32, (16, 508), 1)
    height = row & 7
    want = 512 - (512 >> height) + (jnp.full_like(row, dev) >> height)
    want = jnp.where(row >= 8, want ^ 1, want)
    pick = jnp.where((col == want) & (height < 7), 1.0, 0.0).astype(BF16)
    crow = lax.broadcasted_iota(jnp.int32, (16, 255), 0)
    ccol = lax.broadcasted_iota(jnp.int32, (16, 255), 1)
    cwant = 256 - (256 >> crow) + (jnp.full_like(crow, dev) >> (crow + 1))
    cpick = jnp.where((ccol == cwant) & (crow < 8), 1.0, 0.0).astype(BF16)
    for i in range(64):
        slab[pl.ds(i * 24, 16), :64] = mxu(pick, transfer[i], NT)
        slab2[pl.ds(i * 24, 16), :64] = mxu(cpick, coupling[i], NT)
    chain = None
    for level in range(8):
        pair = slab2[pl.ds(level, 64, stride=24), :][:, :64]
        odd = (dev >> level) & 1
        turned = jnp.where(odd == 1, pair, pair.T).astype(BF16)
        if level == 0:
            fields_out[0] = turned.astype(F32)
        else:
            hi = chain.astype(BF16)
            lo = (chain - hi.astype(F32)).astype(BF16)
            fields_out[level] = mxu(turned, hi, NN) + mxu(turned, lo, NN)
        if level < 7:
            own = slab[pl.ds(level, 64, stride=24), :][:, :64]
            own_out[level] = own
            sib_out[level] = slab[pl.ds(level + 8, 64, stride=24), :][:, :64]
            turned_own = own.T
            if level == 0:
                chain = turned_own
            else:
                e = turned_own.astype(BF16)
                chain = mxu(e, hi, NN) + mxu(e, lo, NN)


def top_matrices(device, transfer, coupling):
    return pl.pallas_call(
        top_kernel,
        out_shape=[
            jax.ShapeDtypeStruct((7, 64, 64), F32),
            jax.ShapeDtypeStruct((7, 64, 64), F32),
            jax.ShapeDtypeStruct((8, 64, 64), F32),
        ],
        in_specs=[
            pl.BlockSpec(memory_space=pltpu.SMEM),
            pl.BlockSpec(memory_space=VMEM),
            pl.BlockSpec(memory_space=VMEM),
        ],
        out_specs=[pl.BlockSpec(memory_space=VMEM)] * 3,
        scratch_shapes=[VMEM((64 * 24, 128), F32), VMEM((64 * 24, 128), F32)],
        compiler_params=pltpu.CompilerParams(vmem_limit_bytes=32 * 2**20),
        cost_estimate=pl.CostEstimate(flops=10**9, bytes_accessed=8 * 2**20, transcendentals=0),
        name="top_matrices",
    )(device, transfer, coupling)


def thirds(x):
    a = x.astype(BF16).astype(F32)
    b = (x - a).astype(BF16).astype(F32)
    return a, b, x - a - b


def near_kernel(groups, first, coords, vectors, out):
    eye = (
        lax.broadcasted_iota(jnp.int32, (128, 128), 0)
        == lax.broadcasted_iota(jnp.int32, (128, 128), 1)
    )
    five = jnp.zeros((5, 256), F32)
    one8 = jnp.where(lax.broadcasted_iota(jnp.int32, (8, 256), 0) == 0, 1.0, 0.0)
    for g in range(groups):
        at = 256 * (first + g)
        xyz = coords[:, at : at + 256] * CHORD
        x = jnp.concatenate([xyz, five], 0)
        x1, x2, x3 = thirds(x)
        norm = jnp.sum(x * x, axis=0, keepdims=True) * one8
        n1, n2, n3 = thirds(norm)
        left = jnp.concatenate([x1, x1, x2, x2, x1, x3, n1, n2, n3, one8, one8, one8], 0)
        right = jnp.concatenate(
            [-2 * x1, -2 * x2, -2 * x1, -2 * x2, -2 * x3, -2 * x1, one8, one8, one8, n1, n2, n3], 0
        )
        left_t = left.T.astype(BF16)
        right = right.astype(BF16)

        def kernel_block(a, b):
            square = mxu(left_t[128 * a : 128 * a + 128], right[:, 128 * b : 128 * b + 128], NN)
            square = jnp.maximum(square, 1e-30)
            value = jnp.exp2(-(square * lax.rsqrt(square)))
            if a == b:
                value = jnp.where(eye, NUGGET_DIAG, value)
            return value.astype(BF16)

        v0 = vectors[:, at : at + 128]
        v1 = vectors[:, at + 128 : at + 256]
        side = kernel_block(0, 1)
        out[:, 256 * g : 256 * g + 128] = mxu(v0, kernel_block(0, 0), NN) + mxu(v1, side, NT)
        out[:, 256 * g + 128 : 256 * g + 256] = mxu(v0, side, NN) + mxu(v1, kernel_block(1, 1), NN)


def near(coords, vectors, first, groups):
    return pl.pallas_call(
        functools.partial(near_kernel, groups, first),
        out_shape=jax.ShapeDtypeStruct((64, 256 * groups), F32),
        in_specs=[pl.BlockSpec(memory_space=VMEM)] * 2,
        out_specs=pl.BlockSpec(memory_space=VMEM),
        compiler_params=pltpu.CompilerParams(vmem_limit_bytes=32 * 2**20),
        cost_estimate=pl.CostEstimate(
            flops=groups * 10**8, bytes_accessed=groups * 2**18, transcendentals=groups * 2 * 65536
        ),
        name="near",
    )(coords, vectors)


def down_kernel(pieces, top, coupling, levels, quads, pairs, *refs):
    nears = refs[:pieces]
    out_h = refs[pieces]
    going, shifted, out, sems = refs[pieces + 1 :]
    shift = jnp.where(
        lax.broadcasted_iota(jnp.int32, (64, 128), 1)
        == lax.broadcasted_iota(jnp.int32, (64, 128), 0) + 64,
        1.0,
        0.0,
    ).astype(BF16)
    for p in range(31):
        shifted[64 * p : 64 * p + 64, :] = mxu(coupling[p], shift, NN).astype(BF16)
    blank = jnp.zeros((64, 128), BF16)

    def field(level, pair):
        base = 32 - (32 >> (level - 2))
        s = split(levels[:, LEVEL_AT[level] + 128 * pair : LEVEL_AT[level] + 128 * pair + 128])
        z = jnp.concatenate([shifted[64 * (base + pair) : 64 * (base + pair) + 64, :], blank], 0)
        return fold(mxu(s, z, NN) + mxu(s, z, NT))

    at = LEVEL_AT[6]
    s = split(jnp.concatenate([top[...], jnp.zeros((64, 64), F32)], 1))
    going[:, at : at + 128] = fold(mxu(s, quads[63, :128, :], NT)) + field(6, 0)
    for level in range(5, 0, -1):
        count = 128 >> level
        for q in range(count // 4):
            above = LEVEL_AT[level + 1] + 128 * q
            s = split(going[:, above : above + 128])
            g = fold(mxu(s, quads[NODE_AT[level] // 4 + q], NT))
            at = LEVEL_AT[level] + 256 * q
            if level >= 2:
                g = g + jnp.concatenate([field(level, 2 * q), field(level, 2 * q + 1)], 1)
            going[:, at : at + 256] = g
    copies = []
    width = 8192 // pieces
    for q in range(32):
        above = LEVEL_AT[1] + 128 * q
        s = split(going[:, above : above + 128])
        g = fold(mxu(s, quads[q], NT)).astype(BF16)
        for u in range(2):
            at = 256 * q + 128 * u
            piece, local = divmod(at, width)
            out[:, at : at + 128] = (
                mxu(g[:, 128 * u : 128 * u + 128], pairs[2 * q + u], NT)
                + nears[piece][:, local : local + 128]
            )
        if q % 8 == 7:
            part = pl.ds(256 * (q - 7), 2048)
            copies.append(
                pltpu.make_async_copy(out.at[:, part], out_h.at[:, part], sems.at[q // 8])
            )
            copies[-1].start()
    for copy in copies:
        copy.wait()


def downward(top, coupling, levels, quads, pairs, nears):
    return pl.pallas_call(
        functools.partial(down_kernel, len(nears)),
        out_shape=jax.ShapeDtypeStruct((64, 8192), F32),
        in_specs=[pl.BlockSpec(memory_space=VMEM)] * (5 + len(nears)),
        out_specs=pl.BlockSpec(memory_space=pl.ANY),
        scratch_shapes=[
            VMEM((64, 8064), F32),
            VMEM((31 * 64, 128), BF16),
            VMEM((64, 8192), F32),
            pltpu.SemaphoreType.DMA((4,)),
        ],
        compiler_params=pltpu.CompilerParams(vmem_limit_bytes=36 * 2**20),
        cost_estimate=pl.CostEstimate(flops=10**9, bytes_accessed=8 * 2**20, transcendentals=0),
        name="downward",
    )(top, coupling, levels, quads, pairs, *nears)


def exchanged(value, mask):
    devices = lax.axis_size(AXES)
    return lax.ppermute(value, AXES, [(s, s ^ mask) for s in range(devices)])


def dot(a, b):
    return jnp.dot(a, b, precision=HIGH)


def on_device(coords, vectors, bases, transfer, coupling, top_transfer, top_coupling):
    vectors = vectors.T
    device = lax.axis_index(AXES).astype(jnp.int32).reshape(1)
    climbing, levels, pairs, quads = upward(
        bases.transpose(1, 2, 0), vectors, transfer[0].transpose(1, 2, 0)
    )
    own, sib, lift = top_matrices(
        device, top_transfer.transpose(1, 2, 0), top_coupling.transpose(1, 2, 0)
    )
    nears = []
    top = jnp.zeros((64, 64), F32)
    for height in range(8):
        partner = exchanged(climbing, 1 << height)
        if 1 <= height <= 4:
            nears.append(near(coords, vectors, 8 * len(nears), 8))
        top = top + dot(partner, lift[height])
        if height < 7:
            climbing = dot(climbing, own[height]) + dot(partner, sib[height])
    result = downward(top, coupling[0], levels, quads, pairs, nears)
    return result.T


def solution(mesh):
    both = ("leaf", "sub")
    return jax.shard_map(
        on_device,
        mesh=mesh,
        in_specs=(
            P(None, both),
            P(both, None),
            P(both, None, None),
            P(both, None, None, None),
            P(both, None, None, None),
            P(),
            P(),
        ),
        out_specs=P(both, None),
        check_vma=False,
    )
```

profile of v0, /device:TPU:24, one launch (start us, length us, event | category | flops | bytes accessed | tf_op | source)
XLA Modules:
  0.0 75.6 jit_solution(17682285877100247025)
XLA Ops:
  0.0 12.1 %upward.1 = (f32[64,64]{1,0:T(8,128)}, f32[64,8064]{1,0:T(8,128)}, bf16[64,128,128]{2,1,0:T(8,128)(2,1)}, bf16[64,256,128]{2,1,0:T(8,128)(2,1)}) custom-call(bf16[64,64,128]{2,1,0:T(8,128)(2,1)} %bitcast.107, bf16[64,8192]{1,0:T(8,128)(2,1)} %bitcast.100, bf16[64,64,254]{2,1,0:T(8,128)(2,1)} %bitcast.106), custom_call_target="tpu_custom_call" | custom-call | flops 1000000000 | bytes 8388608 | tf_op jit(solution)/shard_map/upward/pallas_call | solution.py:126
  12.4 1.8 %near.7.refs_3_ = f32[64,2048]{1,0:T(8,128)S(1)} custom-call(f32[3,8192]{1,0:T(4,128)S(1)} %copy-done.13, bf16[64,8192]{1,0:T(8,128)(2,1)S(1)} %bitcast.101), custom_call_target="tpu_custom_call" | custom-call | flops 800000000 | bytes 2097152 | tf_op jit(solution)/shard_map/near/pallas_call | solution.py:256
  14.2 0.8 %copy-done.6 = f32[64,2048]{1,0:T(8,128)} copy-done((f32[64,2048]{1,0:T(8,128)}, f32[64,2048]{1,0:T(8,128)S(1)}, u32[]{:S(2)}) %copy-start.6) | copy-done | bytes 524312
  15.0 1.8 %near.6.refs_2_ = f32[64,2048]{1,0:T(8,128)S(1)} custom-call(f32[3,8192]{1,0:T(4,128)S(1)} %copy-done.13, bf16[64,8192]{1,0:T(8,128)(2,1)S(1)} %bitcast.102), custom_call_target="tpu_custom_call" | custom-call | flops 800000000 | bytes 2097152 | tf_op jit(solution)/shard_map/near/pallas_call | solution.py:256
  16.8 0.8 %copy-done.8 = f32[64,2048]{1,0:T(8,128)} copy-done((f32[64,2048]{1,0:T(8,128)}, f32[64,2048]{1,0:T(8,128)S(1)}, u32[]{:S(2)}) %copy-start.8) | copy-done | bytes 524312
  17.7 1.8 %near.5.refs_1_ = f32[64,2048]{1,0:T(8,128)S(1)} custom-call(f32[3,8192]{1,0:T(4,128)S(1)} %copy-done.13, bf16[64,8192]{1,0:T(8,128)(2,1)S(1)} %bitcast.103), custom_call_target="tpu_custom_call" | custom-call | flops 800000000 | bytes 2097152 | tf_op jit(solution)/shard_map/near/pallas_call | solution.py:256
  20.3 2.2 %copy-done = bf16[508,64,64]{0,2,1:T(8,128)(2,1)S(1)} copy-done((bf16[508,64,64]{0,2,1:T(8,128)(2,1)S(1)}, bf16[508,64,64]{0,2,1:T(8,128)(2,1)}, u32[]{:S(2)}) %copy-start) | copy-done | bytes 4161560
  22.5 2.8 %top_matrices.1 = (f32[7,64,64]{2,1,0:T(8,128)S(1)}, f32[7,64,64]{2,1,0:T(8,128)S(1)}, f32[8,64,64]{2,1,0:T(8,128)S(1)}) custom-call(s32[1]{0:T(128)} %bitcast.4.device, bf16[64,64,508]{2,1,0:T(8,128)(2,1)S(1)} %bitcast.98, bf16[64,64,255]{2,1,0:T(8,128)(2,1)S(1)} %bitcast.99), custom_call_target="tpu_custom_call" | custom-call | flops 1000000000 | bytes 8388608 | tf_op jit(solution)/shard_map/top_matrices/pallas_call | solution.py:193
  25.5 1.8 %near.4.refs_0_ = f32[64,2048]{1,0:T(8,128)S(1)} custom-call(f32[3,8192]{1,0:T(4,128)S(1)} %copy-done.13, bf16[64,8192]{1,0:T(8,128)(2,1)S(1)} %bitcast.104), custom_call_target="tpu_custom_call" | custom-call | flops 800000000 | bytes 2097152 | tf_op jit(solution)/shard_map/near/pallas_call | solution.py:256
  27.5 1.6 %collective-permute-start.1 = (f32[64,64]{1,0:T(8,128)S(1)}, f32[64,64]{1,0:T(8,128)S(1)}, u32[]{:S(2)}, u32[]{:S(2)}) collective-permute-start(f32[64,64]{1,0:T(8,128)S(1)} %convolution_add_fusion.6), channel_id=1, source_target_pairs={{0,2},{1,3},{2,0},{3,1},{4,6},{5,7},{6,4},{7,5},{8,10},{9,11},{10,... | collective-permute-start | bytes 49160 | tf_op jit(solution)/shard_map/ppermute | solution.py:345
  29.3 2.3 %collective-permute-done.1 = f32[64,64]{1,0:T(8,128)S(1)} collective-permute-done((f32[64,64]{1,0:T(8,128)S(1)}, f32[64,64]{1,0:T(8,128)S(1)}, u32[]{:S(2)}, u32[]{:S(2)}) %collective-permute-start.1) | collective-permute-done | bytes 16416 | tf_op jit(solution)/shard_map/ppermute | solution.py:345
  31.9 3.1 %collective-permute-start.2 = (f32[64,64]{1,0:T(8,128)S(1)}, f32[64,64]{1,0:T(8,128)S(1)}, u32[]{:S(2)}, u32[]{:S(2)}) collective-permute-start(f32[64,64]{1,0:T(8,128)S(1)} %convolution_add_fusion.5), channel_id=1, source_target_pairs={{0,4},{1,5},{2,6},{3,7},{4,0},{5,1},{6,2},{7,3},{8,12},{9,13},{10,... | collective-permute-start | bytes 49160 | tf_op jit(solution)/shard_map/ppermute | solution.py:345
  35.1 2.2 %collective-permute-done.2 = f32[64,64]{1,0:T(8,128)S(1)} collective-permute-done((f32[64,64]{1,0:T(8,128)S(1)}, f32[64,64]{1,0:T(8,128)S(1)}, u32[]{:S(2)}, u32[]{:S(2)}) %collective-permute-start.2) | collective-permute-done | bytes 16416 | tf_op jit(solution)/shard_map/ppermute | solution.py:345
  37.7 2.0 %collective-permute-start.3 = (f32[64,64]{1,0:T(8,128)S(1)}, f32[64,64]{1,0:T(8,128)S(1)}, u32[]{:S(2)}, u32[]{:S(2)}) collective-permute-start(f32[64,64]{1,0:T(8,128)S(1)} %convolution_add_fusion.4), channel_id=1, source_target_pairs={{0,8},{1,9},{2,10},{3,11},{4,12},{5,13},{6,14},{7,15},{8,0},{9,1},... | collective-permute-start | bytes 49160 | tf_op jit(solution)/shard_map/ppermute | solution.py:345
  39.9 1.8 %collective-permute-done.3 = f32[64,64]{1,0:T(8,128)S(1)} collective-permute-done((f32[64,64]{1,0:T(8,128)S(1)}, f32[64,64]{1,0:T(8,128)S(1)}, u32[]{:S(2)}, u32[]{:S(2)}) %collective-permute-start.3) | collective-permute-done | bytes 16416 | tf_op jit(solution)/shard_map/ppermute | solution.py:345
  42.0 3.4 %collective-permute-start.4 = (f32[64,64]{1,0:T(8,128)S(1)}, f32[64,64]{1,0:T(8,128)S(1)}, u32[]{:S(2)}, u32[]{:S(2)}) collective-permute-start(f32[64,64]{1,0:T(8,128)S(1)} %convolution_add_fusion.3), channel_id=1, source_target_pairs={{0,16},{1,17},{2,18},{3,19},{4,20},{5,21},{6,22},{7,23},{8,24},{9,... | collective-permute-start | bytes 49160 | tf_op jit(solution)/shard_map/ppermute | solution.py:345
  45.6 1.7 %collective-permute-done.4 = f32[64,64]{1,0:T(8,128)S(1)} collective-permute-done((f32[64,64]{1,0:T(8,128)S(1)}, f32[64,64]{1,0:T(8,128)S(1)}, u32[]{:S(2)}, u32[]{:S(2)}) %collective-permute-start.4) | collective-permute-done | bytes 16416 | tf_op jit(solution)/shard_map/ppermute | solution.py:345
  47.6 6.9 %collective-permute-start.5 = (f32[64,64]{1,0:T(8,128)S(1)}, f32[64,64]{1,0:T(8,128)S(1)}, u32[]{:S(2)}, u32[]{:S(2)}) collective-permute-start(f32[64,64]{1,0:T(8,128)S(1)} %convolution_add_fusion.2), channel_id=1, source_target_pairs={{0,32},{1,33},{2,34},{3,35},{4,36},{5,37},{6,38},{7,39},{8,40},{9,... | collective-permute-start | bytes 49160 | tf_op jit(solution)/shard_map/ppermute | solution.py:345
  54.7 1.7 %collective-permute-done.5 = f32[64,64]{1,0:T(8,128)S(1)} collective-permute-done((f32[64,64]{1,0:T(8,128)S(1)}, f32[64,64]{1,0:T(8,128)S(1)}, u32[]{:S(2)}, u32[]{:S(2)}) %collective-permute-start.5) | collective-permute-done | bytes 16416 | tf_op jit(solution)/shard_map/ppermute | solution.py:345
  56.8 0.8 %collective-permute-start.6 = (f32[64,64]{1,0:T(8,128)S(1)}, f32[64,64]{1,0:T(8,128)S(1)}, u32[]{:S(2)}, u32[]{:S(2)}) collective-permute-start(f32[64,64]{1,0:T(8,128)S(1)} %convolution_add_fusion.1), channel_id=1, source_target_pairs={{0,64},{1,65},{2,66},{3,67},{4,68},{5,69},{6,70},{7,71},{8,72},{9,... | collective-permute-start | bytes 49160 | tf_op jit(solution)/shard_map/ppermute | solution.py:345
  57.8 3.0 %collective-permute-done.6 = f32[64,64]{1,0:T(8,128)S(1)} collective-permute-done((f32[64,64]{1,0:T(8,128)S(1)}, f32[64,64]{1,0:T(8,128)S(1)}, u32[]{:S(2)}, u32[]{:S(2)}) %collective-permute-start.6) | collective-permute-done | bytes 16416 | tf_op jit(solution)/shard_map/ppermute | solution.py:345
  61.0 1.5 %collective-permute-start.7 = (f32[64,64]{1,0:T(8,128)S(1)}, f32[64,64]{1,0:T(8,128)S(1)}, u32[]{:S(2)}, u32[]{:S(2)}) collective-permute-start(f32[64,64]{1,0:T(8,128)S(1)} %convolution_add_fusion), channel_id=1, source_target_pairs={{0,128},{1,129},{2,130},{3,131},{4,132},{5,133},{6,134},{7,135},{8... | collective-permute-start | bytes 49160 | tf_op jit(solution)/shard_map/ppermute | solution.py:345
  62.7 4.0 %collective-permute-done.7 = f32[64,64]{1,0:T(8,128)S(1)} collective-permute-done((f32[64,64]{1,0:T(8,128)S(1)}, f32[64,64]{1,0:T(8,128)S(1)}, u32[]{:S(2)}, u32[]{:S(2)}) %collective-permute-start.7) | collective-permute-done | bytes 16416 | tf_op jit(solution)/shard_map/ppermute | solution.py:345
  67.1 8.3 %downward.1 = f32[64,8192]{1,0:T(8,128)} custom-call(f32[64,64]{1,0:T(8,128)S(1)} %fusion.5.top, bf16[31,64,64]{2,1,0:T(8,128)(2,1)S(1)} %bitcast.105, f32[64,8064]{1,0:T(8,128)S(1)} %copy-done.4, bf16[64,256,128]{2,1,0:T(8,128)(2,1)S(1)} %copy-done.1, bf16[64,128,128]{2,1,0:T(8,128)(2,1)S(1)} %copy-done.3, f32[64,2048]{1,0:T(8,128)S(1)} %near.4.refs_0_, ...), custom_call_target="tpu_custom_call" | custom-call | flops 1000000000 | bytes 8388608 | tf_op jit(solution)/shard_map/downward/pallas_call | solution.py:326
  (51 shorter events, 4.7 us)
Async XLA Ops:
  0.0 12.4 %copy-start.5 = (bf16[8192,64]{0,1:T(8,128)(2,1)S(1)}, bf16[8192,64]{0,1:T(8,128)(2,1)}, u32[]{:S(2)}) copy-start(bf16[8192,64]{0,1:T(8,128)(2,1)} %param.8) | copy-start | bytes 3145732
  0.0 12.4 %copy-start.13 = (f32[3,8192]{1,0:T(4,128)S(1)}, f32[3,8192]{1,0:T(4,128)}, u32[]{:S(2)}) copy-start(f32[3,8192]{1,0:T(4,128)} %coords.7) | copy-start | bytes 294916
  12.1 15.2 %collective-permute-start = (f32[64,64]{1,0:T(8,128)}, f32[64,64]{1,0:T(8,128)S(1)}, u32[]{:S(2)}, u32[]{:S(2)}) collective-permute-start(f32[64,64]{1,0:T(8,128)} %get-tuple-element.12), channel_id=1, source_target_pairs={{0,1},{1,0},{2,3},{3,2},{4,5},{5,4},{6,7},{7,6},{8,9},{9,8},{10,11... | collective-permute-start | bytes 49160 | tf_op jit(solution)/shard_map/ppermute | solution.py:345
  14.2 0.8 %copy-start.6 = (f32[64,2048]{1,0:T(8,128)}, f32[64,2048]{1,0:T(8,128)S(1)}, u32[]{:S(2)}) copy-start(f32[64,2048]{1,0:T(8,128)S(1)} %near.7.refs_3_) | copy-start | bytes 1572868
  16.8 0.8 %copy-start.8 = (f32[64,2048]{1,0:T(8,128)}, f32[64,2048]{1,0:T(8,128)S(1)}, u32[]{:S(2)}) copy-start(f32[64,2048]{1,0:T(8,128)S(1)} %near.6.refs_2_) | copy-start | bytes 1572868
  17.7 2.6 %copy-start.2 = (bf16[255,64,64]{0,2,1:T(8,128)(2,1)S(1)}, bf16[255,64,64]{0,2,1:T(8,128)(2,1)}, u32[]{:S(2)}) copy-start(bf16[255,64,64]{0,2,1:T(8,128)(2,1)} %param.13) | copy-start | bytes 6266884
  19.5 0.8 %copy-start.10 = (f32[64,2048]{1,0:T(8,128)}, f32[64,2048]{1,0:T(8,128)S(1)}, u32[]{:S(2)}) copy-start(f32[64,2048]{1,0:T(8,128)S(1)} %near.5.refs_1_) | copy-start | bytes 1572868
  20.3 2.2 %copy-start = (bf16[508,64,64]{0,2,1:T(8,128)(2,1)S(1)}, bf16[508,64,64]{0,2,1:T(8,128)(2,1)}, u32[]{:S(2)}) copy-start(bf16[508,64,64]{0,2,1:T(8,128)(2,1)} %param.12) | copy-start | bytes 12484612
  22.4 2.9 %copy-start.14 = (f32[64,64]{1,0:T(8,128)S(1)}, f32[64,64]{1,0:T(8,128)}, u32[]{:S(2)}) copy-start(f32[64,64]{1,0:T(8,128)} %get-tuple-element.12) | copy-start | bytes 49156
  22.5 44.6 %copy-start.3 = (bf16[64,128,128]{2,1,0:T(8,128)(2,1)S(1)}, bf16[64,128,128]{2,1,0:T(8,128)(2,1)}, u32[]{:S(2)}) copy-start(bf16[64,128,128]{2,1,0:T(8,128)(2,1)} %get-tuple-element.18.pairs) | copy-start | bytes 6291460
  22.5 44.6 %copy-start.4 = (f32[64,8064]{1,0:T(8,128)S(1)}, f32[64,8064]{1,0:T(8,128)}, u32[]{:S(2)}) copy-start(f32[64,8064]{1,0:T(8,128)} %get-tuple-element.16.levels) | copy-start | bytes 6193156
  22.5 44.6 %copy-start.11 = (f32[64,2048]{1,0:T(8,128)S(1)}, f32[64,2048]{1,0:T(8,128)}, u32[]{:S(2)}) copy-start(f32[64,2048]{1,0:T(8,128)} %copy-done.10) | copy-start | bytes 1572868
  22.5 44.6 %copy-start.12 = (bf16[1,31,64,64]{3,2,1,0:T(8,128)(2,1)S(1)}, bf16[1,31,64,64]{3,2,1,0:T(8,128)(2,1)}, u32[]{:S(2)}) copy-start(bf16[1,31,64,64]{3,2,1,0:T(8,128)(2,1)} %param.11) | copy-start | bytes 761860
  25.5 41.6 %copy-start.1 = (bf16[64,256,128]{2,1,0:T(8,128)(2,1)S(1)}, bf16[64,256,128]{2,1,0:T(8,128)(2,1)}, u32[]{:S(2)}) copy-start(bf16[64,256,128]{2,1,0:T(8,128)(2,1)} %get-tuple-element.17.quads) | copy-start | bytes 12582916
  25.5 41.6 %copy-start.7 = (f32[64,2048]{1,0:T(8,128)S(1)}, f32[64,2048]{1,0:T(8,128)}, u32[]{:S(2)}) copy-start(f32[64,2048]{1,0:T(8,128)} %copy-done.6) | copy-start | bytes 1572868
  25.5 41.6 %copy-start.9 = (f32[64,2048]{1,0:T(8,128)S(1)}, f32[64,2048]{1,0:T(8,128)}, u32[]{:S(2)}) copy-start(f32[64,2048]{1,0:T(8,128)} %copy-done.8) | copy-start | bytes 1572868
  27.5 4.0 %collective-permute-start.1 = (f32[64,64]{1,0:T(8,128)S(1)}, f32[64,64]{1,0:T(8,128)S(1)}, u32[]{:S(2)}, u32[]{:S(2)}) collective-permute-start(f32[64,64]{1,0:T(8,128)S(1)} %convolution_add_fusion.6), channel_id=1, source_target_pairs={{0,2},{1,3},{2,0},{3,1},{4,6},{5,7},{6,4},{7,5},{8,10},{9,11},{10,... | collective-permute-start | bytes 49160 | tf_op jit(solution)/shard_map/ppermute | solution.py:345
  31.9 5.5 %collective-permute-start.2 = (f32[64,64]{1,0:T(8,128)S(1)}, f32[64,64]{1,0:T(8,128)S(1)}, u32[]{:S(2)}, u32[]{:S(2)}) collective-permute-start(f32[64,64]{1,0:T(8,128)S(1)} %convolution_add_fusion.5), channel_id=1, source_target_pairs={{0,4},{1,5},{2,6},{3,7},{4,0},{5,1},{6,2},{7,3},{8,12},{9,13},{10,... | collective-permute-start | bytes 49160 | tf_op jit(solution)/shard_map/ppermute | solution.py:345
  37.7 4.0 %collective-permute-start.3 = (f32[64,64]{1,0:T(8,128)S(1)}, f32[64,64]{1,0:T(8,128)S(1)}, u32[]{:S(2)}, u32[]{:S(2)}) collective-permute-start(f32[64,64]{1,0:T(8,128)S(1)} %convolution_add_fusion.4), channel_id=1, source_target_pairs={{0,8},{1,9},{2,10},{3,11},{4,12},{5,13},{6,14},{7,15},{8,0},{9,1},... | collective-permute-start | bytes 49160 | tf_op jit(solution)/shard_map/ppermute | solution.py:345
  42.0 5.2 %collective-permute-start.4 = (f32[64,64]{1,0:T(8,128)S(1)}, f32[64,64]{1,0:T(8,128)S(1)}, u32[]{:S(2)}, u32[]{:S(2)}) collective-permute-start(f32[64,64]{1,0:T(8,128)S(1)} %convolution_add_fusion.3), channel_id=1, source_target_pairs={{0,16},{1,17},{2,18},{3,19},{4,20},{5,21},{6,22},{7,23},{8,24},{9,... | collective-permute-start | bytes 49160 | tf_op jit(solution)/shard_map/ppermute | solution.py:345
  47.6 8.8 %collective-permute-start.5 = (f32[64,64]{1,0:T(8,128)S(1)}, f32[64,64]{1,0:T(8,128)S(1)}, u32[]{:S(2)}, u32[]{:S(2)}) collective-permute-start(f32[64,64]{1,0:T(8,128)S(1)} %convolution_add_fusion.2), channel_id=1, source_target_pairs={{0,32},{1,33},{2,34},{3,35},{4,36},{5,37},{6,38},{7,39},{8,40},{9,... | collective-permute-start | bytes 49160 | tf_op jit(solution)/shard_map/ppermute | solution.py:345
  56.8 4.0 %collective-permute-start.6 = (f32[64,64]{1,0:T(8,128)S(1)}, f32[64,64]{1,0:T(8,128)S(1)}, u32[]{:S(2)}, u32[]{:S(2)}) collective-permute-start(f32[64,64]{1,0:T(8,128)S(1)} %convolution_add_fusion.1), channel_id=1, source_target_pairs={{0,64},{1,65},{2,66},{3,67},{4,68},{5,69},{6,70},{7,71},{8,72},{9,... | collective-permute-start | bytes 49160 | tf_op jit(solution)/shard_map/ppermute | solution.py:345
  61.0 5.7 %collective-permute-start.7 = (f32[64,64]{1,0:T(8,128)S(1)}, f32[64,64]{1,0:T(8,128)S(1)}, u32[]{:S(2)}, u32[]{:S(2)}) collective-permute-start(f32[64,64]{1,0:T(8,128)S(1)} %convolution_add_fusion), channel_id=1, source_target_pairs={{0,128},{1,129},{2,130},{3,131},{4,132},{5,133},{6,134},{7,135},{8... | collective-permute-start | bytes 49160 | tf_op jit(solution)/shard_map/ppermute | solution.py:345
where the time goes:
time: 75.7 us; the launch traced here: 75.6 us
  Pallas kernels  30.5 us (40%)
  starting transfers between devices  19.6 us (26%)
  waiting for transfers between devices  16.8 us (22%)
  local copies, waits for them, and re-layouts  4.66 us (6%)
  matrix products  3.58 us (5%)
    ppermute x8, starting transfers between devices, exchanged(): return lax.ppermute(value, AXES, [(s, s ^ mask) for s in range(devices)])  19.6 us
    ppermute x8, waiting for transfers between devices, exchanged(): return lax.ppermute(value, AXES, [(s, s ^ mask) for s in range(devices)])  16.8 us
    pallas_call x1, Pallas kernels, upward(): pl.pallas_call(up_kernel, out_shape=[jax.ShapeDtypeStruct((64, 64), F32),...  12.1 us
    pallas_call x1, Pallas kernels, downward(): pl.pallas_call(functools.partial(down_kernel, len(nears)), out_shape=jax....  8.33 us
    pallas_call x4, Pallas kernels, near(): pl.pallas_call(functools.partial(near_kernel, groups, first), out_shape=j...  7.19 us
    unnamed x30, local copies, waits for them, and re-layouts  4.66 us
    dot_general x22, matrix products, dot(): return jnp.dot(a, b, precision=HIGH)  3.58 us
    pallas_call x1, Pallas kernels, top_matrices(): pl.pallas_call(top_kernel, out_shape=[jax.ShapeDtypeStruct((7, 64, 64), F...  2.85 us
  transfers between devices with their start and end apart: 8, of which 7 were waited for; matrix products, arithmetic and copies ran while one was open for 2% of the time, Pallas kernels for 13%

commit v1 on v0

v1 whole, which is shorter than its diff:
```python
import functools

import jax
import jax.numpy as jnp
from jax import lax
from jax.experimental import pallas as pl
from jax.experimental.pallas import tpu as pltpu
from jax.sharding import PartitionSpec as P

F32 = jnp.float32
BF16 = jnp.bfloat16
VMEM = pltpu.VMEM
AXES = ("leaf", "sub")
HIGH = lax.Precision.HIGHEST

STEP = 136
NN = (((1,), (0,)), ((), ()))
NT = (((1,), (1,)), ((), ()))
LEVEL_AT = (None, 0, 4096, 6144, 7168, 7680, 7936)
NODE_AT = (0, 128, 192, 224, 240, 248, 252)
NUGGET_DIAG = 1.5
MASKS = (1, 2, 6, 8, 16, 48, 64, 192)
BESIDE = {4: (0,), 5: (1,), 6: (2,), 7: (3,)}
CHORD = 2.0 * 1.4426950408889634


def mxu(a, b, dims):
    return lax.dot_general(a, b, dims, preferred_element_type=F32)


def split(c):
    hi = c.astype(BF16)
    lo = (c - hi.astype(F32)).astype(BF16)
    return jnp.concatenate([hi, lo], 0)


def fold(t):
    half = t.shape[0] // 2
    return t[:half] + t[half:]


def half_mask():
    return lax.broadcasted_iota(jnp.int32, (32, 128), 1) < 64


def spread(src, width, lane0, slab, rows):
    for i in rows:
        w = jnp.concatenate([src[i, :, lane0 : lane0 + width], src[i + 32, :, lane0 : lane0 + width]], 0)
        if width < 128:
            w = jnp.concatenate([w, jnp.zeros((128, 128 - width), BF16)], 1)
        slab[pl.ds(i * STEP, 128), :] = w.T.astype(F32)


def box_matrix(slab, box, right, low):
    x = slab[pl.ds(box, 32, stride=STEP), :]
    y = pltpu.roll(x, 64, 1)
    if right:
        return jnp.concatenate([jnp.where(low, 0.0, y), jnp.where(low, 0.0, x)], 0)
    return jnp.concatenate([jnp.where(low, x, 0.0), jnp.where(low, y, 0.0)], 0)


def up_kernel(
    bases_h, vectors_h, transfer_h, own_out, levels_h, pairs_h, quads_h,
    bases, vectors, transfer, slab0, slab1, slab2, leaf_coef, levels, pairs, quads, sems, out_sems,
):
    loads = []
    for k in range(4):
        part = pl.ds(16 * (k // 2) + 32 * (k % 2), 16)
        loads.append(pltpu.make_async_copy(bases_h.at[part], bases.at[part], sems.at[k]))
    loads.append(pltpu.make_async_copy(vectors_h, vectors, sems.at[4]))
    loads.append(pltpu.make_async_copy(transfer_h, transfer, sems.at[5]))
    for copy in loads:
        copy.start()
    stores = []

    def store(src, dst):
        copy = pltpu.make_async_copy(src, dst, out_sems.at[len(stores)])
        copy.start()
        stores.append(copy)

    low = half_mask()
    for k in range(2):
        loads[2 * k].wait()
        loads[2 * k + 1].wait()
        spread(bases, 128, 0, slab0, range(16 * k, 16 * k + 16))
    loads[4].wait()
    for j in range(64):
        pair = jnp.concatenate(
            [box_matrix(slab0, 2 * j, False, low), box_matrix(slab0, 2 * j + 1, True, low)], 0
        ).astype(BF16)
        pairs[j] = pair
        leaf_coef[:, 128 * j : 128 * j + 128] = mxu(
            vectors[:, 128 * j : 128 * j + 128], pair, NN
        )
    store(pairs, pairs_h)
    loads[5].wait()
    spread(transfer, 128, 0, slab1, range(32))
    spread(transfer, 126, 128, slab2, range(32))
    for level in range(6):
        count = 128 >> level
        for q in range(count // 4):
            first = NODE_AT[level] + 4 * q
            slab = slab1 if first < 128 else slab2
            quad = jnp.concatenate(
                [box_matrix(slab, (first + u) % 128, u >= 2, low) for u in range(4)], 0
            ).astype(BF16)
            quads[first // 4] = quad
            if level == 0:
                coef = leaf_coef[:, 256 * q : 256 * q + 256]
            else:
                at = LEVEL_AT[level] + 256 * q
                coef = levels[:, at : at + 256]
            at = LEVEL_AT[level + 1] + 128 * q
            levels[:, at : at + 128] = fold(mxu(split(coef), quad, NN))
        if level < 2:
            part = pl.ds(NODE_AT[level] // 4, count // 4)
            store(quads.at[part], quads_h.at[part])
            part = pl.ds(LEVEL_AT[level + 1], 32 * count)
            store(levels.at[:, part], levels_h.at[:, part])
    last = jnp.concatenate(
        [box_matrix(slab2, 124, False, low), box_matrix(slab2, 125, False, low)], 0
    ).astype(BF16)
    quads[63, :128, :] = last
    quads[63, 128:, :] = jnp.zeros((128, 128), BF16)
    part = pl.ds(48, 16)
    store(quads.at[part], quads_h.at[part])
    part = pl.ds(LEVEL_AT[3], 1920)
    store(levels.at[:, part], levels_h.at[:, part])
    at = LEVEL_AT[6]
    own_out[...] = fold(mxu(split(levels[:, at : at + 128]), last, NN))[:, :64]
    for copy in stores:
        copy.wait()


def params(mib):
    return pltpu.CompilerParams(vmem_limit_bytes=mib * 2**20)


def cost(us):
    return pl.CostEstimate(flops=int(us * 10**9), bytes_accessed=2**16, transcendentals=0)


IN_VMEM = pl.BlockSpec(memory_space=VMEM)
IN_HBM = pl.BlockSpec(memory_space=pl.ANY)
IN_SMEM = pl.BlockSpec(memory_space=pltpu.SMEM)


def upward(bases, vectors, transfer):
    return pl.pallas_call(
        up_kernel,
        out_shape=[
            jax.ShapeDtypeStruct((64, 64), F32),
            jax.ShapeDtypeStruct((64, 8064), F32),
            jax.ShapeDtypeStruct((64, 128, 128), BF16),
            jax.ShapeDtypeStruct((64, 256, 128), BF16),
        ],
        in_specs=[IN_HBM] * 3,
        out_specs=[IN_VMEM] + [IN_HBM] * 3,
        scratch_shapes=[
            VMEM((64, 64, 128), BF16),
            VMEM((64, 8192), BF16),
            VMEM((64, 64, 254), BF16),
            VMEM((32 * STEP, 128), F32),
            VMEM((32 * STEP, 128), F32),
            VMEM((32 * STEP, 128), F32),
            VMEM((64, 8192), F32),
            VMEM((64, 8064), F32),
            VMEM((64, 128, 128), BF16),
            VMEM((64, 256, 128), BF16),
            pltpu.SemaphoreType.DMA((6,)),
            pltpu.SemaphoreType.DMA((7,)),
        ],
        compiler_params=params(58),
        cost_estimate=cost(8),
        name="upward",
    )(bases, vectors, transfer)


def pick_rows(table, pick, slab):
    for i in range(16):
        rows = jnp.concatenate(
            [table[2 * i], table[2 * i + 32], table[2 * i + 1], table[2 * i + 33]], 0
        )
        out = mxu(pick, rows, NT)
        slab[pl.ds(48 * i, 16), :] = out[:, :128]
        slab[pl.ds(48 * i + 24, 16), :] = out[:, 128:]


def picked(slab, row):
    x = slab[pl.ds(row, 32, stride=24), :]
    return jnp.concatenate([x, pltpu.roll(x, 64, 1)], 0)[:, :64]


def transfer_pick(dev, heights, lane0, width):
    row = lax.broadcasted_iota(jnp.int32, (16, width), 0)
    col = lax.broadcasted_iota(jnp.int32, (16, width), 1)
    hit = jnp.zeros((16, width), jnp.bool_)
    for n, height in enumerate(heights):
        box = 512 - (512 >> height) + (dev >> height) - lane0
        hit = hit | ((row == n) & (col == box))
        hit = hit | ((row == n + 8) & (col == (box ^ 1)))
    return jnp.where(hit, 1.0, 0.0).astype(BF16)


def thirds(x):
    a = x.astype(BF16).astype(F32)
    b = (x - a).astype(BF16).astype(F32)
    return a, b, x - a - b


def near_field(coords, vectors, out, square_x, left_t, right):
    square_x[0:3, :] = coords[...] * CHORD
    square_x[3:8, :] = jnp.zeros((5, 2048), F32)
    x = square_x[...]
    one8 = jnp.where(lax.broadcasted_iota(jnp.int32, (8, 2048), 0) == 0, 1.0, 0.0)
    x1, x2, x3 = thirds(x)
    n1, n2, n3 = thirds(jnp.sum(x * x, axis=0, keepdims=True) * one8)
    left = jnp.concatenate([x1, x1, x2, x2, x1, x3, n1, n2, n3, one8, one8, one8], 0)
    left_t[...] = left.astype(BF16).T
    y1, y2, y3 = -2 * x1, -2 * x2, -2 * x3
    right[...] = jnp.concatenate(
        [y1, y2, y1, y2, y3, y1, one8, one8, one8, n1, n2, n3], 0
    ).astype(BF16)
    eye = (
        lax.broadcasted_iota(jnp.int32, (128, 128), 0)
        == lax.broadcasted_iota(jnp.int32, (128, 128), 1)
    )
    for g in range(8):
        at = 256 * g

        def block(a, b):
            square = mxu(left_t[at + a : at + a + 128, :], right[:, at + b : at + b + 128], NN)
            square = jnp.maximum(square, 1e-30)
            value = jnp.exp2(-(square * lax.rsqrt(square)))
            if a == b:
                value = jnp.where(eye, NUGGET_DIAG, value)
            return value.astype(BF16)

        v0 = vectors[:, at : at + 128]
        v1 = vectors[:, at + 128 : at + 256]
        side = block(0, 128)
        out[:, at : at + 128] = mxu(v0, block(0, 0), NN) + mxu(v1, side, NT)
        out[:, at + 128 : at + 256] = mxu(v0, side, NN) + mxu(v1, block(128, 128), NN)


NEAR_SCRATCH = [
    VMEM((3, 2048), F32),
    VMEM((64, 2048), BF16),
    VMEM((8, 2048), F32),
    VMEM((2048, 96), BF16),
    VMEM((96, 2048), BF16),
]


def start_near(piece, coords_h, vectors_h, coords, vectors, sems):
    part = pl.ds(2048 * piece, 2048)
    copies = [
        pltpu.make_async_copy(coords_h.at[:, part], coords, sems.at[0]),
        pltpu.make_async_copy(vectors_h.at[:, part], vectors, sems.at[1]),
    ]
    for copy in copies:
        copy.start()
    return copies


def first_kernel(after, device, transfer_h, own_out, sib_out, table, slab, sems):
    dev = device[0]
    lane0 = pl.multiple_of(128 * (dev >> 7), 128)
    load = pltpu.make_async_copy(transfer_h.at[:, :, pl.ds(lane0, 128)], table, sems.at[0])
    load.start()
    load.wait()
    pick_rows(table, transfer_pick(dev, [0], lane0, 128), slab)
    own_out[...] = picked(slab, 0)
    sib_out[...] = picked(slab, 8)


def first_pick(after, device, transfer):
    return pl.pallas_call(
        first_kernel,
        out_shape=[jax.ShapeDtypeStruct((64, 64), F32)] * 2,
        in_specs=[IN_VMEM, IN_SMEM, IN_HBM],
        out_specs=[IN_VMEM] * 2,
        scratch_shapes=[
            VMEM((64, 64, 128), BF16),
            VMEM((32 * 24, 128), F32),
            pltpu.SemaphoreType.DMA((1,)),
        ],
        compiler_params=params(58),
        cost_estimate=cost(1),
        name="first_pick",
    )(after, device, transfer)


def second_kernel(
    after, device, coords_h, vectors_h, transfer_h, near_out, own_out, sib_out,
    coords, vectors, square_x, left_t, right, table, slab, sems,
):
    dev = device[0]
    load = pltpu.make_async_copy(transfer_h.at[:, :, pl.ds(256, 252)], table, sems.at[2])
    load.start()
    for copy in start_near(0, coords_h, vectors_h, coords, vectors, sems):
        copy.wait()
    near_field(coords, vectors, near_out, square_x, left_t, right)
    load.wait()
    pick_rows(table, transfer_pick(dev, range(1, 7), 256, 252), slab)
    for n in range(6):
        own_out[n] = picked(slab, n)
        sib_out[n] = picked(slab, 8 + n)


def second_pick(after, device, coords, vectors, transfer):
    return pl.pallas_call(
        second_kernel,
        out_shape=[jax.ShapeDtypeStruct((64, 2048), F32)]
        + [jax.ShapeDtypeStruct((6, 64, 64), F32)] * 2,
        in_specs=[IN_VMEM, IN_SMEM] + [IN_HBM] * 3,
        out_specs=[IN_VMEM] * 3,
        scratch_shapes=NEAR_SCRATCH
        + [
            VMEM((64, 64, 252), BF16),
            VMEM((32 * 24, 128), F32),
            pltpu.SemaphoreType.DMA((3,)),
        ],
        compiler_params=params(58),
        cost_estimate=cost(2),
        name="second_pick",
    )(after, device, coords, vectors, transfer)


def lift_kernel(
    after, device, own0, own, coords_h, vectors_h, coupling_h, near_out, lift_out,
    coords, vectors, square_x, left_t, right, table, slab, sems,
):
    dev = device[0]
    load = pltpu.make_async_copy(coupling_h, table, sems.at[2])
    load.start()
    for copy in start_near(1, coords_h, vectors_h, coords, vectors, sems):
        copy.wait()
    near_field(coords, vectors, near_out, square_x, left_t, right)
    load.wait()
    row = lax.broadcasted_iota(jnp.int32, (16, 255), 0)
    col = lax.broadcasted_iota(jnp.int32, (16, 255), 1)
    want = 256 - (256 >> row) + (jnp.full_like(row, dev) >> (row + 1))
    pick_rows(table, jnp.where((col == want) & (row < 8), 1.0, 0.0).astype(BF16), slab)
    chain = None
    for level in range(8):
        pair = picked(slab, level)
        odd = (dev >> level) & 1
        turned = jnp.where(odd == 1, pair, pair.T).astype(BF16)
        if level == 0:
            lift_out[0] = turned.astype(F32)
        else:
            hi = chain.astype(BF16)
            lo = (chain - hi.astype(F32)).astype(BF16)
            lift_out[level] = mxu(turned, hi, NN) + mxu(turned, lo, NN)
        if level < 7:
            e = (own0[...] if level == 0 else own[level - 1]).T
            if level == 0:
                chain = e
            else:
                e = e.astype(BF16)
                chain = mxu(e, hi, NN) + mxu(e, lo, NN)


def lifts(after, device, own0, own, coords, vectors, coupling):
    return pl.pallas_call(
        lift_kernel,
        out_shape=[
            jax.ShapeDtypeStruct((64, 2048), F32),
            jax.ShapeDtypeStruct((8, 64, 64), F32),
        ],
        in_specs=[IN_VMEM, IN_SMEM, IN_VMEM, IN_VMEM] + [IN_HBM] * 3,
        out_specs=[IN_VMEM] * 2,
        scratch_shapes=NEAR_SCRATCH
        + [
            VMEM((64, 64, 255), BF16),
            VMEM((32 * 24, 128), F32),
            pltpu.SemaphoreType.DMA((3,)),
        ],
        compiler_params=params(58),
        cost_estimate=cost(2),
        name="lifts",
    )(after, device, own0, own, coords, vectors, coupling)


def near_kernel(piece, after, coords_h, vectors_h, near_out, coords, vectors, square_x, left_t, right, sems):
    for copy in start_near(piece, coords_h, vectors_h, coords, vectors, sems):
        copy.wait()
    near_field(coords, vectors, near_out, square_x, left_t, right)


def near(piece, after, coords, vectors):
    return pl.pallas_call(
        functools.partial(near_kernel, piece),
        out_shape=jax.ShapeDtypeStruct((64, 2048), F32),
        in_specs=[IN_VMEM] + [IN_HBM] * 2,
        out_specs=IN_VMEM,
        scratch_shapes=NEAR_SCRATCH + [pltpu.SemaphoreType.DMA((2,))],
        compiler_params=params(58),
        cost_estimate=cost(1.5),
        name="near",
    )(after, coords, vectors)


def shift_right():
    row = lax.broadcasted_iota(jnp.int32, (64, 128), 0)
    col = lax.broadcasted_iota(jnp.int32, (64, 128), 1)
    return jnp.where(col == row + 64, 1.0, 0.0).astype(BF16)


def pair_field(coef, coupling, shift):
    z = mxu(coupling, shift, NN).astype(BF16)
    z = jnp.concatenate([z, jnp.zeros((64, 128), BF16)], 0)
    s = split(coef)
    return fold(mxu(s, z, NN) + mxu(s, z, NT))


def with_fields(state, fields):
    return jnp.concatenate([state[:64] + jnp.concatenate(fields, 1), state[64:]], 0)


def descend(state, quad):
    return fold(mxu(split(state), quad, NT))


def upper_kernel(after, coupling_h, levels_h, quads_h, state_out, coupling, levels, quads, sems):
    copies = [
        pltpu.make_async_copy(coupling_h.at[pl.ds(16, 15)], coupling, sems.at[0]),
        pltpu.make_async_copy(levels_h.at[:, pl.ds(LEVEL_AT[3], 1920)], levels, sems.at[1]),
        pltpu.make_async_copy(quads_h.at[pl.ds(56, 8)], quads, sems.at[2]),
    ]
    for copy in copies:
        copy.start()
    for copy in copies:
        copy.wait()
    shift = shift_right()

    def field(level, pair):
        base = 16 - (32 >> (level - 2))
        at = LEVEL_AT[level] - LEVEL_AT[3] + 128 * pair
        return pair_field(levels[:, at : at + 128], coupling[base + pair], shift)

    unit = jnp.where(
        lax.broadcasted_iota(jnp.int32, (64, 64), 0)
        == lax.broadcasted_iota(jnp.int32, (64, 64), 1),
        1.0,
        0.0,
    ).astype(BF16)
    state = jnp.concatenate([field(6, 0), mxu(unit, quads[7, :128, :64], NT)], 0)
    for level in range(5, 2, -1):
        below = []
        for q in range((128 >> level) // 4):
            s = descend(state[:, 128 * q : 128 * q + 128], quads[NODE_AT[level] // 4 - 56 + q])
            below.append(with_fields(s, [field(level, 2 * q), field(level, 2 * q + 1)]))
        state = jnp.concatenate(below, 1)
    state_out[...] = state


def upper(after, coupling, levels, quads):
    return pl.pallas_call(
        upper_kernel,
        out_shape=jax.ShapeDtypeStruct((128, 1024), F32),
        in_specs=[IN_VMEM] + [IN_HBM] * 3,
        out_specs=IN_VMEM,
        scratch_shapes=[
            VMEM((15, 64, 64), BF16),
            VMEM((64, 1920), F32),
            VMEM((8, 256, 128), BF16),
            pltpu.SemaphoreType.DMA((3,)),
        ],
        compiler_params=params(58),
        cost_estimate=cost(1.5),
        name="upper",
    )(after, coupling, levels, quads)


def lower_kernel(
    piece, after, state3, near_in, coupling_h, levels_h, quads_h, pairs_h, base_out, top_out,
    coupling, levels, quads, pairs, sems,
):
    copies = [
        pltpu.make_async_copy(coupling_h.at[pl.ds(4 * piece, 4)], coupling, sems.at[0]),
        pltpu.make_async_copy(
            levels_h.at[:, pl.ds(LEVEL_AT[2] + 512 * piece, 512)], levels, sems.at[1]
        ),
        pltpu.make_async_copy(quads_h.at[pl.ds(48 + 2 * piece, 2)], quads.at[pl.ds(12, 2)], sems.at[2]),
        pltpu.make_async_copy(quads_h.at[pl.ds(32 + 4 * piece, 4)], quads.at[pl.ds(8, 4)], sems.at[3]),
        pltpu.make_async_copy(quads_h.at[pl.ds(8 * piece, 8)], quads.at[pl.ds(0, 8)], sems.at[4]),
        pltpu.make_async_copy(pairs_h.at[pl.ds(16 * piece, 16)], pairs, sems.at[5]),
    ]
    for copy in copies:
        copy.start()
    shift = shift_right()
    copies[0].wait()
    copies[1].wait()
    fields = [
        pair_field(levels[:, 128 * p : 128 * p + 128], coupling[p], shift) for p in range(4)
    ]
    for copy in copies[2:]:
        copy.wait()
    state = state3[:, 256 * piece : 256 * piece + 256]
    state = jnp.concatenate(
        [
            with_fields(
                descend(state[:, 128 * q : 128 * q + 128], quads[12 + q]),
                fields[2 * q : 2 * q + 2],
            )
            for q in range(2)
        ],
        1,
    )
    state = jnp.concatenate(
        [descend(state[:, 128 * q : 128 * q + 128], quads[8 + q]) for q in range(4)], 1
    )
    for q in range(8):
        leaf = descend(state[:, 128 * q : 128 * q + 128], quads[q])
        for u in range(2):
            at = 256 * q + 128 * u
            t = descend(leaf[:, 128 * u : 128 * u + 128], pairs[2 * q + u])
            base_out[:, at : at + 128] = t[:64] + near_in[:, at : at + 128]
            top_out[:, at : at + 128] = split(t[64:])


def lower_piece(piece, after, state3, near_in, coupling, levels, quads, pairs):
    return pl.pallas_call(
        functools.partial(lower_kernel, piece),
        out_shape=[
            jax.ShapeDtypeStruct((64, 2048), F32),
            jax.ShapeDtypeStruct((128, 2048), BF16),
        ],
        in_specs=[IN_VMEM] * 3 + [IN_HBM] * 4,
        out_specs=[IN_VMEM] * 2,
        scratch_shapes=[
            VMEM((4, 64, 64), BF16),
            VMEM((64, 512), F32),
            VMEM((14, 256, 128), BF16),
            VMEM((16, 128, 128), BF16),
            pltpu.SemaphoreType.DMA((6,)),
        ],
        compiler_params=params(50),
        cost_estimate=cost(1.5),
        name="lower",
    )(after, state3, near_in, coupling, levels, quads, pairs)


def final_kernel(lift, *refs):
    partners = refs[:8]
    bases = refs[8:12]
    tops = refs[12:16]
    out_h, out, sems = refs[16:]
    g = jnp.zeros((64, 64), F32)
    for height in range(8):
        w = lift[height]
        hi = w.astype(BF16)
        lo = (w - hi.astype(F32)).astype(BF16)
        p = split(partners[height][...])
        g = g + fold(mxu(p, hi, NN)) + mxu(p[:64], lo, NN)
    hi = g.astype(BF16)
    lo = (g - hi.astype(F32)).astype(BF16)
    g = jnp.concatenate(
        [jnp.concatenate([hi, hi], 1), jnp.concatenate([lo, jnp.zeros_like(lo)], 1)], 0
    )
    copies = []
    for piece in range(4):
        for q in range(8):
            at = 256 * q
            out[:, 2048 * piece + at : 2048 * piece + at + 256] = (
                fold(mxu(g, tops[piece][:, at : at + 256], NN)) + bases[piece][:, at : at + 256]
            )
        part = pl.ds(2048 * piece, 2048)
        copies.append(pltpu.make_async_copy(out.at[:, part], out_h.at[:, part], sems.at[piece]))
        copies[-1].start()
    for copy in copies:
        copy.wait()


def final(lift, partners, bases, tops):
    return pl.pallas_call(
        final_kernel,
        out_shape=jax.ShapeDtypeStruct((64, 8192), F32),
        in_specs=[IN_VMEM] * 17,
        out_specs=IN_HBM,
        scratch_shapes=[VMEM((64, 8192), F32), pltpu.SemaphoreType.DMA((4,))],
        compiler_params=params(16),
        cost_estimate=cost(2),
        name="final",
    )(lift, *partners, *bases, *tops)


def exchanged(value, mask):
    devices = lax.axis_size(AXES)
    return lax.ppermute(value, AXES, [(s, s ^ mask) for s in range(devices)])


def dot(a, b):
    return jnp.dot(a, b, precision=HIGH)


def on_device(coords, vectors, bases, transfer, coupling, top_transfer, top_coupling):
    vectors = vectors.T
    device = lax.axis_index(AXES).astype(jnp.int32).reshape(1)
    climbing, levels, pairs, quads = upward(
        bases.transpose(1, 2, 0), vectors, transfer[0].transpose(1, 2, 0)
    )
    top_transfer = top_transfer.transpose(1, 2, 0)
    top_coupling = top_coupling.transpose(1, 2, 0)
    coupling = coupling[0]
    partners, nears, lows = [], [None] * 4, []
    for height, mask in enumerate(MASKS):
        partner = exchanged(climbing, mask)
        if height == 0:
            own0, sib0 = first_pick(climbing, device, top_transfer)
            own, sib = [own0], [sib0]
        elif height == 1:
            nears[0], owns, sibs = second_pick(climbing, device, coords, vectors, top_transfer)
            own += [owns[n] for n in range(6)]
            sib += [sibs[n] for n in range(6)]
        elif height == 2:
            nears[1], lift = lifts(climbing, device, own0, owns, coords, vectors, top_coupling)
        elif height == 3:
            nears[2] = near(2, climbing, coords, vectors)
            state = upper(climbing, coupling, levels, quads)
        elif height == 4:
            nears[3] = near(3, climbing, coords, vectors)
        for piece in BESIDE.get(height, ()):
            lows.append(
                lower_piece(piece, climbing, state, nears[piece], coupling, levels, quads, pairs)
            )
        partners.append(partner)
        if height < 7:
            climbing = dot(climbing, own[height]) + dot(partner, sib[height])
    result = final(lift, partners, [low[0] for low in lows], [low[1] for low in lows])
    return result.T


def solution(mesh):
    both = ("leaf", "sub")
    return jax.shard_map(
        on_device,
        mesh=mesh,
        in_specs=(
            P(None, both),
            P(both, None),
            P(both, None, None),
            P(both, None, None, None),
            P(both, None, None, None),
            P(),
            P(),
        ),
        out_specs=P(both, None),
        check_vma=False,
    )
```

time: 75.7 us -> 76 us (level); the launches traced: 75.6 us -> 74.9 us
  Pallas kernels: 30.5 us -> 50.6 us
  waiting for transfers between devices: 16.8 us -> 2.19 us
  starting transfers between devices: 19.6 us -> 14.6 us
  local copies, waits for them, and re-layouts: 4.66 us -> 0.81 us
  matrix products: 3.58 us -> 6.08 us
    pallas_call x6 -> x11, Pallas kernels: 18.4 us -> 43.4 us  [the longest x4 11 us: lower_piece(): pl.pallas_call(functools.partial(lower_kernel, piece), out_shape=[jax.Sha...]
    ppermute x8, waiting for transfers between devices: 16.8 us -> 2.19 us  [exchanged(): return lax.ppermute(value, AXES, [(s, s ^ mask) for s in range(devices)])]
    ppermute x8, starting transfers between devices: 19.6 us -> 14.6 us  [exchanged(): return lax.ppermute(value, AXES, [(s, s ^ mask) for s in range(devices)])]
    pallas_call x1, Pallas kernels: 12.1 us -> 7.25 us  [upward(): pl.pallas_call(up_kernel, out_shape=[jax.ShapeDtypeStruct((64, 64), F32),...]
    unnamed x30, local copies, waits for them, and re-layouts: 4.66 us -> 0.81 us
    dot_general x22 -> x14, matrix products: 3.58 us -> 6.08 us  [dot(): return jnp.dot(a, b, precision=HIGH)]
  transfers between devices with their start and end apart: 8 -> 8, of which waited for: 7 -> 2; matrix products, arithmetic and copies ran while one was open for 2% -> 2% of each run, Pallas kernels for 13% -> 55%
where the time goes in v1:
time: 76 us; the launch traced here: 74.9 us
  Pallas kernels  50.6 us (67%)
  starting transfers between devices  14.6 us (19%)
  matrix products  6.08 us (8%)
  waiting for transfers between devices  2.19 us (3%)
  local copies, waits for them, and re-layouts  0.81 us (1%)
    ppermute x8, starting transfers between devices, exchanged(): return lax.ppermute(value, AXES, [(s, s ^ mask) for s in range(devices)])  14.6 us
    pallas_call x4, Pallas kernels, lower_piece(): pl.pallas_call(functools.partial(lower_kernel, piece), out_shape=[jax.Sha...  11 us
    pallas_call x2, Pallas kernels, near(): pl.pallas_call(functools.partial(near_kernel, piece), out_shape=jax.Shape...  8.83 us
    pallas_call x1, Pallas kernels, upward(): pl.pallas_call(up_kernel, out_shape=[jax.ShapeDtypeStruct((64, 64), F32),...  7.25 us
    pallas_call x1, Pallas kernels, lifts(): pl.pallas_call(lift_kernel, out_shape=[jax.ShapeDtypeStruct((64, 2048), F...  7.02 us
    dot_general x14, matrix products, dot(): return jnp.dot(a, b, precision=HIGH)  6.08 us
    pallas_call x1, Pallas kernels, second_pick(): pl.pallas_call(second_kernel, out_shape=[jax.ShapeDtypeStruct((64, 2048),...  5.72 us
    pallas_call x1, Pallas kernels, upper(): pl.pallas_call(upper_kernel, out_shape=jax.ShapeDtypeStruct((128, 1024),...  5.52 us
  transfers between devices with their start and end apart: 8, of which 2 were waited for; matrix products, arithmetic and copies ran while one was open for 2% of the time, Pallas kernels for 55%

profile of v1, /device:TPU:24, one launch (start us, length us, event | category | flops | bytes accessed | tf_op | source)
XLA Modules:
  0.0 74.9 jit_solution(6438043388696686951)
XLA Ops:
  0.0 7.2 %upward.1 = (f32[64,64]{1,0:T(8,128)}, f32[64,8064]{1,0:T(8,128)}, bf16[64,128,128]{2,1,0:T(8,128)(2,1)}, bf16[64,256,128]{2,1,0:T(8,128)(2,1)}) custom-call(bf16[64,64,128]{2,1,0:T(8,128)(2,1)} %bitcast.71, bf16[64,8192]{1,0:T(8,128)(2,1)} %bitcast.72, bf16[64,64,254]{2,1,0:T(8,128)(2,1)} %bitcast.69), custom_call_target="tpu_custom_call" | custom-call | flops 8000000000 | bytes 65536 | tf_op jit(solution)/shard_map/upward/pallas_call | solution.py:149
  7.4 3.2 %first_pick.1 = (f32[64,64]{1,0:T(8,128)}, f32[64,64]{1,0:T(8,128)}) custom-call(f32[64,64]{1,0:T(8,128)} %get-tuple-element.24.after, s32[1]{0:T(128)} %bitcast.4.device, bf16[64,64,508]{2,1,0:T(8,128)(2,1)} %bitcast.67), custom_call_target="tpu_custom_call" | custom-call | flops 1000000000 | bytes 65536 | tf_op jit(solution)/shard_map/first_pick/pallas_call | solution.py:278
  10.5 0.9 %fusion.30 = f32[64,64]{1,0:T(8,128)S(1)} fusion(f32[64,64]{1,0:T(8,128)S(1)} %copy-done.12, f32[64,64]{1,0:T(8,128)} %get-tuple-element.25.own0), kind=kOutput, calls=%fused_computation.37 | convolution fusion | flops 3145728 | bytes 49152 | tf_op jit(solution)/shard_map/dot_general | solution.py:596
  11.5 0.9 %convolution_add_fusion.6.after = f32[64,64]{1,0:T(8,128)S(1)} fusion(f32[64,64]{1,0:T(8,128)S(1)} %fusion.30, f32[64,64]{1,0:T(8,128)S(1)} %collective-permute-done.refs_0_, f32[64,64]{1,0:T(8,128)} %get-tuple-element.26), kind=kOutput, calls=%fused_computation.6 | convolution fusion | flops 3149824 | bytes 65536 | tf_op jit(solution)/shard_map/dot_general | solution.py:596
  12.4 1.6 %collective-permute-start.1 = (f32[64,64]{1,0:T(8,128)S(1)}, f32[64,64]{1,0:T(8,128)S(1)}, u32[]{:S(2)}, u32[]{:S(2)}) collective-permute-start(f32[64,64]{1,0:T(8,128)S(1)} %convolution_add_fusion.6.after), channel_id=1, source_target_pairs={{0,2},{1,3},{2,0},{3,1},{4,6},{5,7},{6,4},{7,5},{8,10},{9,11},{10,... | collective-permute-start | bytes 49160 | tf_op jit(solution)/shard_map/ppermute | solution.py:592
  14.0 5.7 %second_pick.1 = (f32[64,2048]{1,0:T(8,128)}, f32[6,64,64]{2,1,0:T(8,128)}, f32[6,64,64]{2,1,0:T(8,128)}) custom-call(f32[64,64]{1,0:T(8,128)} %copy-done.13, s32[1]{0:T(128)} %bitcast.4.device, f32[3,8192]{1,0:T(4,128)} %coords_h.7, bf16[64,8192]{1,0:T(8,128)(2,1)} %bitcast.73, bf16[64,64,508]{2,1,0:T(8,128)(2,1)} %bitcast.68), custom_call_target="tpu_custom_call" | custom-call | flops 2000000000 | bytes 65536 | tf_op jit(solution)/shard_map/second_pick/pallas_call | solution.py:312
  19.7 0.9 %fusion.16 = f32[64,64]{1,0:T(8,128)S(1)} fusion(f32[64,64]{1,0:T(8,128)} %copy-done.13, f32[6,64,64]{2,1,0:T(8,128)} %get-tuple-element.27.own), kind=kOutput, calls=%fused_computation.23 | convolution fusion | flops 3145728 | bytes 81920 | tf_op jit(solution)/shard_map/dot_general | solution.py:596
  20.7 0.9 %convolution_add_fusion.5.after = f32[64,64]{1,0:T(8,128)S(1)} fusion(f32[64,64]{1,0:T(8,128)S(1)} %fusion.16, f32[64,64]{1,0:T(8,128)S(1)} %collective-permute-done.1.refs_1_, f32[6,64,64]{2,1,0:T(8,128)} %get-tuple-element.28), kind=kOutput, calls=%fused_computation.5 | convolution fusion | flops 3149824 | bytes 81920 | tf_op jit(solution)/shard_map/dot_general | solution.py:596
  21.6 0.9 %fusion.13 = f32[64,64]{1,0:T(8,128)S(1)} fusion(f32[64,64]{1,0:T(8,128)S(1)} %convolution_add_fusion.5.after, f32[6,64,64]{2,1,0:T(8,128)} %get-tuple-element.27.own), kind=kOutput, calls=%fused_computation.20 | convolution fusion | flops 3145728 | bytes 65536 | tf_op jit(solution)/shard_map/dot_general | solution.py:596
  22.6 2.2 %collective-permute-start.2 = (f32[64,64]{1,0:T(8,128)S(1)}, f32[64,64]{1,0:T(8,128)S(1)}, u32[]{:S(2)}, u32[]{:S(2)}) collective-permute-start(f32[64,64]{1,0:T(8,128)S(1)} %convolution_add_fusion.5.after), channel_id=1, source_target_pairs={{0,6},{1,7},{2,4},{3,5},{4,2},{5,3},{6,0},{7,1},{8,14},{9,15},{10,... | collective-permute-start | bytes 49160 | tf_op jit(solution)/shard_map/ppermute | solution.py:592
  24.7 7.0 %lifts.1 = (f32[64,2048]{1,0:T(8,128)}, f32[8,64,64]{2,1,0:T(8,128)}) custom-call(f32[64,64]{1,0:T(8,128)} %copy-done.14, s32[1]{0:T(128)} %bitcast.4.device, f32[64,64]{1,0:T(8,128)} %get-tuple-element.25.own0, f32[6,64,64]{2,1,0:T(8,128)} %get-tuple-element.27.own, f32[3,8192]{1,0:T(4,128)} %coords_h.7, bf16[64,8192]{1,0:T(8,128)(2,1)} %bitcast.74, ...), custom_call_target="tpu_custom_call" | custom-call | flops 2000000000 | bytes 65536 | tf_op jit(solution)/shard_map/lifts/pallas_call | solution.py:366
  32.1 2.2 %collective-permute-start.3 = (f32[64,64]{1,0:T(8,128)S(1)}, f32[64,64]{1,0:T(8,128)S(1)}, u32[]{:S(2)}, u32[]{:S(2)}) collective-permute-start(f32[64,64]{1,0:T(8,128)S(1)} %convolution_add_fusion.4.after), channel_id=1, source_target_pairs={{0,8},{1,9},{2,10},{3,11},{4,12},{5,13},{6,14},{7,15},{8,0},{9,1},... | collective-permute-start | bytes 49160 | tf_op jit(solution)/shard_map/ppermute | solution.py:592
  34.3 4.4 %near.2.near_in = f32[64,2048]{1,0:T(8,128)} custom-call(f32[64,64]{1,0:T(8,128)} %copy-done.9, f32[3,8192]{1,0:T(4,128)} %coords_h.7, bf16[64,8192]{1,0:T(8,128)(2,1)} %bitcast.75), custom_call_target="tpu_custom_call" | custom-call | flops 1500000000 | bytes 65536 | tf_op jit(solution)/shard_map/near/pallas_call | solution.py:393
  38.7 5.5 %upper.1.state3 = f32[128,1024]{1,0:T(8,128)} custom-call(f32[64,64]{1,0:T(8,128)} %copy-done.9, bf16[31,64,64]{2,1,0:T(8,128)(2,1)} %bitcast.62, f32[64,8064]{1,0:T(8,128)} %get-tuple-element.30.levels_h, bf16[64,256,128]{2,1,0:T(8,128)(2,1)} %get-tuple-element.31.quads_h), custom_call_target="tpu_custom_call" | custom-call | flops 1500000000 | bytes 65536 | tf_op jit(solution)/shard_map/upper/pallas_call | solution.py:460
  44.7 3.4 %collective-permute-start.4 = (f32[64,64]{1,0:T(8,128)S(1)}, f32[64,64]{1,0:T(8,128)S(1)}, u32[]{:S(2)}, u32[]{:S(2)}) collective-permute-start(f32[64,64]{1,0:T(8,128)S(1)} %convolution_add_fusion.3.after), channel_id=1, source_target_pairs={{0,16},{1,17},{2,18},{3,19},{4,20},{5,21},{6,22},{7,23},{8,24},{9,... | collective-permute-start | bytes 49160 | tf_op jit(solution)/shard_map/ppermute | solution.py:592
  48.0 4.4 %near.3.near_in = f32[64,2048]{1,0:T(8,128)} custom-call(f32[64,64]{1,0:T(8,128)} %copy-done.6, f32[3,8192]{1,0:T(4,128)} %coords_h.7, bf16[64,8192]{1,0:T(8,128)(2,1)} %bitcast.76), custom_call_target="tpu_custom_call" | custom-call | flops 1500000000 | bytes 65536 | tf_op jit(solution)/shard_map/near/pallas_call | solution.py:393
  53.3 2.8 %lower.4 = (f32[64,2048]{1,0:T(8,128)S(1)}, bf16[128,2048]{1,0:T(8,128)(2,1)S(1)}) custom-call(f32[64,64]{1,0:T(8,128)S(1)} %copy-done.7, f32[128,1024]{1,0:T(8,128)S(1)} %copy-done, f32[64,2048]{1,0:T(8,128)S(1)} %copy-done.3, bf16[31,64,64]{2,1,0:T(8,128)(2,1)S(1)} %bitcast.63, f32[64,8064]{1,0:T(8,128)} %get-tuple-element.30.levels_h, ...), custom_call_target="tpu_custom_call" | custom-call | flops 1500000000 | bytes 65536 | tf_op jit(solution)/shard_map/lower/pallas_call | solution.py:525
  56.4 3.7 %collective-permute-start.5 = (f32[64,64]{1,0:T(8,128)S(1)}, f32[64,64]{1,0:T(8,128)S(1)}, u32[]{:S(2)}, u32[]{:S(2)}) collective-permute-start(f32[64,64]{1,0:T(8,128)S(1)} %convolution_add_fusion.2.after), channel_id=1, source_target_pairs={{0,48},{1,49},{2,50},{3,51},{4,52},{5,53},{6,54},{7,55},{8,56},{9,... | collective-permute-start | bytes 49160 | tf_op jit(solution)/shard_map/ppermute | solution.py:592
  60.1 2.8 %lower.5 = (f32[64,2048]{1,0:T(8,128)S(1)}, bf16[128,2048]{1,0:T(8,128)(2,1)S(1)}) custom-call(f32[64,64]{1,0:T(8,128)S(1)} %convolution_add_fusion.2.after, f32[128,1024]{1,0:T(8,128)S(1)} %copy-done, f32[64,2048]{1,0:T(8,128)S(1)} %copy-done.4, bf16[31,64,64]{2,1,0:T(8,128)(2,1)S(1)} %bitcast.64, f32[64,8064]{1,0:T(8,128)} %get-tuple-element.30.levels_h, ...), custom_call_target="tpu_custom_call" | custom-call | flops 1500000000 | bytes 65536 | tf_op jit(solution)/shard_map/lower/pallas_call | solution.py:525
  63.2 0.8 %collective-permute-start.6 = (f32[64,64]{1,0:T(8,128)S(1)}, f32[64,64]{1,0:T(8,128)S(1)}, u32[]{:S(2)}, u32[]{:S(2)}) collective-permute-start(f32[64,64]{1,0:T(8,128)S(1)} %convolution_add_fusion.1.after), channel_id=1, source_target_pairs={{0,64},{1,65},{2,66},{3,67},{4,68},{5,69},{6,70},{7,71},{8,72},{9,... | collective-permute-start | bytes 49160 | tf_op jit(solution)/shard_map/ppermute | solution.py:592
  64.0 2.7 %lower.6 = (f32[64,2048]{1,0:T(8,128)S(1)}, bf16[128,2048]{1,0:T(8,128)(2,1)S(1)}) custom-call(f32[64,64]{1,0:T(8,128)S(1)} %convolution_add_fusion.1.after, f32[128,1024]{1,0:T(8,128)S(1)} %copy-done, f32[64,2048]{1,0:T(8,128)S(1)} %copy-done.5, bf16[31,64,64]{2,1,0:T(8,128)(2,1)S(1)} %bitcast.65, f32[64,8064]{1,0:T(8,128)} %get-tuple-element.30.levels_h, ...), custom_call_target="tpu_custom_call" | custom-call | flops 1500000000 | bytes 65536 | tf_op jit(solution)/shard_map/lower/pallas_call | solution.py:525
  68.1 2.7 %lower.7 = (f32[64,2048]{1,0:T(8,128)S(1)}, bf16[128,2048]{1,0:T(8,128)(2,1)S(1)}) custom-call(f32[64,64]{1,0:T(8,128)S(1)} %convolution_add_fusion.after, f32[128,1024]{1,0:T(8,128)S(1)} %copy-done, f32[64,2048]{1,0:T(8,128)S(1)} %copy-done.2, bf16[31,64,64]{2,1,0:T(8,128)(2,1)S(1)} %bitcast.66, f32[64,8064]{1,0:T(8,128)} %get-tuple-element.30.levels_h, ...), custom_call_target="tpu_custom_call" | custom-call | flops 1500000000 | bytes 65536 | tf_op jit(solution)/shard_map/lower/pallas_call | solution.py:525
  70.8 1.7 %collective-permute-done.7.refs_7_ = f32[64,64]{1,0:T(8,128)S(1)} collective-permute-done((f32[64,64]{1,0:T(8,128)S(1)}, f32[64,64]{1,0:T(8,128)S(1)}, u32[]{:S(2)}, u32[]{:S(2)}) %collective-permute-start.7) | collective-permute-done | bytes 16416 | tf_op jit(solution)/shard_map/ppermute | solution.py:592
  72.6 2.1 %final.1 = f32[64,8192]{1,0:T(8,128)} custom-call(f32[8,64,64]{2,1,0:T(8,128)S(1)} %copy-done.8, f32[64,64]{1,0:T(8,128)S(1)} %collective-permute-done.refs_0_, f32[64,64]{1,0:T(8,128)S(1)} %collective-permute-done.1.refs_1_, f32[64,64]{1,0:T(8,128)S(1)} %collective-permute-done.2.refs_2_, f32[64,64]{1,0:T(8,128)S(1)} %collective-permute-done.3.refs_3_, ...), custom_call_target="tpu_custom_call" | custom-call | flops 2000000000 | bytes 65536 | tf_op jit(solution)/shard_map/final/pallas_call | solution.py:578
  (48 shorter events, 3.5 us)
Async XLA Ops:
  7.3 4.2 %collective-permute-start = (f32[64,64]{1,0:T(8,128)}, f32[64,64]{1,0:T(8,128)S(1)}, u32[]{:S(2)}, u32[]{:S(2)}) collective-permute-start(f32[64,64]{1,0:T(8,128)} %get-tuple-element.24.after), channel_id=1, source_target_pairs={{0,1},{1,0},{2,3},{3,2},{4,5},{5,4},{6,7},{7,6},{8,9},{9,8},{10,11... | collective-permute-start | bytes 49160 | tf_op jit(solution)/shard_map/ppermute | solution.py:592
  7.4 3.2 %copy-start.12 = (f32[64,64]{1,0:T(8,128)S(1)}, f32[64,64]{1,0:T(8,128)}, u32[]{:S(2)}) copy-start(f32[64,64]{1,0:T(8,128)} %get-tuple-element.24.after) | copy-start | bytes 49156
  12.4 1.6 %copy-start.13 = (f32[64,64]{1,0:T(8,128)}, f32[64,64]{1,0:T(8,128)S(1)}, u32[]{:S(2)}) copy-start(f32[64,64]{1,0:T(8,128)S(1)} %convolution_add_fusion.6.after) | copy-start | bytes 49156
  12.4 8.3 %collective-permute-start.1 = (f32[64,64]{1,0:T(8,128)S(1)}, f32[64,64]{1,0:T(8,128)S(1)}, u32[]{:S(2)}, u32[]{:S(2)}) collective-permute-start(f32[64,64]{1,0:T(8,128)S(1)} %convolution_add_fusion.6.after), channel_id=1, source_target_pairs={{0,2},{1,3},{2,0},{3,1},{4,6},{5,7},{6,4},{7,5},{8,10},{9,11},{10,... | collective-permute-start | bytes 49160 | tf_op jit(solution)/shard_map/ppermute | solution.py:592
  21.6 3.1 %copy-start.14 = (f32[64,64]{1,0:T(8,128)}, f32[64,64]{1,0:T(8,128)S(1)}, u32[]{:S(2)}) copy-start(f32[64,64]{1,0:T(8,128)S(1)} %convolution_add_fusion.5.after) | copy-start | bytes 49156
  22.6 9.2 %collective-permute-start.2 = (f32[64,64]{1,0:T(8,128)S(1)}, f32[64,64]{1,0:T(8,128)S(1)}, u32[]{:S(2)}, u32[]{:S(2)}) collective-permute-start(f32[64,64]{1,0:T(8,128)S(1)} %convolution_add_fusion.5.after), channel_id=1, source_target_pairs={{0,6},{1,7},{2,4},{3,5},{4,2},{5,3},{6,0},{7,1},{8,14},{9,15},{10,... | collective-permute-start | bytes 49160 | tf_op jit(solution)/shard_map/ppermute | solution.py:592
  24.7 7.0 %copy-start.11 = (f32[6,64,64]{2,1,0:T(8,128)S(1)}, f32[6,64,64]{2,1,0:T(8,128)}, u32[]{:S(2)}) copy-start(f32[6,64,64]{2,1,0:T(8,128)} %get-tuple-element.28) | copy-start | bytes 294916
  24.7 7.2 %copy-start.10 = (f32[6,64,64]{2,1,0:T(8,128)S(1)}, f32[6,64,64]{2,1,0:T(8,128)}, u32[]{:S(2)}) copy-start(f32[6,64,64]{2,1,0:T(8,128)} %get-tuple-element.27.own) | copy-start | bytes 294916
  32.0 2.4 %copy-start.9 = (f32[64,64]{1,0:T(8,128)}, f32[64,64]{1,0:T(8,128)S(1)}, u32[]{:S(2)}) copy-start(f32[64,64]{1,0:T(8,128)S(1)} %convolution_add_fusion.4.after) | copy-start | bytes 49156
  32.1 12.1 %collective-permute-start.3 = (f32[64,64]{1,0:T(8,128)S(1)}, f32[64,64]{1,0:T(8,128)S(1)}, u32[]{:S(2)}, u32[]{:S(2)}) collective-permute-start(f32[64,64]{1,0:T(8,128)S(1)} %convolution_add_fusion.4.after), channel_id=1, source_target_pairs={{0,8},{1,9},{2,10},{3,11},{4,12},{5,13},{6,14},{7,15},{8,0},{9,1},... | collective-permute-start | bytes 49160 | tf_op jit(solution)/shard_map/ppermute | solution.py:592
  44.4 3.6 %copy-start.6 = (f32[64,64]{1,0:T(8,128)}, f32[64,64]{1,0:T(8,128)S(1)}, u32[]{:S(2)}) copy-start(f32[64,64]{1,0:T(8,128)S(1)} %convolution_add_fusion.3.after) | copy-start | bytes 49156
  44.6 7.8 %copy-start = (f32[128,1024]{1,0:T(8,128)S(1)}, f32[128,1024]{1,0:T(8,128)}, u32[]{:S(2)}) copy-start(f32[128,1024]{1,0:T(8,128)} %upper.1.state3) | copy-start | bytes 1572868
  44.6 7.8 %copy-start.1 = (bf16[1,31,64,64]{3,2,1,0:T(8,128)(2,1)S(1)}, bf16[1,31,64,64]{3,2,1,0:T(8,128)(2,1)}, u32[]{:S(2)}) copy-start(bf16[1,31,64,64]{3,2,1,0:T(8,128)(2,1)} %param.11) | copy-start | bytes 761860
  44.6 7.8 %copy-start.3 = (f32[64,2048]{1,0:T(8,128)S(1)}, f32[64,2048]{1,0:T(8,128)}, u32[]{:S(2)}) copy-start(f32[64,2048]{1,0:T(8,128)} %get-tuple-element.32.near_in) | copy-start | bytes 1572868
  44.7 11.4 %collective-permute-start.4 = (f32[64,64]{1,0:T(8,128)S(1)}, f32[64,64]{1,0:T(8,128)S(1)}, u32[]{:S(2)}, u32[]{:S(2)}) collective-permute-start(f32[64,64]{1,0:T(8,128)S(1)} %convolution_add_fusion.3.after), channel_id=1, source_target_pairs={{0,16},{1,17},{2,18},{3,19},{4,20},{5,21},{6,22},{7,23},{8,24},{9,... | collective-permute-start | bytes 49160 | tf_op jit(solution)/shard_map/ppermute | solution.py:592
  52.5 0.8 %copy-start.7 = (f32[64,64]{1,0:T(8,128)S(1)}, f32[64,64]{1,0:T(8,128)}, u32[]{:S(2)}) copy-start(f32[64,64]{1,0:T(8,128)} %copy-done.6) | copy-start | bytes 49156
  53.3 6.8 %copy-start.4 = (f32[64,2048]{1,0:T(8,128)S(1)}, f32[64,2048]{1,0:T(8,128)}, u32[]{:S(2)}) copy-start(f32[64,2048]{1,0:T(8,128)} %get-tuple-element.35.near_in) | copy-start | bytes 1572868
  56.4 6.5 %collective-permute-start.5 = (f32[64,64]{1,0:T(8,128)S(1)}, f32[64,64]{1,0:T(8,128)S(1)}, u32[]{:S(2)}, u32[]{:S(2)}) collective-permute-start(f32[64,64]{1,0:T(8,128)S(1)} %convolution_add_fusion.2.after), channel_id=1, source_target_pairs={{0,48},{1,49},{2,50},{3,51},{4,52},{5,53},{6,54},{7,55},{8,56},{9,... | collective-permute-start | bytes 49160 | tf_op jit(solution)/shard_map/ppermute | solution.py:592
  60.0 4.0 %copy-start.5 = (f32[64,2048]{1,0:T(8,128)S(1)}, f32[64,2048]{1,0:T(8,128)}, u32[]{:S(2)}) copy-start(f32[64,2048]{1,0:T(8,128)} %near.2.near_in) | copy-start | bytes 1572868
  63.2 4.9 %copy-start.2 = (f32[64,2048]{1,0:T(8,128)S(1)}, f32[64,2048]{1,0:T(8,128)}, u32[]{:S(2)}) copy-start(f32[64,2048]{1,0:T(8,128)} %near.3.near_in) | copy-start | bytes 1572868
  63.2 4.0 %collective-permute-start.6 = (f32[64,64]{1,0:T(8,128)S(1)}, f32[64,64]{1,0:T(8,128)S(1)}, u32[]{:S(2)}, u32[]{:S(2)}) collective-permute-start(f32[64,64]{1,0:T(8,128)S(1)} %convolution_add_fusion.1.after), channel_id=1, source_target_pairs={{0,64},{1,65},{2,66},{3,67},{4,68},{5,69},{6,70},{7,71},{8,72},{9,... | collective-permute-start | bytes 49160 | tf_op jit(solution)/shard_map/ppermute | solution.py:592
  67.4 5.2 %copy-start.8 = (f32[8,64,64]{2,1,0:T(8,128)S(1)}, f32[8,64,64]{2,1,0:T(8,128)}, u32[]{:S(2)}) copy-start(f32[8,64,64]{2,1,0:T(8,128)} %get-tuple-element.29.lift) | copy-start | bytes 393220
  67.4 5.2 %collective-permute-start.7 = (f32[64,64]{1,0:T(8,128)S(1)}, f32[64,64]{1,0:T(8,128)S(1)}, u32[]{:S(2)}, u32[]{:S(2)}) collective-permute-start(f32[64,64]{1,0:T(8,128)S(1)} %convolution_add_fusion.after), channel_id=1, source_target_pairs={{0,192},{1,193},{2,194},{3,195},{4,196},{5,197},{6,198},{7,199},{8... | collective-permute-start | bytes 49160 | tf_op jit(solution)/shard_map/ppermute | solution.py:592

commit v2 on v1

v2 whole, which is shorter than its diff:
```python
import functools

import jax
import jax.numpy as jnp
from jax import lax
from jax.experimental import pallas as pl
from jax.experimental.pallas import tpu as pltpu
from jax.sharding import PartitionSpec as P

F32 = jnp.float32
BF16 = jnp.bfloat16
VMEM = pltpu.VMEM
AXES = ("leaf", "sub")
HIGH = lax.Precision.HIGHEST

STEP = 136
NN = (((1,), (0,)), ((), ()))
NT = (((1,), (1,)), ((), ()))
LEVEL_AT = (None, 0, 4096, 6144, 7168, 7680, 7936)
NODE_AT = (0, 128, 192, 224, 240, 248, 252)
NUGGET_DIAG = 1.5
MASKS = (1, 2, 6, 8, 16, 48, 64, 192)
NEAR_BESIDE = {2: (0, 1), 3: (2,), 5: (3,)}
BESIDE = {5: (0,), 6: (1, 2), 7: (3,)}
CHORD = 2.0 * 1.4426950408889634


def mxu(a, b, dims):
    return lax.dot_general(a, b, dims, preferred_element_type=F32)


def split(c):
    hi = c.astype(BF16)
    lo = (c - hi.astype(F32)).astype(BF16)
    return jnp.concatenate([hi, lo], 0)


def fold(t):
    half = t.shape[0] // 2
    return t[:half] + t[half:]


def half_mask():
    return lax.broadcasted_iota(jnp.int32, (32, 128), 1) < 64


def spread(src, width, lane0, slab, rows):
    for i in rows:
        w = jnp.concatenate([src[i, :, lane0 : lane0 + width], src[i + 32, :, lane0 : lane0 + width]], 0)
        if width < 128:
            w = jnp.concatenate([w, jnp.zeros((128, 128 - width), BF16)], 1)
        slab[pl.ds(i * STEP, 128), :] = w.T.astype(F32)


def box_matrix(slab, box, right, low):
    x = slab[pl.ds(box, 32, stride=STEP), :]
    y = pltpu.roll(x, 64, 1)
    if right:
        return jnp.concatenate([jnp.where(low, 0.0, y), jnp.where(low, 0.0, x)], 0)
    return jnp.concatenate([jnp.where(low, x, 0.0), jnp.where(low, y, 0.0)], 0)


def up_kernel(
    device, bases_h, vectors_h, transfer_h, top_transfer_h, top_coupling_h,
    own_out, table0, table1, table2, levels_h, pairs_h, quads_h,
    bases, vectors, transfer, slab0, slab1, slab2, leaf_coef, levels, pairs, quads, sems, out_sems,
):
    loads = []
    for k in range(4):
        part = pl.ds(16 * (k // 2) + 32 * (k % 2), 16)
        loads.append(pltpu.make_async_copy(bases_h.at[part], bases.at[part], sems.at[k]))
    loads.append(pltpu.make_async_copy(vectors_h, vectors, sems.at[4]))
    loads.append(pltpu.make_async_copy(transfer_h, transfer, sems.at[5]))
    lane0 = pl.multiple_of(128 * (device[0] >> 7), 128)
    tables = [
        (top_transfer_h.at[:, :, pl.ds(lane0, 128)], table0),
        (top_transfer_h.at[:, :, pl.ds(256, 252)], table1),
        (top_coupling_h, table2),
    ]
    loads += [
        pltpu.make_async_copy(src, dst, sems.at[6 + n]) for n, (src, dst) in enumerate(tables)
    ]
    for copy in loads:
        copy.start()
    stores = []

    def store(src, dst):
        copy = pltpu.make_async_copy(src, dst, out_sems.at[len(stores)])
        copy.start()
        stores.append(copy)

    low = half_mask()
    for k in range(2):
        loads[2 * k].wait()
        loads[2 * k + 1].wait()
        spread(bases, 128, 0, slab0, range(16 * k, 16 * k + 16))
    loads[4].wait()
    held = []
    for j in range(64 + DEPTH):
        if j == 16:
            loads[5].wait()
        if j < 64:
            pair = jnp.concatenate(
                [box_matrix(slab0, 2 * j, False, low), box_matrix(slab0, 2 * j + 1, True, low)], 0
            ).astype(BF16)
            pairs[j] = pair
            held.append(pair)
        if 16 <= j < 48:
            spread(transfer, 128, 0, slab1, [j - 16])
        if j >= DEPTH:
            at = 128 * (j - DEPTH)
            leaf_coef[:, at : at + 128] = mxu(vectors[:, at : at + 128], held[j - DEPTH], NN)
    store(pairs, pairs_h)
    steps = [(level, q) for level in range(6) for q in range((128 >> level) // 4)]
    held = []
    for k in range(len(steps) + UP_DEPTH):
        if k < 16:
            spread(transfer, 126, 128, slab2, [2 * k, 2 * k + 1])
        if k < len(steps):
            level, q = steps[k]
            first = NODE_AT[level] + 4 * q
            slab = slab1 if first < 128 else slab2
            quad = jnp.concatenate(
                [box_matrix(slab, (first + u) % 128, u >= 2, low) for u in range(4)], 0
            ).astype(BF16)
            quads[first // 4] = quad
            held.append(quad)
        if k >= UP_DEPTH:
            level, q = steps[k - UP_DEPTH]
            count = 128 >> level
            if level == 0:
                coef = leaf_coef[:, 256 * q : 256 * q + 256]
            else:
                at = LEVEL_AT[level] + 256 * q
                coef = levels[:, at : at + 256]
            at = LEVEL_AT[level + 1] + 128 * q
            levels[:, at : at + 128] = fold(mxu(split(coef), held[k - UP_DEPTH], NN))
            if level < 2 and q == count // 4 - 1:
                part = pl.ds(NODE_AT[level] // 4, count // 4)
                store(quads.at[part], quads_h.at[part])
                part = pl.ds(LEVEL_AT[level + 1], 32 * count)
                store(levels.at[:, part], levels_h.at[:, part])
    last = jnp.concatenate(
        [box_matrix(slab2, 124, False, low), box_matrix(slab2, 125, False, low)], 0
    ).astype(BF16)
    quads[63, :128, :] = last
    quads[63, 128:, :] = jnp.zeros((128, 128), BF16)
    part = pl.ds(48, 16)
    store(quads.at[part], quads_h.at[part])
    part = pl.ds(LEVEL_AT[3], 1920)
    store(levels.at[:, part], levels_h.at[:, part])
    at = LEVEL_AT[6]
    own_out[...] = fold(mxu(split(levels[:, at : at + 128]), last, NN))[:, :64]
    for copy in loads[6:] + stores:
        copy.wait()


def params(mib):
    return pltpu.CompilerParams(vmem_limit_bytes=mib * 2**20)


def cost(us):
    return pl.CostEstimate(flops=int(us * 10**9), bytes_accessed=2**16, transcendentals=0)


UP_MIB = 52
WINDOW_MIB = 12
UP_DEPTH = 4
DEPTH = 2
IN_VMEM = pl.BlockSpec(memory_space=VMEM)
IN_HBM = pl.BlockSpec(memory_space=pl.ANY)
IN_SMEM = pl.BlockSpec(memory_space=pltpu.SMEM)


def upward(device, bases, vectors, transfer, top_transfer, top_coupling):
    return pl.pallas_call(
        up_kernel,
        out_shape=[
            jax.ShapeDtypeStruct((64, 64), F32),
            jax.ShapeDtypeStruct((64, 64, 128), BF16),
            jax.ShapeDtypeStruct((64, 64, 252), BF16),
            jax.ShapeDtypeStruct((64, 64, 255), BF16),
            jax.ShapeDtypeStruct((64, 8064), F32),
            jax.ShapeDtypeStruct((64, 128, 128), BF16),
            jax.ShapeDtypeStruct((64, 256, 128), BF16),
        ],
        in_specs=[IN_SMEM] + [IN_HBM] * 5,
        out_specs=[IN_VMEM] * 4 + [IN_HBM] * 3,
        scratch_shapes=[
            VMEM((64, 64, 128), BF16),
            VMEM((64, 8192), BF16),
            VMEM((64, 64, 254), BF16),
            VMEM((32 * STEP, 128), F32),
            VMEM((32 * STEP, 128), F32),
            VMEM((32 * STEP, 128), F32),
            VMEM((64, 8192), F32),
            VMEM((64, 8064), F32),
            VMEM((64, 128, 128), BF16),
            VMEM((64, 256, 128), BF16),
            pltpu.SemaphoreType.DMA((9,)),
            pltpu.SemaphoreType.DMA((7,)),
        ],
        compiler_params=params(UP_MIB),
        cost_estimate=cost(8),
        name="upward",
    )(device, bases, vectors, transfer, top_transfer, top_coupling)


def pick_rows(table, pick, slab):
    for i in range(16):
        rows = jnp.concatenate(
            [table[2 * i], table[2 * i + 32], table[2 * i + 1], table[2 * i + 33]], 0
        )
        out = mxu(pick, rows, NT)
        slab[pl.ds(48 * i, 16), :] = out[:, :128]
        slab[pl.ds(48 * i + 24, 16), :] = out[:, 128:]


def picked(slab, row):
    x = slab[pl.ds(row, 32, stride=24), :]
    return jnp.concatenate([x, pltpu.roll(x, 64, 1)], 0)[:, :64]


def transfer_pick(dev, heights, lane0, width):
    row = lax.broadcasted_iota(jnp.int32, (16, width), 0)
    col = lax.broadcasted_iota(jnp.int32, (16, width), 1)
    hit = jnp.zeros((16, width), jnp.bool_)
    for n, height in enumerate(heights):
        box = 512 - (512 >> height) + (dev >> height) - lane0
        hit = hit | ((row == n) & (col == box))
        hit = hit | ((row == n + 8) & (col == (box ^ 1)))
    return jnp.where(hit, 1.0, 0.0).astype(BF16)


def thirds(x):
    a = x.astype(BF16).astype(F32)
    b = (x - a).astype(BF16).astype(F32)
    return a, b, x - a - b


def near_field(piece, coords, vectors, out, square_x, left_t, right):
    square_x[0:3, :] = coords[:, 2048 * piece : 2048 * piece + 2048] * CHORD
    square_x[3:8, :] = jnp.zeros((5, 2048), F32)
    x = square_x[...]
    one8 = jnp.where(lax.broadcasted_iota(jnp.int32, (8, 2048), 0) == 0, 1.0, 0.0)
    x1, x2, x3 = thirds(x)
    n1, n2, n3 = thirds(jnp.sum(x * x, axis=0, keepdims=True) * one8)
    left = jnp.concatenate([x1, x1, x2, x2, x1, x3, n1, n2, n3, one8, one8, one8], 0)
    left_t[...] = left.astype(BF16).T
    y1, y2, y3 = -2 * x1, -2 * x2, -2 * x3
    right[...] = jnp.concatenate(
        [y1, y2, y1, y2, y3, y1, one8, one8, one8, n1, n2, n3], 0
    ).astype(BF16)
    eye = (
        lax.broadcasted_iota(jnp.int32, (128, 128), 0)
        == lax.broadcasted_iota(jnp.int32, (128, 128), 1)
    )
    held = []

    def apply(at, side, first, second):
        here = 2048 * piece + at
        v0 = vectors[:, here : here + 128]
        v1 = vectors[:, here + 128 : here + 256]
        out[:, at : at + 128] = mxu(v0, first, NN) + mxu(v1, side, NT)
        out[:, at + 128 : at + 256] = mxu(v0, side, NN) + mxu(v1, second, NN)

    for g in range(8 + DEPTH):
        if g < 8:
            at = 256 * g

            def block(a, b):
                square = mxu(left_t[at + a : at + a + 128, :], right[:, at + b : at + b + 128], NN)
                square = jnp.maximum(square, 1e-30)
                value = jnp.exp2(-(square * lax.rsqrt(square)))
                if a == b:
                    value = jnp.where(eye, NUGGET_DIAG, value)
                return value.astype(BF16)

            held.append((at, block(0, 128), block(0, 0), block(128, 128)))
        if g >= DEPTH:
            apply(*held[g - DEPTH])


NEAR_SCRATCH = [
    VMEM((8, 2048), F32),
    VMEM((2048, 96), BF16),
    VMEM((96, 2048), BF16),
]


def first_kernel(after, device, transfer, own_out, sib_out, slab):
    dev = device[0]
    lane0 = pl.multiple_of(128 * (dev >> 7), 128)
    pick_rows(transfer, transfer_pick(dev, [0], lane0, 128), slab)
    own_out[...] = picked(slab, 0)
    sib_out[...] = picked(slab, 8)


def first_pick(after, device, transfer):
    return pl.pallas_call(
        first_kernel,
        out_shape=[jax.ShapeDtypeStruct((64, 64), F32)] * 2,
        in_specs=[IN_VMEM, IN_SMEM, IN_VMEM],
        out_specs=[IN_VMEM] * 2,
        scratch_shapes=[VMEM((32 * 24, 128), F32)],
        compiler_params=params(WINDOW_MIB),
        cost_estimate=cost(1),
        name="first_pick",
    )(after, device, transfer)


def second_kernel(after, device, transfer, own_out, sib_out, slab):
    dev = device[0]
    pick_rows(transfer, transfer_pick(dev, range(1, 7), 256, 252), slab)
    for n in range(6):
        own_out[n] = picked(slab, n)
        sib_out[n] = picked(slab, 8 + n)


def second_pick(after, device, transfer):
    return pl.pallas_call(
        second_kernel,
        out_shape=[jax.ShapeDtypeStruct((6, 64, 64), F32)] * 2,
        in_specs=[IN_VMEM, IN_SMEM, IN_VMEM],
        out_specs=[IN_VMEM] * 2,
        scratch_shapes=[VMEM((32 * 24, 128), F32)],
        compiler_params=params(WINDOW_MIB),
        cost_estimate=cost(1),
        name="second_pick",
    )(after, device, transfer)


def lift_kernel(after, device, own0, own, table, lift_out, slab):
    dev = device[0]
    row = lax.broadcasted_iota(jnp.int32, (16, 255), 0)
    col = lax.broadcasted_iota(jnp.int32, (16, 255), 1)
    want = 256 - (256 >> row) + (jnp.full_like(row, dev) >> (row + 1))
    pick_rows(table, jnp.where((col == want) & (row < 8), 1.0, 0.0).astype(BF16), slab)
    turned = []
    for level in range(8):
        pair = picked(slab, level)
        odd = (dev >> level) & 1
        turned.append(jnp.where(odd == 1, pair, pair.T).astype(BF16))
    steps = [own0[...].T] + [own[n].T.astype(BF16) for n in range(6)]
    lift_out[0] = turned[0].astype(F32)
    chain = steps[0]
    for level in range(1, 8):
        hi = chain.astype(BF16)
        lo = (chain - hi.astype(F32)).astype(BF16)
        if level < 7:
            chain = mxu(steps[level], hi, NN) + mxu(steps[level], lo, NN)
        lift_out[level] = mxu(turned[level], hi, NN) + mxu(turned[level], lo, NN)


def lifts(after, device, own0, own, coupling):
    return pl.pallas_call(
        lift_kernel,
        out_shape=jax.ShapeDtypeStruct((8, 64, 64), F32),
        in_specs=[IN_VMEM, IN_SMEM, IN_VMEM, IN_VMEM, IN_VMEM],
        out_specs=IN_VMEM,
        scratch_shapes=[VMEM((32 * 24, 128), F32)],
        compiler_params=params(WINDOW_MIB),
        cost_estimate=cost(2),
        name="lifts",
    )(after, device, own0, own, coupling)


def near_kernel(piece, after, coords, vectors, near_out, square_x, left_t, right):
    near_field(piece, coords, vectors, near_out, square_x, left_t, right)


def near(piece, after, coords, vectors):
    return pl.pallas_call(
        functools.partial(near_kernel, piece),
        out_shape=jax.ShapeDtypeStruct((64, 2048), F32),
        in_specs=[IN_VMEM] * 3,
        out_specs=IN_VMEM,
        scratch_shapes=NEAR_SCRATCH,
        compiler_params=params(WINDOW_MIB),
        cost_estimate=cost(1.5),
        name="near",
    )(after, coords, vectors)


def shift_right():
    row = lax.broadcasted_iota(jnp.int32, (64, 128), 0)
    col = lax.broadcasted_iota(jnp.int32, (64, 128), 1)
    return jnp.where(col == row + 64, 1.0, 0.0).astype(BF16)


def pair_fields(coefs, couplings, shift):
    blank = jnp.zeros((64, 128), BF16)
    sides = [jnp.concatenate([mxu(c[...], shift, NN).astype(BF16), blank], 0) for c in couplings]
    parts = [split(c[...]) for c in coefs]
    terms = [(mxu(s, z, NN), mxu(s, z, NT)) for s, z in zip(parts, sides)]
    return [fold(a + b) for a, b in terms]


def with_fields(state, fields):
    return jnp.concatenate([state[:64] + jnp.concatenate(fields, 1), state[64:]], 0)


def descend(state, quad):
    return fold(mxu(split(state), quad, NT))


def upper_kernel(after, coupling, levels, quads, state_out):
    shift = shift_right()

    where = [(level, pair) for level in range(6, 2, -1) for pair in range((64 >> level))]
    found = pair_fields(
        [levels.at[:, pl.ds(LEVEL_AT[level] + 128 * pair, 128)] for level, pair in where],
        [coupling.at[32 - (32 >> (level - 2)) + pair] for level, pair in where],
        shift,
    )
    found = dict(zip(where, found))

    def field(level, pair):
        return found[level, pair]

    unit = jnp.where(
        lax.broadcasted_iota(jnp.int32, (64, 64), 0)
        == lax.broadcasted_iota(jnp.int32, (64, 64), 1),
        1.0,
        0.0,
    ).astype(BF16)
    state = jnp.concatenate([field(6, 0), mxu(unit, quads[63, :128, :64], NT)], 0)
    for level in range(5, 2, -1):
        below = []
        for q in range((128 >> level) // 4):
            s = descend(state[:, 128 * q : 128 * q + 128], quads[NODE_AT[level] // 4 + q])
            below.append(with_fields(s, [field(level, 2 * q), field(level, 2 * q + 1)]))
        state = jnp.concatenate(below, 1)
    state_out[...] = state


def upper(after, coupling, levels, quads):
    return pl.pallas_call(
        upper_kernel,
        out_shape=jax.ShapeDtypeStruct((128, 1024), F32),
        in_specs=[IN_VMEM] * 4,
        out_specs=IN_VMEM,
        compiler_params=params(WINDOW_MIB),
        cost_estimate=cost(1.5),
        name="upper",
    )(after, coupling, levels, quads)


def lower_kernel(piece, after, state3, near_in, coupling, levels, quads, pairs, base_out, top_out):
    shift = shift_right()
    mine = range(4 * piece, 4 * piece + 4)
    fields = pair_fields(
        [levels.at[:, pl.ds(LEVEL_AT[2] + 128 * p, 128)] for p in mine],
        [coupling.at[p] for p in mine],
        shift,
    )
    state = state3[:, 256 * piece : 256 * piece + 256]
    state = jnp.concatenate(
        [
            with_fields(
                descend(state[:, 128 * q : 128 * q + 128], quads[48 + 2 * piece + q]),
                fields[2 * q : 2 * q + 2],
            )
            for q in range(2)
        ],
        1,
    )
    state = jnp.concatenate(
        [descend(state[:, 128 * q : 128 * q + 128], quads[32 + 4 * piece + q]) for q in range(4)], 1
    )
    leaves = []
    for q in range(8 + DEPTH):
        if q < 8:
            leaves.append(descend(state[:, 128 * q : 128 * q + 128], quads[8 * piece + q]))
        if q >= DEPTH:
            for u in range(2):
                pair = 2 * (q - DEPTH) + u
                at = 128 * pair
                t = descend(
                    leaves[q - DEPTH][:, 128 * u : 128 * u + 128], pairs[16 * piece + pair]
                )
                base_out[:, at : at + 128] = t[:64] + near_in[:, at : at + 128]
                top_out[:, at : at + 128] = split(t[64:])


def lower_piece(piece, after, state3, near_in, coupling, levels, quads, pairs):
    return pl.pallas_call(
        functools.partial(lower_kernel, piece),
        out_shape=[
            jax.ShapeDtypeStruct((64, 2048), F32),
            jax.ShapeDtypeStruct((128, 2048), BF16),
        ],
        in_specs=[IN_VMEM] * 7,
        out_specs=[IN_VMEM] * 2,
        compiler_params=params(WINDOW_MIB),
        cost_estimate=cost(1.5),
        name="lower",
    )(after, state3, near_in, coupling, levels, quads, pairs)


def field_term(partner, lift):
    hi = lift.astype(BF16)
    lo = (lift - hi.astype(F32)).astype(BF16)
    p = split(partner)
    return fold(mxu(p, hi, NN)) + mxu(p[:64], lo, NN)


def partial_kernel(after, lift, *refs):
    terms = [field_term(refs[height][...], lift[height]) for height in range(7)]
    refs[7][...] = sum(terms[1:], terms[0])


def partial_field(after, lift, partners):
    return pl.pallas_call(
        partial_kernel,
        out_shape=jax.ShapeDtypeStruct((64, 64), F32),
        in_specs=[IN_VMEM] * 9,
        out_specs=IN_VMEM,
        compiler_params=params(WINDOW_MIB),
        cost_estimate=cost(0.5),
        name="partial_field",
    )(after, lift, *partners)


def final_kernel(lift, partial, partner, *refs):
    bases = refs[:4]
    tops = refs[4:8]
    out_h, out, sems = refs[8:]
    g = partial[...] + field_term(partner[...], lift[7])
    hi = g.astype(BF16)
    lo = (g - hi.astype(F32)).astype(BF16)
    g = jnp.concatenate(
        [jnp.concatenate([hi, hi], 1), jnp.concatenate([lo, jnp.zeros_like(lo)], 1)], 0
    )
    copies = []
    for piece in range(4):
        for q in range(8):
            at = 256 * q
            out[:, 2048 * piece + at : 2048 * piece + at + 256] = (
                fold(mxu(g, tops[piece][:, at : at + 256], NN)) + bases[piece][:, at : at + 256]
            )
        part = pl.ds(2048 * piece, 2048)
        copies.append(pltpu.make_async_copy(out.at[:, part], out_h.at[:, part], sems.at[piece]))
        copies[-1].start()
    for copy in copies:
        copy.wait()


def final(lift, partial, partner, bases, tops):
    return pl.pallas_call(
        final_kernel,
        out_shape=jax.ShapeDtypeStruct((64, 8192), F32),
        in_specs=[IN_VMEM] * 11,
        out_specs=IN_HBM,
        scratch_shapes=[VMEM((64, 8192), F32), pltpu.SemaphoreType.DMA((4,))],
        compiler_params=params(16),
        cost_estimate=cost(2),
        name="final",
    )(lift, partial, partner, *bases, *tops)


def exchanged(value, mask):
    devices = lax.axis_size(AXES)
    return lax.ppermute(value, AXES, [(s, s ^ mask) for s in range(devices)])


def dot(a, b):
    return jnp.dot(a, b, precision=HIGH)


def on_device(coords, vectors, bases, transfer, coupling, top_transfer, top_coupling):
    vectors = vectors.T
    device = lax.axis_index(AXES).astype(jnp.int32).reshape(1)
    climbing, table0, table1, table2, levels, pairs, quads = upward(
        device,
        bases.transpose(1, 2, 0),
        vectors,
        transfer[0].transpose(1, 2, 0),
        top_transfer.transpose(1, 2, 0),
        top_coupling.transpose(1, 2, 0),
    )
    coupling = coupling[0]
    partners, nears, lows = [], [None] * 4, []
    for height, mask in enumerate(MASKS):
        partner = exchanged(climbing, mask)
        if height == 0:
            own0, sib0 = first_pick(climbing, device, table0)
            own, sib = [own0], [sib0]
        elif height == 1:
            owns, sibs = second_pick(climbing, device, table1)
            own += [owns[n] for n in range(6)]
            sib += [sibs[n] for n in range(6)]
        elif height == 3:
            lift = lifts(climbing, device, own0, owns, table2)
        elif height == 4:
            state = upper(climbing, coupling, levels, quads)
        for piece in NEAR_BESIDE.get(height, ()):
            nears[piece] = near(piece, climbing, coords, vectors)
        for piece in BESIDE.get(height, ()):
            lows.append(
                lower_piece(piece, climbing, state, nears[piece], coupling, levels, quads, pairs)
            )
        if height == 7:
            partial = partial_field(climbing, lift, partners)
        partners.append(partner)
        if height < 7:
            climbing = dot(climbing, own[height]) + dot(partner, sib[height])
    result = final(lift, partial, partner, [low[0] for low in lows], [low[1] for low in lows])
    return result.T


def solution(mesh):
    both = ("leaf", "sub")
    return jax.shard_map(
        on_device,
        mesh=mesh,
        in_specs=(
            P(None, both),
            P(both, None),
            P(both, None, None),
            P(both, None, None, None),
            P(both, None, None, None),
            P(),
            P(),
        ),
        out_specs=P(both, None),
        check_vma=False,
    )
```

time: 76 us -> 51.2 us (0.67)
  Pallas kernels: 50.6 us -> 24.4 us
  waiting for transfers between devices: 2.19 us -> 6.42 us
  matrix products: 6.08 us -> 2.28 us
  starting transfers between devices: 14.6 us -> 17.2 us
  local copies, waits for them, and re-layouts: 0.81 us -> 0.04 us
    pallas_call x2 -> x3, Pallas kernels: 12.7 us -> 2.52 us  [the longest x1 1.52 us: lifts(): pl.pallas_call(lift_kernel, out_shape=jax.ShapeDtypeStruct((8, 64, 64), F...]
    pallas_call x4, Pallas kernels: 11 us -> 5.49 us  [lower_piece(): pl.pallas_call(functools.partial(lower_kernel, piece), out_shape=[jax.Sha...]
    pallas_call x2 -> x4, Pallas kernels: 8.83 us -> 3.79 us  [near(): pl.pallas_call(functools.partial(near_kernel, piece), out_shape=jax.Shape...]
    pallas_call x1, Pallas kernels: 5.52 us -> 1.18 us  [upper(): pl.pallas_call(upper_kernel, out_shape=jax.ShapeDtypeStruct((128, 1024),...]
    ppermute x8, waiting for transfers between devices: 2.19 us -> 6.42 us  [exchanged(): return lax.ppermute(value, AXES, [(s, s ^ mask) for s in range(devices)])]
    dot_general x14, matrix products: 6.08 us -> 2.28 us  [dot(): return jnp.dot(a, b, precision=HIGH)]
    pallas_call x1, Pallas kernels: 3.15 us -> 0.46 us  [first_pick(): pl.pallas_call(first_kernel, out_shape=[jax.ShapeDtypeStruct((64, 64), F3...]
    ppermute x8, starting transfers between devices: 14.6 us -> 17.2 us  [exchanged(): return lax.ppermute(value, AXES, [(s, s ^ mask) for s in range(devices)])]
  transfers between devices with their start and end apart: 8 -> 8, of which waited for: 2 -> 6; matrix products, arithmetic and copies ran while one was open for 2% -> 1% of each run, Pallas kernels for 55% -> 26%
where the time goes in v2:
time: 51.2 us; the launch traced here: 50.7 us
  Pallas kernels  24.4 us (48%)
  starting transfers between devices  17.2 us (34%)
  waiting for transfers between devices  6.42 us (13%)
  matrix products  2.28 us (4%)
    ppermute x8, starting transfers between devices, exchanged(): return lax.ppermute(value, AXES, [(s, s ^ mask) for s in range(devices)])  17.2 us
    pallas_call x1, Pallas kernels, upward(): pl.pallas_call(up_kernel, out_shape=[jax.ShapeDtypeStruct((64, 64), F32),...  9.11 us
    ppermute x8, waiting for transfers between devices, exchanged(): return lax.ppermute(value, AXES, [(s, s ^ mask) for s in range(devices)])  6.42 us
    pallas_call x4, Pallas kernels, lower_piece(): pl.pallas_call(functools.partial(lower_kernel, piece), out_shape=[jax.Sha...  5.49 us
    pallas_call x4, Pallas kernels, near(): pl.pallas_call(functools.partial(near_kernel, piece), out_shape=jax.Shape...  3.79 us
    dot_general x14, matrix products, dot(): return jnp.dot(a, b, precision=HIGH)  2.28 us
    pallas_call x1, Pallas kernels, final(): pl.pallas_call(final_kernel, out_shape=jax.ShapeDtypeStruct((64, 8192), F...  1.82 us
    pallas_call x1, Pallas kernels, lifts(): pl.pallas_call(lift_kernel, out_shape=jax.ShapeDtypeStruct((8, 64, 64), F...  1.52 us
  transfers between devices with their start and end apart: 8, of which 6 were waited for; matrix products, arithmetic and copies ran while one was open for 1% of the time, Pallas kernels for 26%

profile of v2, /device:TPU:24, one launch (start us, length us, event | category | flops | bytes accessed | tf_op | source)
XLA Modules:
  0.0 50.7 jit_solution(4323241432170792695)
XLA Ops:
  0.0 9.1 %upward.1 = (f32[64,64]{1,0:T(8,128)S(1)}, bf16[64,64,128]{2,1,0:T(8,128)(2,1)S(1)}, bf16[64,64,252]{2,1,0:T(8,128)(2,1)}, bf16[64,64,255]{2,1,0:T(8,128)(2,1)},...) custom-call(s32[1]{0:T(128)} %bitcast.device, bf16[64,64,128]{2,1,0:T(8,128)(2,1)} %bitcast.75, ...), custom_call_target="tpu_custom_call" | custom-call | flops 8000000000 | bytes 65536 | tf_op jit(solution)/shard_map/upward/pallas_call | solution.py:176
  9.9 0.5 %collective-permute-done.refs_0_ = f32[64,64]{1,0:T(8,128)S(1)} collective-permute-done((f32[64,64]{1,0:T(8,128)S(1)}, f32[64,64]{1,0:T(8,128)S(1)}, u32[]{:S(2)}, u32[]{:S(2)}) %collective-permute-start) | collective-permute-done | bytes 16416 | tf_op jit(solution)/shard_map/ppermute | solution.py:564
  10.6 1.6 %collective-permute-start.1 = (f32[64,64]{1,0:T(8,128)S(1)}, f32[64,64]{1,0:T(8,128)S(1)}, u32[]{:S(2)}, u32[]{:S(2)}) collective-permute-start(f32[64,64]{1,0:T(8,128)S(1)} %convolution_add_fusion.6.after), channel_id=1, source_target_pairs={{0,2},{1,3},{2,0},{3,1},{4,6},{5,7},{6,4},{7,5},{8,10},{9,11},{10,... | collective-permute-start | bytes 49160 | tf_op jit(solution)/shard_map/ppermute | solution.py:564
  12.2 0.8 %second_pick.1 = (f32[6,64,64]{2,1,0:T(8,128)S(1)}, f32[6,64,64]{2,1,0:T(8,128)S(1)}) custom-call(f32[64,64]{1,0:T(8,128)S(1)} %convolution_add_fusion.6.after, s32[1]{0:T(128)} %bitcast.device, bf16[64,64,252]{2,1,0:T(8,128)(2,1)S(1)} %copy-done.6), custom_call_target="tpu_custom_call" | custom-call | flops 1000000000 | bytes 65536 | tf_op jit(solution)/shard_map/second_pick/pallas_call | solution.py:321
  13.1 1.5 %collective-permute-done.1.refs_1_ = f32[64,64]{1,0:T(8,128)S(1)} collective-permute-done((f32[64,64]{1,0:T(8,128)S(1)}, f32[64,64]{1,0:T(8,128)S(1)}, u32[]{:S(2)}, u32[]{:S(2)}) %collective-permute-start.1) | collective-permute-done | bytes 16416 | tf_op jit(solution)/shard_map/ppermute | solution.py:564
  14.9 2.8 %collective-permute-start.2 = (f32[64,64]{1,0:T(8,128)S(1)}, f32[64,64]{1,0:T(8,128)S(1)}, u32[]{:S(2)}, u32[]{:S(2)}) collective-permute-start(f32[64,64]{1,0:T(8,128)S(1)} %convolution_add_fusion.5.after), channel_id=1, source_target_pairs={{0,6},{1,7},{2,4},{3,5},{4,2},{5,3},{6,0},{7,1},{8,14},{9,15},{10,... | collective-permute-start | bytes 49160 | tf_op jit(solution)/shard_map/ppermute | solution.py:564
  17.8 0.9 %near.5.near_in = f32[64,2048]{1,0:T(8,128)S(1)} custom-call(f32[64,64]{1,0:T(8,128)S(1)} %convolution_add_fusion.5.after, f32[3,8192]{1,0:T(4,128)S(1)} %copy-done.5, bf16[64,8192]{1,0:T(8,128)(2,1)S(1)} %bitcast.68), custom_call_target="tpu_custom_call" | custom-call | flops 1500000000 | bytes 65536 | tf_op jit(solution)/shard_map/near/pallas_call | solution.py:373
  18.8 0.9 %near.4.near_in = f32[64,2048]{1,0:T(8,128)S(1)} custom-call(f32[64,64]{1,0:T(8,128)S(1)} %convolution_add_fusion.5.after, f32[3,8192]{1,0:T(4,128)S(1)} %copy-done.5, bf16[64,8192]{1,0:T(8,128)(2,1)S(1)} %bitcast.69), custom_call_target="tpu_custom_call" | custom-call | flops 1500000000 | bytes 65536 | tf_op jit(solution)/shard_map/near/pallas_call | solution.py:373
  20.5 2.0 %collective-permute-start.3 = (f32[64,64]{1,0:T(8,128)S(1)}, f32[64,64]{1,0:T(8,128)S(1)}, u32[]{:S(2)}, u32[]{:S(2)}) collective-permute-start(f32[64,64]{1,0:T(8,128)S(1)} %convolution_add_fusion.4.after), channel_id=1, source_target_pairs={{0,8},{1,9},{2,10},{3,11},{4,12},{5,13},{6,14},{7,15},{8,0},{9,1},... | collective-permute-start | bytes 49160 | tf_op jit(solution)/shard_map/ppermute | solution.py:564
  22.5 1.5 %lifts.1.lift = f32[8,64,64]{2,1,0:T(8,128)S(1)} custom-call(f32[64,64]{1,0:T(8,128)S(1)} %convolution_add_fusion.4.after, s32[1]{0:T(128)} %bitcast.device, f32[64,64]{1,0:T(8,128)S(1)} %get-tuple-element.26.own0, f32[6,64,64]{2,1,0:T(8,128)S(1)} %get-tuple-element.29.own, bf16[64,64,255]{2,1,0:T(8,128)(2,1)S(1)} %copy-done.7), custom_call_target="tpu_custom_call" | custom-call | flops 2000000000 | bytes 65536 | tf_op jit(solution)/shard_map/lifts/pallas_call | solution.py:356
  24.0 1.0 %near.6.near_in = f32[64,2048]{1,0:T(8,128)S(1)} custom-call(f32[64,64]{1,0:T(8,128)S(1)} %convolution_add_fusion.4.after, f32[3,8192]{1,0:T(4,128)S(1)} %copy-done.5, bf16[64,8192]{1,0:T(8,128)(2,1)S(1)} %bitcast.70), custom_call_target="tpu_custom_call" | custom-call | flops 1500000000 | bytes 65536 | tf_op jit(solution)/shard_map/near/pallas_call | solution.py:373
  25.3 3.4 %collective-permute-start.4 = (f32[64,64]{1,0:T(8,128)S(1)}, f32[64,64]{1,0:T(8,128)S(1)}, u32[]{:S(2)}, u32[]{:S(2)}) collective-permute-start(f32[64,64]{1,0:T(8,128)S(1)} %convolution_add_fusion.3.after), channel_id=1, source_target_pairs={{0,16},{1,17},{2,18},{3,19},{4,20},{5,21},{6,22},{7,23},{8,24},{9,... | collective-permute-start | bytes 49160 | tf_op jit(solution)/shard_map/ppermute | solution.py:564
  28.7 1.2 %upper.1.state3 = f32[128,1024]{1,0:T(8,128)S(1)} custom-call(f32[64,64]{1,0:T(8,128)S(1)} %convolution_add_fusion.3.after, bf16[31,64,64]{2,1,0:T(8,128)(2,1)S(1)} %bitcast.62, f32[64,8064]{1,0:T(8,128)S(1)} %copy-done.1, bf16[64,256,128]{2,1,0:T(8,128)(2,1)S(1)} %copy-done), custom_call_target="tpu_custom_call" | custom-call | flops 1500000000 | bytes 65536 | tf_op jit(solution)/shard_map/upper/pallas_call | solution.py:438
  29.9 0.7 %collective-permute-done.4.refs_4_ = f32[64,64]{1,0:T(8,128)S(1)} collective-permute-done((f32[64,64]{1,0:T(8,128)S(1)}, f32[64,64]{1,0:T(8,128)S(1)}, u32[]{:S(2)}, u32[]{:S(2)}) %collective-permute-start.4) | collective-permute-done | bytes 16416 | tf_op jit(solution)/shard_map/ppermute | solution.py:564
  30.9 5.7 %collective-permute-start.5 = (f32[64,64]{1,0:T(8,128)S(1)}, f32[64,64]{1,0:T(8,128)S(1)}, u32[]{:S(2)}, u32[]{:S(2)}) collective-permute-start(f32[64,64]{1,0:T(8,128)S(1)} %convolution_add_fusion.2.after), channel_id=1, source_target_pairs={{0,48},{1,49},{2,50},{3,51},{4,52},{5,53},{6,54},{7,55},{8,56},{9,... | collective-permute-start | bytes 49160 | tf_op jit(solution)/shard_map/ppermute | solution.py:564
  36.6 0.9 %near.7.near_in = f32[64,2048]{1,0:T(8,128)S(1)} custom-call(f32[64,64]{1,0:T(8,128)S(1)} %convolution_add_fusion.2.after, f32[3,8192]{1,0:T(4,128)S(1)} %copy-done.5, bf16[64,8192]{1,0:T(8,128)(2,1)S(1)} %bitcast.71), custom_call_target="tpu_custom_call" | custom-call | flops 1500000000 | bytes 65536 | tf_op jit(solution)/shard_map/near/pallas_call | solution.py:373
  37.6 1.4 %lower.4 = (f32[64,2048]{1,0:T(8,128)S(1)}, bf16[128,2048]{1,0:T(8,128)(2,1)S(1)}) custom-call(f32[64,64]{1,0:T(8,128)S(1)} %convolution_add_fusion.2.after, f32[128,1024]{1,0:T(8,128)S(1)} %upper.1.state3, f32[64,2048]{1,0:T(8,128)S(1)} %near.4.near_in, bf16[31,64,64]{2,1,0:T(8,128)(2,1)S(1)} %bitcast.63, f32[64,8064]{1,0:T(8,128)S(1)} %copy-done.1, ...), custom_call_target="tpu_custom_call" | custom-call | flops 1500000000 | bytes 65536 | tf_op jit(solution)/shard_map/lower/pallas_call | solution.py:487
  39.3 0.8 %collective-permute-start.6 = (f32[64,64]{1,0:T(8,128)S(1)}, f32[64,64]{1,0:T(8,128)S(1)}, u32[]{:S(2)}, u32[]{:S(2)}) collective-permute-start(f32[64,64]{1,0:T(8,128)S(1)} %convolution_add_fusion.1.after), channel_id=1, source_target_pairs={{0,64},{1,65},{2,66},{3,67},{4,68},{5,69},{6,70},{7,71},{8,72},{9,... | collective-permute-start | bytes 49160 | tf_op jit(solution)/shard_map/ppermute | solution.py:564
  40.2 1.4 %lower.5 = (f32[64,2048]{1,0:T(8,128)S(1)}, bf16[128,2048]{1,0:T(8,128)(2,1)S(1)}) custom-call(f32[64,64]{1,0:T(8,128)S(1)} %convolution_add_fusion.1.after, f32[128,1024]{1,0:T(8,128)S(1)} %upper.1.state3, f32[64,2048]{1,0:T(8,128)S(1)} %near.5.near_in, bf16[31,64,64]{2,1,0:T(8,128)(2,1)S(1)} %bitcast.64, f32[64,8064]{1,0:T(8,128)S(1)} %copy-done.1, ...), custom_call_target="tpu_custom_call" | custom-call | flops 1500000000 | bytes 65536 | tf_op jit(solution)/shard_map/lower/pallas_call | solution.py:487
  41.5 1.4 %lower.6 = (f32[64,2048]{1,0:T(8,128)S(1)}, bf16[128,2048]{1,0:T(8,128)(2,1)S(1)}) custom-call(f32[64,64]{1,0:T(8,128)S(1)} %convolution_add_fusion.1.after, f32[128,1024]{1,0:T(8,128)S(1)} %upper.1.state3, f32[64,2048]{1,0:T(8,128)S(1)} %near.6.near_in, bf16[31,64,64]{2,1,0:T(8,128)(2,1)S(1)} %bitcast.65, f32[64,8064]{1,0:T(8,128)S(1)} %copy-done.1, ...), custom_call_target="tpu_custom_call" | custom-call | flops 1500000000 | bytes 65536 | tf_op jit(solution)/shard_map/lower/pallas_call | solution.py:487
  43.5 0.7 %collective-permute-start.7 = (f32[64,64]{1,0:T(8,128)S(1)}, f32[64,64]{1,0:T(8,128)S(1)}, u32[]{:S(2)}, u32[]{:S(2)}) collective-permute-start(f32[64,64]{1,0:T(8,128)S(1)} %convolution_add_fusion.after), channel_id=1, source_target_pairs={{0,192},{1,193},{2,194},{3,195},{4,196},{5,197},{6,198},{7,199},{8... | collective-permute-start | bytes 49160 | tf_op jit(solution)/shard_map/ppermute | solution.py:564
  44.2 1.4 %lower.7 = (f32[64,2048]{1,0:T(8,128)S(1)}, bf16[128,2048]{1,0:T(8,128)(2,1)S(1)}) custom-call(f32[64,64]{1,0:T(8,128)S(1)} %convolution_add_fusion.after, f32[128,1024]{1,0:T(8,128)S(1)} %upper.1.state3, f32[64,2048]{1,0:T(8,128)S(1)} %near.7.near_in, bf16[31,64,64]{2,1,0:T(8,128)(2,1)S(1)} %bitcast.66, f32[64,8064]{1,0:T(8,128)S(1)} %copy-done.1, ...), custom_call_target="tpu_custom_call" | custom-call | flops 1500000000 | bytes 65536 | tf_op jit(solution)/shard_map/lower/pallas_call | solution.py:487
  45.9 2.8 %collective-permute-done.7.partner = f32[64,64]{1,0:T(8,128)S(1)} collective-permute-done((f32[64,64]{1,0:T(8,128)S(1)}, f32[64,64]{1,0:T(8,128)S(1)}, u32[]{:S(2)}, u32[]{:S(2)}) %collective-permute-start.7) | collective-permute-done | bytes 16416 | tf_op jit(solution)/shard_map/ppermute | solution.py:564
  48.7 1.8 %final.1 = f32[64,8192]{1,0:T(8,128)} custom-call(f32[8,64,64]{2,1,0:T(8,128)S(1)} %lifts.1.lift, f32[64,64]{1,0:T(8,128)S(1)} %partial_field.1.partial, f32[64,64]{1,0:T(8,128)S(1)} %collective-permute-done.7.partner, f32[64,2048]{1,0:T(8,128)S(1)} %get-tuple-element.35.refs_0_, f32[64,2048]{1,0:T(8,128)S(1)} %get-tuple-element.36.refs_1_, ...), custom_call_target="tpu_custom_call" | custom-call | flops 2000000000 | bytes 65536 | tf_op jit(solution)/shard_map/final/pallas_call | solution.py:550
  (37 shorter events, 4.0 us)
Async XLA Ops:
  9.1 3.1 %copy-start.6 = (bf16[64,64,252]{2,1,0:T(8,128)(2,1)S(1)}, bf16[64,64,252]{2,1,0:T(8,128)(2,1)}, u32[]{:S(2)}) copy-start(bf16[64,64,252]{2,1,0:T(8,128)(2,1)} %get-tuple-element.28.transfer) | copy-start | bytes 6193156
  9.1 1.3 %collective-permute-start = (f32[64,64]{1,0:T(8,128)S(1)}, f32[64,64]{1,0:T(8,128)S(1)}, u32[]{:S(2)}, u32[]{:S(2)}) collective-permute-start(f32[64,64]{1,0:T(8,128)S(1)} %get-tuple-element.24.after), channel_id=1, source_target_pairs={{0,1},{1,0},{2,3},{3,2},{4,5},{5,4},{6,7},{7,6},{8,9},{9,8},{10,11... | collective-permute-start | bytes 49160 | tf_op jit(solution)/shard_map/ppermute | solution.py:564
  9.9 7.9 %copy-start.4 = (bf16[8192,64]{0,1:T(8,128)(2,1)S(1)}, bf16[8192,64]{0,1:T(8,128)(2,1)}, u32[]{:S(2)}) copy-start(bf16[8192,64]{0,1:T(8,128)(2,1)} %param.8) | copy-start | bytes 3145732
  9.9 7.9 %copy-start.5 = (f32[3,8192]{1,0:T(4,128)S(1)}, f32[3,8192]{1,0:T(4,128)}, u32[]{:S(2)}) copy-start(f32[3,8192]{1,0:T(4,128)} %coords.7) | copy-start | bytes 294916
  10.6 4.0 %collective-permute-start.1 = (f32[64,64]{1,0:T(8,128)S(1)}, f32[64,64]{1,0:T(8,128)S(1)}, u32[]{:S(2)}, u32[]{:S(2)}) collective-permute-start(f32[64,64]{1,0:T(8,128)S(1)} %convolution_add_fusion.6.after), channel_id=1, source_target_pairs={{0,2},{1,3},{2,0},{3,1},{4,6},{5,7},{6,4},{7,5},{8,10},{9,11},{10,... | collective-permute-start | bytes 49160 | tf_op jit(solution)/shard_map/ppermute | solution.py:564
  14.9 5.2 %collective-permute-start.2 = (f32[64,64]{1,0:T(8,128)S(1)}, f32[64,64]{1,0:T(8,128)S(1)}, u32[]{:S(2)}, u32[]{:S(2)}) collective-permute-start(f32[64,64]{1,0:T(8,128)S(1)} %convolution_add_fusion.5.after), channel_id=1, source_target_pairs={{0,6},{1,7},{2,4},{3,5},{4,2},{5,3},{6,0},{7,1},{8,14},{9,15},{10,... | collective-permute-start | bytes 49160 | tf_op jit(solution)/shard_map/ppermute | solution.py:564
  18.7 3.8 %copy-start.7 = (bf16[64,64,255]{2,1,0:T(8,128)(2,1)S(1)}, bf16[64,64,255]{2,1,0:T(8,128)(2,1)}, u32[]{:S(2)}) copy-start(bf16[64,64,255]{2,1,0:T(8,128)(2,1)} %get-tuple-element.31.table) | copy-start | bytes 6266884
  20.5 4.5 %collective-permute-start.3 = (f32[64,64]{1,0:T(8,128)S(1)}, f32[64,64]{1,0:T(8,128)S(1)}, u32[]{:S(2)}, u32[]{:S(2)}) collective-permute-start(f32[64,64]{1,0:T(8,128)S(1)} %convolution_add_fusion.4.after), channel_id=1, source_target_pairs={{0,8},{1,9},{2,10},{3,11},{4,12},{5,13},{6,14},{7,15},{8,0},{9,1},... | collective-permute-start | bytes 49160 | tf_op jit(solution)/shard_map/ppermute | solution.py:564
  22.5 6.2 %copy-start.1 = (f32[64,8064]{1,0:T(8,128)S(1)}, f32[64,8064]{1,0:T(8,128)}, u32[]{:S(2)}) copy-start(f32[64,8064]{1,0:T(8,128)} %get-tuple-element.32.levels) | copy-start | bytes 6193156
  24.0 4.7 %copy-start = (bf16[64,256,128]{2,1,0:T(8,128)(2,1)S(1)}, bf16[64,256,128]{2,1,0:T(8,128)(2,1)}, u32[]{:S(2)}) copy-start(bf16[64,256,128]{2,1,0:T(8,128)(2,1)} %get-tuple-element.33.quads) | copy-start | bytes 12582916
  24.0 4.7 %copy-start.3 = (bf16[1,31,64,64]{3,2,1,0:T(8,128)(2,1)S(1)}, bf16[1,31,64,64]{3,2,1,0:T(8,128)(2,1)}, u32[]{:S(2)}) copy-start(bf16[1,31,64,64]{3,2,1,0:T(8,128)(2,1)} %param.11) | copy-start | bytes 761860
  25.3 5.2 %collective-permute-start.4 = (f32[64,64]{1,0:T(8,128)S(1)}, f32[64,64]{1,0:T(8,128)S(1)}, u32[]{:S(2)}, u32[]{:S(2)}) collective-permute-start(f32[64,64]{1,0:T(8,128)S(1)} %convolution_add_fusion.3.after), channel_id=1, source_target_pairs={{0,16},{1,17},{2,18},{3,19},{4,20},{5,21},{6,22},{7,23},{8,24},{9,... | collective-permute-start | bytes 49160 | tf_op jit(solution)/shard_map/ppermute | solution.py:564
  30.9 6.7 %copy-start.2 = (bf16[64,128,128]{2,1,0:T(8,128)(2,1)S(1)}, bf16[64,128,128]{2,1,0:T(8,128)(2,1)}, u32[]{:S(2)}) copy-start(bf16[64,128,128]{2,1,0:T(8,128)(2,1)} %get-tuple-element.34.pairs) | copy-start | bytes 6291460
  30.9 8.1 %collective-permute-start.5 = (f32[64,64]{1,0:T(8,128)S(1)}, f32[64,64]{1,0:T(8,128)S(1)}, u32[]{:S(2)}, u32[]{:S(2)}) collective-permute-start(f32[64,64]{1,0:T(8,128)S(1)} %convolution_add_fusion.2.after), channel_id=1, source_target_pairs={{0,48},{1,49},{2,50},{3,51},{4,52},{5,53},{6,54},{7,55},{8,56},{9,... | collective-permute-start | bytes 49160 | tf_op jit(solution)/shard_map/ppermute | solution.py:564
  39.3 4.0 %collective-permute-start.6 = (f32[64,64]{1,0:T(8,128)S(1)}, f32[64,64]{1,0:T(8,128)S(1)}, u32[]{:S(2)}, u32[]{:S(2)}) collective-permute-start(f32[64,64]{1,0:T(8,128)S(1)} %convolution_add_fusion.1.after), channel_id=1, source_target_pairs={{0,64},{1,65},{2,66},{3,67},{4,68},{5,69},{6,70},{7,71},{8,72},{9,... | collective-permute-start | bytes 49160 | tf_op jit(solution)/shard_map/ppermute | solution.py:564
  43.5 5.2 %collective-permute-start.7 = (f32[64,64]{1,0:T(8,128)S(1)}, f32[64,64]{1,0:T(8,128)S(1)}, u32[]{:S(2)}, u32[]{:S(2)}) collective-permute-start(f32[64,64]{1,0:T(8,128)S(1)} %convolution_add_fusion.after), channel_id=1, source_target_pairs={{0,192},{1,193},{2,194},{3,195},{4,196},{5,197},{6,198},{7,199},{8... | collective-permute-start | bytes 49160 | tf_op jit(solution)/shard_map/ppermute | solution.py:564

commit v3 on v2

--- a/solution.py
+++ b/solution.py
@@ -19,9 +19,6 @@
 LEVEL_AT = (None, 0, 4096, 6144, 7168, 7680, 7936)
 NODE_AT = (0, 128, 192, 224, 240, 248, 252)
 NUGGET_DIAG = 1.5
-MASKS = (1, 2, 6, 8, 16, 48, 64, 192)
-NEAR_BESIDE = {2: (0, 1), 3: (2,), 5: (3,)}
-BESIDE = {5: (0,), 6: (1, 2), 7: (3,)}
 CHORD = 2.0 * 1.4426950408889634
 
 
@@ -61,8 +58,8 @@
 
 
 def up_kernel(
-    device, bases_h, vectors_h, transfer_h, top_transfer_h, top_coupling_h,
-    own_out, table0, table1, table2, levels_h, pairs_h, quads_h,
+    device, bases_h, vectors_h, transfer_h, top_transfer_h,
+    own_out, table0, table1, levels_h, pairs_h, quads_h,
     bases, vectors, transfer, slab0, slab1, slab2, leaf_coef, levels, pairs, quads, sems, out_sems,
 ):
     loads = []
@@ -75,7 +72,6 @@
     tables = [
         (top_transfer_h.at[:, :, pl.ds(lane0, 128)], table0),
         (top_transfer_h.at[:, :, pl.ds(256, 252)], table1),
-        (top_coupling_h, table2),
     ]
     loads += [
         pltpu.make_async_copy(src, dst, sems.at[6 + n]) for n, (src, dst) in enumerate(tables)
@@ -138,8 +134,9 @@
             if level < 2 and q == count // 4 - 1:
                 part = pl.ds(NODE_AT[level] // 4, count // 4)
                 store(quads.at[part], quads_h.at[part])
-                part = pl.ds(LEVEL_AT[level + 1], 32 * count)
-                store(levels.at[:, part], levels_h.at[:, part])
+                if level == 1:
+                    part = pl.ds(LEVEL_AT[2], 2048)
+                    store(levels.at[:, part], levels_h.at[:, pl.ds(0, 2048)])
     last = jnp.concatenate(
         [box_matrix(slab2, 124, False, low), box_matrix(slab2, 125, False, low)], 0
     ).astype(BF16)
@@ -148,7 +145,7 @@
     part = pl.ds(48, 16)
     store(quads.at[part], quads_h.at[part])
     part = pl.ds(LEVEL_AT[3], 1920)
-    store(levels.at[:, part], levels_h.at[:, part])
+    store(levels.at[:, part], levels_h.at[:, pl.ds(2048, 1920)])
     at = LEVEL_AT[6]
     own_out[...] = fold(mxu(split(levels[:, at : at + 128]), last, NN))[:, :64]
     for copy in loads[6:] + stores:
@@ -172,20 +169,19 @@
 IN_SMEM = pl.BlockSpec(memory_space=pltpu.SMEM)
 
 
-def upward(device, bases, vectors, transfer, top_transfer, top_coupling):
+def upward(device, bases, vectors, transfer, top_transfer):
     return pl.pallas_call(
         up_kernel,
         out_shape=[
             jax.ShapeDtypeStruct((64, 64), F32),
             jax.ShapeDtypeStruct((64, 64, 128), BF16),
             jax.ShapeDtypeStruct((64, 64, 252), BF16),
-            jax.ShapeDtypeStruct((64, 64, 255), BF16),
-            jax.ShapeDtypeStruct((64, 8064), F32),
+            jax.ShapeDtypeStruct((64, 3968), F32),
             jax.ShapeDtypeStruct((64, 128, 128), BF16),
             jax.ShapeDtypeStruct((64, 256, 128), BF16),
         ],
-        in_specs=[IN_SMEM] + [IN_HBM] * 5,
-        out_specs=[IN_VMEM] * 4 + [IN_HBM] * 3,
+        in_specs=[IN_SMEM] + [IN_HBM] * 4,
+        out_specs=[IN_VMEM] * 3 + [IN_HBM] * 3,
         scratch_shapes=[
             VMEM((64, 64, 128), BF16),
             VMEM((64, 8192), BF16),
@@ -197,13 +193,13 @@
             VMEM((64, 8064), F32),
             VMEM((64, 128, 128), BF16),
             VMEM((64, 256, 128), BF16),
-            pltpu.SemaphoreType.DMA((9,)),
+            pltpu.SemaphoreType.DMA((8,)),
             pltpu.SemaphoreType.DMA((7,)),
         ],
         compiler_params=params(UP_MIB),
         cost_estimate=cost(8),
         name="upward",
-    )(device, bases, vectors, transfer, top_transfer, top_coupling)
+    )(device, bases, vectors, transfer, top_transfer)
 
 
 def pick_rows(table, pick, slab):
@@ -229,6 +225,10 @@
         box = 512 - (512 >> height) + (dev >> height) - lane0
         hit = hit | ((row == n) & (col == box))
         hit = hit | ((row == n + 8) & (col == (box ^ 1)))
+        if height in (1, 6):
+            extra = 6 if height == 1 else 14
+            hit = hit | ((row == extra) & (col == (box ^ 2)))
+            hit = hit | ((row == extra + 1) & (col == (box ^ 3)))
     return jnp.where(hit, 1.0, 0.0).astype(BF16)
 
 
@@ -309,25 +309,56 @@
     )(after, device, transfer)
 
 
-def second_kernel(after, device, transfer, own_out, sib_out, slab):
+def second_kernel(after, device, transfer, own_out, sib_out, quad_out, slab):
     dev = device[0]
     pick_rows(transfer, transfer_pick(dev, range(1, 7), 256, 252), slab)
+    rows = [picked(slab, n) for n in range(16)]
     for n in range(6):
-        own_out[n] = picked(slab, n)
-        sib_out[n] = picked(slab, 8 + n)
+        own_out[n] = rows[n]
+        sib_out[n] = rows[8 + n]
+    own_out[6] = rows[14]
+    own_out[7] = rows[15]
+    up = [rows[1].astype(BF16), rows[9].astype(BF16)]
+    for n, (row, side) in enumerate([(0, 0), (8, 0), (6, 1), (7, 1)]):
+        quad_out[n] = mxu(rows[row].astype(BF16), up[side], NN)
+    quad_out[4] = rows[6]
+    quad_out[5] = rows[7]
 
 
 def second_pick(after, device, transfer):
     return pl.pallas_call(
         second_kernel,
-        out_shape=[jax.ShapeDtypeStruct((6, 64, 64), F32)] * 2,
+        out_shape=[
+            jax.ShapeDtypeStruct((8, 64, 64), F32),
+            jax.ShapeDtypeStruct((6, 64, 64), F32),
+            jax.ShapeDtypeStruct((6, 64, 64), F32),
+        ],
         in_specs=[IN_VMEM, IN_SMEM, IN_VMEM],
-        out_specs=[IN_VMEM] * 2,
+        out_specs=[IN_VMEM] * 3,
         scratch_shapes=[VMEM((32 * 24, 128), F32)],
         compiler_params=params(WINDOW_MIB),
         cost_estimate=cost(1),
         name="second_pick",
     )(after, device, transfer)
+
+
+def combine_kernel(quad, own, a, b, c, up_out, sib_out):
+    blocks = [own[...], a[...], b[...], c[...]]
+    terms = [field_term(x, quad[n]) for n, x in enumerate(blocks)]
+    up_out[...] = (terms[0] + terms[1]) + (terms[2] + terms[3])
+    sib_out[...] = field_term(b[...], quad[4]) + field_term(c[...], quad[5])
+
+
+def combine(quad, own, a, b, c):
+    return pl.pallas_call(
+        combine_kernel,
+        out_shape=[jax.ShapeDtypeStruct((64, 64), F32)] * 2,
+        in_specs=[IN_VMEM] * 5,
+        out_specs=[IN_VMEM] * 2,
+        compiler_params=params(WINDOW_MIB),
+        cost_estimate=cost(0.3),
+        name="combine",
+    )(quad, own, a, b, c)
 
 
 def lift_kernel(after, device, own0, own, table, lift_out, slab):
@@ -349,13 +380,20 @@
         lo = (chain - hi.astype(F32)).astype(BF16)
         if level < 7:
             chain = mxu(steps[level], hi, NN) + mxu(steps[level], lo, NN)
-        lift_out[level] = mxu(turned[level], hi, NN) + mxu(turned[level], lo, NN)
+        last = mxu(turned[level], hi, NN) + mxu(turned[level], lo, NN)
+        if level < 7:
+            lift_out[level] = last
+    hi = last.astype(BF16)
+    lo = (last - hi.astype(F32)).astype(BF16)
+    for n in range(2):
+        e = own[6 + n].astype(BF16)
+        lift_out[7 + n] = mxu(e, hi, NN) + mxu(e, lo, NN)
 
 
 def lifts(after, device, own0, own, coupling):
     return pl.pallas_call(
         lift_kernel,
-        out_shape=jax.ShapeDtypeStruct((8, 64, 64), F32),
+        out_shape=jax.ShapeDtypeStruct((9, 64, 64), F32),
         in_specs=[IN_VMEM, IN_SMEM, IN_VMEM, IN_VMEM, IN_VMEM],
         out_specs=IN_VMEM,
         scratch_shapes=[VMEM((32 * 24, 128), F32)],
@@ -409,7 +447,7 @@
 
     where = [(level, pair) for level in range(6, 2, -1) for pair in range((64 >> level))]
     found = pair_fields(
-        [levels.at[:, pl.ds(LEVEL_AT[level] + 128 * pair, 128)] for level, pair in where],
+        [levels.at[:, pl.ds(LEVEL_AT[level] - 4096 + 128 * pair, 128)] for level, pair in where],
         [coupling.at[32 - (32 >> (level - 2)) + pair] for level, pair in where],
         shift,
     )
@@ -450,7 +488,7 @@
     shift = shift_right()
     mine = range(4 * piece, 4 * piece + 4)
     fields = pair_fields(
-        [levels.at[:, pl.ds(LEVEL_AT[2] + 128 * p, 128)] for p in mine],
+        [levels.at[:, pl.ds(128 * p, 128)] for p in mine],
         [coupling.at[p] for p in mine],
         shift,
     )
@@ -506,15 +544,15 @@
 
 
 def partial_kernel(after, lift, *refs):
-    terms = [field_term(refs[height][...], lift[height]) for height in range(7)]
-    refs[7][...] = sum(terms[1:], terms[0])
+    terms = [field_term(refs[height][...], lift[height]) for height in range(6)]
+    refs[6][...] = sum(terms[1:], terms[0])
 
 
 def partial_field(after, lift, partners):
     return pl.pallas_call(
         partial_kernel,
         out_shape=jax.ShapeDtypeStruct((64, 64), F32),
-        in_specs=[IN_VMEM] * 9,
+        in_specs=[IN_VMEM] * 8,
         out_specs=IN_VMEM,
         compiler_params=params(WINDOW_MIB),
         cost_estimate=cost(0.5),
@@ -522,11 +560,12 @@
     )(after, lift, *partners)
 
 
-def final_kernel(lift, partial, partner, *refs):
-    bases = refs[:4]
-    tops = refs[4:8]
-    out_h, out, sems = refs[8:]
-    g = partial[...] + field_term(partner[...], lift[7])
+def final_kernel(lift, partial, *refs):
+    bases = refs[3:7]
+    tops = refs[7:11]
+    out_h, out, sems = refs[11:]
+    terms = [field_term(refs[n][...], lift[6 + n]) for n in range(3)]
+    g = (partial[...] + terms[0]) + (terms[1] + terms[2])
     hi = g.astype(BF16)
     lo = (g - hi.astype(F32)).astype(BF16)
     g = jnp.concatenate(
@@ -546,17 +585,17 @@
         copy.wait()
 
 
-def final(lift, partial, partner, bases, tops):
+def final(lift, partial, partners, bases, tops):
     return pl.pallas_call(
         final_kernel,
         out_shape=jax.ShapeDtypeStruct((64, 8192), F32),
-        in_specs=[IN_VMEM] * 11,
+        in_specs=[IN_VMEM] * 13,
         out_specs=IN_HBM,
         scratch_shapes=[VMEM((64, 8192), F32), pltpu.SemaphoreType.DMA((4,))],
         compiler_params=params(16),
         cost_estimate=cost(2),
         name="final",
-    )(lift, partial, partner, *bases, *tops)
+    )(lift, partial, *partners, *bases, *tops)
 
 
 def exchanged(value, mask):
@@ -571,41 +610,48 @@
 def on_device(coords, vectors, bases, transfer, coupling, top_transfer, top_coupling):
     vectors = vectors.T
     device = lax.axis_index(AXES).astype(jnp.int32).reshape(1)
-    climbing, table0, table1, table2, levels, pairs, quads = upward(
+    climbing, table0, table1, levels, pairs, quads = upward(
         device,
         bases.transpose(1, 2, 0),
         vectors,
         transfer[0].transpose(1, 2, 0),
         top_transfer.transpose(1, 2, 0),
-        top_coupling.transpose(1, 2, 0),
-    )
+    )
+    table2 = top_coupling.transpose(1, 2, 0)
     coupling = coupling[0]
-    partners, nears, lows = [], [None] * 4, []
-    for height, mask in enumerate(MASKS):
-        partner = exchanged(climbing, mask)
-        if height == 0:
-            own0, sib0 = first_pick(climbing, device, table0)
-            own, sib = [own0], [sib0]
-        elif height == 1:
-            owns, sibs = second_pick(climbing, device, table1)
-            own += [owns[n] for n in range(6)]
-            sib += [sibs[n] for n in range(6)]
-        elif height == 3:
-            lift = lifts(climbing, device, own0, owns, table2)
+    lows = []
+
+    def lower_with(after, piece, near_in):
+        lows.append(lower_piece(piece, after, state, near_in, coupling, levels, quads, pairs))
+
+    fields = [exchanged(climbing, 1)]
+    own0, sib0 = first_pick(climbing, device, table0)
+    climbing = dot(climbing, own0) + dot(fields[0], sib0)
+    start = climbing
+    owns, sibs, quad = second_pick(start, device, table1)
+    ring = [exchanged(start, mask) for mask in (2, 4, 6)]
+    near0 = near(0, start, coords, vectors)
+    near1 = near(1, start, coords, vectors)
+    climbing, sibling = combine(quad, start, *ring)
+    fields += [ring[0], sibling]
+    for height, mask in ((3, 8), (4, 16), (5, 48)):
+        start = climbing
+        fields.append(exchanged(start, mask))
+        if height == 3:
+            lift = lifts(start, device, own0, owns, table2)
+            near2 = near(2, start, coords, vectors)
         elif height == 4:
-            state = upper(climbing, coupling, levels, quads)
-        for piece in NEAR_BESIDE.get(height, ()):
-            nears[piece] = near(piece, climbing, coords, vectors)
-        for piece in BESIDE.get(height, ()):
-            lows.append(
-                lower_piece(piece, climbing, state, nears[piece], coupling, levels, quads, pairs)
-            )
-        if height == 7:
-            partial = partial_field(climbing, lift, partners)
-        partners.append(partner)
-        if height < 7:
-            climbing = dot(climbing, own[height]) + dot(partner, sib[height])
-    result = final(lift, partial, partner, [low[0] for low in lows], [low[1] for low in lows])
+            state = upper(start, coupling, levels, quads)
+            lower_with(start, 0, near0)
+        else:
+            near3 = near(3, start, coords, vectors)
+            lower_with(start, 1, near1)
+        climbing = dot(start, owns[height - 1]) + dot(fields[-1], sibs[height - 1])
+    ring = [exchanged(climbing, mask) for mask in (64, 128, 192)]
+    lower_with(climbing, 2, near2)
+    lower_with(climbing, 3, near3)
+    partial = partial_field(climbing, lift, fields)
+    result = final(lift, partial, ring, [low[0] for low in lows], [low[1] for low in lows])
     return result.T
 
 

time: 51.2 us -> 48 us (0.938)
  waiting for transfers between devices: 6.42 us -> 0.76 us
  local copies, waits for them, and re-layouts: 0.04 us -> 2.36 us
  starting transfers between devices: 17.2 us -> 18.3 us
  matrix products: 2.28 us -> 1.31 us
    ppermute x8 -> x10, waiting for transfers between devices: 6.42 us -> 0.76 us  [exchanged(): return lax.ppermute(value, AXES, [(s, s ^ mask) for s in range(devices)])]
    unnamed x16, local copies, waits for them, and re-layouts: 0.04 us -> 2.36 us
    ppermute x8 -> x10, starting transfers between devices: 17.2 us -> 18.3 us  [exchanged(): return lax.ppermute(value, AXES, [(s, s ^ mask) for s in range(devices)])]
    dot_general x14 -> x8, matrix products: 2.28 us -> 1.31 us  [dot(): return jnp.dot(a, b, precision=HIGH)]
    pallas_call x1, Pallas kernels: 9.11 us -> 8.31 us  [upward(): pl.pallas_call(up_kernel, out_shape=[jax.ShapeDtypeStruct((64, 64), F32),...]
    pallas_call x2 -> x3, Pallas kernels: 2.27 us -> 2.69 us  [the longest x1 1.66 us: lifts(): pl.pallas_call(lift_kernel, out_shape=jax.ShapeDtypeStruct((9, 64, 64), F...]
  transfers between devices with their start and end apart: 8 -> 10, of which waited for: 6 -> 1; matrix products, arithmetic and copies ran while one was open for 1% -> 0% of each run, Pallas kernels for 26% -> 29%
where the time goes in v3:
time: 48 us; the launch traced here: 47.2 us
  Pallas kernels  24.1 us (50%)
  starting transfers between devices  18.3 us (38%)
  local copies, waits for them, and re-layouts  2.36 us (5%)
  matrix products  1.31 us (3%)
  waiting for transfers between devices  0.76 us (2%)
    ppermute x10, starting transfers between devices, exchanged(): return lax.ppermute(value, AXES, [(s, s ^ mask) for s in range(devices)])  18.3 us
    pallas_call x1, Pallas kernels, upward(): pl.pallas_call(up_kernel, out_shape=[jax.ShapeDtypeStruct((64, 64), F32),...  8.31 us
    pallas_call x4, Pallas kernels, lower_piece(): pl.pallas_call(functools.partial(lower_kernel, piece), out_shape=[jax.Sha...  5.49 us
    pallas_call x4, Pallas kernels, near(): pl.pallas_call(functools.partial(near_kernel, piece), out_shape=jax.Shape...  3.78 us
    unnamed x16, local copies, waits for them, and re-layouts  2.36 us
    pallas_call x1, Pallas kernels, final(): pl.pallas_call(final_kernel, out_shape=jax.ShapeDtypeStruct((64, 8192), F...  1.92 us
    pallas_call x1, Pallas kernels, lifts(): pl.pallas_call(lift_kernel, out_shape=jax.ShapeDtypeStruct((9, 64, 64), F...  1.66 us
    dot_general x8, matrix products, dot(): return jnp.dot(a, b, precision=HIGH)  1.31 us
  transfers between devices with their start and end apart: 10, of which 1 were waited for; matrix products, arithmetic and copies ran while one was open for 0% of the time, Pallas kernels for 29%

profile of v3, /device:TPU:24, one launch (start us, length us, event | category | flops | bytes accessed | tf_op | source)
XLA Modules:
  0.0 47.2 jit_solution(6217943175811418051)
XLA Ops:
  0.0 8.3 %upward.1 = (f32[64,64]{1,0:T(8,128)S(1)}, bf16[64,64,128]{2,1,0:T(8,128)(2,1)}, bf16[64,64,252]{2,1,0:T(8,128)(2,1)}, f32[64,3968]{1,0:T(8,128)S(1)}, bf16[64,1...) custom-call(s32[1]{0:T(128)} %bitcast.device, bf16[64,64,128]{2,1,0:T(8,128)(2,1)} %bitcast.51, ...), custom_call_target="tpu_custom_call" | custom-call | flops 8000000000 | bytes 65536 | tf_op jit(solution)/shard_map/upward/pallas_call | solution.py:173
  8.5 1.3 %copy-done.7 = bf16[64,64,128]{2,1,0:T(8,128)(2,1)S(1)} copy-done((bf16[64,64,128]{2,1,0:T(8,128)(2,1)S(1)}, bf16[64,64,128]{2,1,0:T(8,128)(2,1)}, u32[]{:S(2)}) %copy-start.7) | copy-done | bytes 1048600
  10.6 2.8 %collective-permute-start.3 = (f32[64,64]{1,0:T(8,128)S(1)}, f32[64,64]{1,0:T(8,128)S(1)}, u32[]{:S(2)}, u32[]{:S(2)}) collective-permute-start(f32[64,64]{1,0:T(8,128)S(1)} %convolution_add_fusion.3.after.own), channel_id=1, source_target_pairs={{0,6},{1,7},{2,4},{3,5},{4,2},{5,3},{6,0},{7,1},{8,14},{9,15},{10,... | collective-permute-start | bytes 49160 | tf_op jit(solution)/shard_map/ppermute | solution.py:603
  13.4 0.8 %collective-permute-start.2 = (f32[64,64]{1,0:T(8,128)S(1)}, f32[64,64]{1,0:T(8,128)S(1)}, u32[]{:S(2)}, u32[]{:S(2)}) collective-permute-start(f32[64,64]{1,0:T(8,128)S(1)} %convolution_add_fusion.3.after.own), channel_id=1, source_target_pairs={{0,4},{1,5},{2,6},{3,7},{4,0},{5,1},{6,2},{7,3},{8,12},{9,13},{10,... | collective-permute-start | bytes 49160 | tf_op jit(solution)/shard_map/ppermute | solution.py:603
  14.2 0.5 %collective-permute-start.1 = (f32[64,64]{1,0:T(8,128)S(1)}, f32[64,64]{1,0:T(8,128)S(1)}, u32[]{:S(2)}, u32[]{:S(2)}) collective-permute-start(f32[64,64]{1,0:T(8,128)S(1)} %convolution_add_fusion.3.after.own), channel_id=1, source_target_pairs={{0,2},{1,3},{2,0},{3,1},{4,6},{5,7},{6,4},{7,5},{8,10},{9,11},{10,... | collective-permute-start | bytes 49160 | tf_op jit(solution)/shard_map/ppermute | solution.py:603
  14.7 0.9 %near.5.near_in = f32[64,2048]{1,0:T(8,128)S(1)} custom-call(f32[64,64]{1,0:T(8,128)S(1)} %convolution_add_fusion.3.after.own, f32[3,8192]{1,0:T(4,128)S(1)} %copy-done.5, bf16[64,8192]{1,0:T(8,128)(2,1)S(1)} %bitcast.45), custom_call_target="tpu_custom_call" | custom-call | flops 1500000000 | bytes 65536 | tf_op jit(solution)/shard_map/near/pallas_call | solution.py:411
  15.7 0.9 %near.4.near_in = f32[64,2048]{1,0:T(8,128)S(1)} custom-call(f32[64,64]{1,0:T(8,128)S(1)} %convolution_add_fusion.3.after.own, f32[3,8192]{1,0:T(4,128)S(1)} %copy-done.5, bf16[64,8192]{1,0:T(8,128)(2,1)S(1)} %bitcast.46), custom_call_target="tpu_custom_call" | custom-call | flops 1500000000 | bytes 65536 | tf_op jit(solution)/shard_map/near/pallas_call | solution.py:411
  16.7 0.6 %copy-done.6 = bf16[64,64,252]{2,1,0:T(8,128)(2,1)S(1)} copy-done((bf16[64,64,252]{2,1,0:T(8,128)(2,1)S(1)}, bf16[64,64,252]{2,1,0:T(8,128)(2,1)}, u32[]{:S(2)}) %copy-start.6) | copy-done | bytes 2064408
  17.3 0.9 %second_pick.1 = (f32[8,64,64]{2,1,0:T(8,128)S(1)}, f32[6,64,64]{2,1,0:T(8,128)S(1)}, f32[6,64,64]{2,1,0:T(8,128)S(1)}) custom-call(f32[64,64]{1,0:T(8,128)S(1)} %convolution_add_fusion.3.after.own, s32[1]{0:T(128)} %bitcast.device, bf16[64,64,252]{2,1,0:T(8,128)(2,1)S(1)} %copy-done.6), custom_call_target="tpu_custom_call" | custom-call | flops 1000000000 | bytes 65536 | tf_op jit(solution)/shard_map/second_pick/pallas_call | solution.py:329
  18.2 0.7 %collective-permute-done.2.b = f32[64,64]{1,0:T(8,128)S(1)} collective-permute-done((f32[64,64]{1,0:T(8,128)S(1)}, f32[64,64]{1,0:T(8,128)S(1)}, u32[]{:S(2)}, u32[]{:S(2)}) %collective-permute-start.2) | collective-permute-done | bytes 16416 | tf_op jit(solution)/shard_map/ppermute | solution.py:603
  19.1 2.0 %collective-permute-start.4 = (f32[64,64]{1,0:T(8,128)S(1)}, f32[64,64]{1,0:T(8,128)S(1)}, u32[]{:S(2)}, u32[]{:S(2)}) collective-permute-start(f32[64,64]{1,0:T(8,128)S(1)} %get-tuple-element.32.after), channel_id=1, source_target_pairs={{0,8},{1,9},{2,10},{3,11},{4,12},{5,13},{6,14},{7,15},{8,0},{9,1},... | collective-permute-start | bytes 49160 | tf_op jit(solution)/shard_map/ppermute | solution.py:603
  21.1 1.7 %lifts.1.lift = f32[9,64,64]{2,1,0:T(8,128)S(1)} custom-call(f32[64,64]{1,0:T(8,128)S(1)} %get-tuple-element.32.after, s32[1]{0:T(128)} %bitcast.device, f32[64,64]{1,0:T(8,128)S(1)} %get-tuple-element.28.own0, f32[8,64,64]{2,1,0:T(8,128)S(1)} %get-tuple-element.33.own, bf16[64,64,255]{2,1,0:T(8,128)(2,1)S(1)} %bitcast.43), custom_call_target="tpu_custom_call" | custom-call | flops 2000000000 | bytes 65536 | tf_op jit(solution)/shard_map/lifts/pallas_call | solution.py:394
  22.8 1.0 %near.6.near_in = f32[64,2048]{1,0:T(8,128)S(1)} custom-call(f32[64,64]{1,0:T(8,128)S(1)} %get-tuple-element.32.after, f32[3,8192]{1,0:T(4,128)S(1)} %copy-done.5, bf16[64,8192]{1,0:T(8,128)(2,1)S(1)} %bitcast.47), custom_call_target="tpu_custom_call" | custom-call | flops 1500000000 | bytes 65536 | tf_op jit(solution)/shard_map/near/pallas_call | solution.py:411
  24.3 3.5 %collective-permute-start.5 = (f32[64,64]{1,0:T(8,128)S(1)}, f32[64,64]{1,0:T(8,128)S(1)}, u32[]{:S(2)}, u32[]{:S(2)}) collective-permute-start(f32[64,64]{1,0:T(8,128)S(1)} %convolution_add_fusion.2.after), channel_id=1, source_target_pairs={{0,16},{1,17},{2,18},{3,19},{4,20},{5,21},{6,22},{7,23},{8,24},{9,... | collective-permute-start | bytes 49160 | tf_op jit(solution)/shard_map/ppermute | solution.py:603
  27.8 1.2 %upper.1.state3 = f32[128,1024]{1,0:T(8,128)S(1)} custom-call(f32[64,64]{1,0:T(8,128)S(1)} %convolution_add_fusion.2.after, bf16[31,64,64]{2,1,0:T(8,128)(2,1)S(1)} %bitcast.38, f32[64,3968]{1,0:T(8,128)S(1)} %get-tuple-element.36.levels, bf16[64,256,128]{2,1,0:T(8,128)(2,1)S(1)} %copy-done), custom_call_target="tpu_custom_call" | custom-call | flops 1500000000 | bytes 65536 | tf_op jit(solution)/shard_map/upper/pallas_call | solution.py:476
  29.4 1.4 %lower.4 = (f32[64,2048]{1,0:T(8,128)S(1)}, bf16[128,2048]{1,0:T(8,128)(2,1)S(1)}) custom-call(f32[64,64]{1,0:T(8,128)S(1)} %convolution_add_fusion.2.after, f32[128,1024]{1,0:T(8,128)S(1)} %upper.1.state3, f32[64,2048]{1,0:T(8,128)S(1)} %near.4.near_in, bf16[31,64,64]{2,1,0:T(8,128)(2,1)S(1)} %bitcast.39, f32[64,3968]{1,0:T(8,128)S(1)} %get-tuple-element.36.levels, ...), custom_call_target="tpu_custom_call" | custom-call | flops 1500000000 | bytes 65536 | tf_op jit(solution)/shard_map/lower/pallas_call | solution.py:525
  31.1 4.3 %collective-permute-start.6 = (f32[64,64]{1,0:T(8,128)S(1)}, f32[64,64]{1,0:T(8,128)S(1)}, u32[]{:S(2)}, u32[]{:S(2)}) collective-permute-start(f32[64,64]{1,0:T(8,128)S(1)} %convolution_add_fusion.1.after), channel_id=1, source_target_pairs={{0,48},{1,49},{2,50},{3,51},{4,52},{5,53},{6,54},{7,55},{8,56},{9,... | collective-permute-start | bytes 49160 | tf_op jit(solution)/shard_map/ppermute | solution.py:603
  35.4 0.9 %near.7.near_in = f32[64,2048]{1,0:T(8,128)S(1)} custom-call(f32[64,64]{1,0:T(8,128)S(1)} %convolution_add_fusion.1.after, f32[3,8192]{1,0:T(4,128)S(1)} %copy-done.5, bf16[64,8192]{1,0:T(8,128)(2,1)S(1)} %bitcast.48), custom_call_target="tpu_custom_call" | custom-call | flops 1500000000 | bytes 65536 | tf_op jit(solution)/shard_map/near/pallas_call | solution.py:411
  36.4 1.4 %lower.5 = (f32[64,2048]{1,0:T(8,128)S(1)}, bf16[128,2048]{1,0:T(8,128)(2,1)S(1)}) custom-call(f32[64,64]{1,0:T(8,128)S(1)} %convolution_add_fusion.1.after, f32[128,1024]{1,0:T(8,128)S(1)} %upper.1.state3, f32[64,2048]{1,0:T(8,128)S(1)} %near.5.near_in, bf16[31,64,64]{2,1,0:T(8,128)(2,1)S(1)} %bitcast.40, f32[64,3968]{1,0:T(8,128)S(1)} %get-tuple-element.36.levels, ...), custom_call_target="tpu_custom_call" | custom-call | flops 1500000000 | bytes 65536 | tf_op jit(solution)/shard_map/lower/pallas_call | solution.py:525
  38.2 2.6 %collective-permute-start.8 = (f32[64,64]{1,0:T(8,128)S(1)}, f32[64,64]{1,0:T(8,128)S(1)}, u32[]{:S(2)}, u32[]{:S(2)}) collective-permute-start(f32[64,64]{1,0:T(8,128)S(1)} %convolution_add_fusion.after), channel_id=1, source_target_pairs={{0,128},{1,129},{2,130},{3,131},{4,132},{5,133},{6,134},{7,135},{8... | collective-permute-start | bytes 49160 | tf_op jit(solution)/shard_map/ppermute | solution.py:603
  40.8 1.3 %collective-permute-start.7 = (f32[64,64]{1,0:T(8,128)S(1)}, f32[64,64]{1,0:T(8,128)S(1)}, u32[]{:S(2)}, u32[]{:S(2)}) collective-permute-start(f32[64,64]{1,0:T(8,128)S(1)} %convolution_add_fusion.after), channel_id=1, source_target_pairs={{0,64},{1,65},{2,66},{3,67},{4,68},{5,69},{6,70},{7,71},{8,72},{9,... | collective-permute-start | bytes 49160 | tf_op jit(solution)/shard_map/ppermute | solution.py:603
  42.1 1.4 %lower.7 = (f32[64,2048]{1,0:T(8,128)S(1)}, bf16[128,2048]{1,0:T(8,128)(2,1)S(1)}) custom-call(f32[64,64]{1,0:T(8,128)S(1)} %convolution_add_fusion.after, f32[128,1024]{1,0:T(8,128)S(1)} %upper.1.state3, f32[64,2048]{1,0:T(8,128)S(1)} %near.7.near_in, bf16[31,64,64]{2,1,0:T(8,128)(2,1)S(1)} %bitcast.41, f32[64,3968]{1,0:T(8,128)S(1)} %get-tuple-element.36.levels, ...), custom_call_target="tpu_custom_call" | custom-call | flops 1500000000 | bytes 65536 | tf_op jit(solution)/shard_map/lower/pallas_call | solution.py:525
  43.5 1.4 %lower.6 = (f32[64,2048]{1,0:T(8,128)S(1)}, bf16[128,2048]{1,0:T(8,128)(2,1)S(1)}) custom-call(f32[64,64]{1,0:T(8,128)S(1)} %convolution_add_fusion.after, f32[128,1024]{1,0:T(8,128)S(1)} %upper.1.state3, f32[64,2048]{1,0:T(8,128)S(1)} %near.6.near_in, bf16[31,64,64]{2,1,0:T(8,128)(2,1)S(1)} %bitcast.42, f32[64,3968]{1,0:T(8,128)S(1)} %get-tuple-element.36.levels, ...), custom_call_target="tpu_custom_call" | custom-call | flops 1500000000 | bytes 65536 | tf_op jit(solution)/shard_map/lower/pallas_call | solution.py:525
  45.1 1.9 %final.1 = f32[64,8192]{1,0:T(8,128)} custom-call(f32[9,64,64]{2,1,0:T(8,128)S(1)} %lifts.1.lift, f32[64,64]{1,0:T(8,128)S(1)} %partial_field.1.partial, f32[64,64]{1,0:T(8,128)S(1)} %collective-permute-done.7.refs_0_, f32[64,64]{1,0:T(8,128)S(1)} %collective-permute-done.8.refs_1_, f32[64,64]{1,0:T(8,128)S(1)} %collective-permute-done.9.refs_2_, ...), custom_call_target="tpu_custom_call" | custom-call | flops 2000000000 | bytes 65536 | tf_op jit(solution)/shard_map/final/pallas_call | solution.py:589
  (36 shorter events, 3.0 us)
Async XLA Ops:
  8.3 6.4 %copy-start.4 = (bf16[8192,64]{0,1:T(8,128)(2,1)S(1)}, bf16[8192,64]{0,1:T(8,128)(2,1)}, u32[]{:S(2)}) copy-start(bf16[8192,64]{0,1:T(8,128)(2,1)} %param.8) | copy-start | bytes 3145732
  8.3 6.4 %copy-start.5 = (f32[3,8192]{1,0:T(4,128)S(1)}, f32[3,8192]{1,0:T(4,128)}, u32[]{:S(2)}) copy-start(f32[3,8192]{1,0:T(4,128)} %coords.7) | copy-start | bytes 294916
  8.3 2.0 %collective-permute-start = (f32[64,64]{1,0:T(8,128)S(1)}, f32[64,64]{1,0:T(8,128)S(1)}, u32[]{:S(2)}, u32[]{:S(2)}) collective-permute-start(f32[64,64]{1,0:T(8,128)S(1)} %get-tuple-element.26.after), channel_id=1, source_target_pairs={{0,1},{1,0},{2,3},{3,2},{4,5},{5,4},{6,7},{7,6},{8,9},{9,8},{10,11... | collective-permute-start | bytes 49160 | tf_op jit(solution)/shard_map/ppermute | solution.py:603
  8.4 1.3 %copy-start.7 = (bf16[64,64,128]{2,1,0:T(8,128)(2,1)S(1)}, bf16[64,64,128]{2,1,0:T(8,128)(2,1)}, u32[]{:S(2)}) copy-start(bf16[64,64,128]{2,1,0:T(8,128)(2,1)} %get-tuple-element.27.transfer) | copy-start | bytes 3145732
  10.6 7.6 %collective-permute-start.3 = (f32[64,64]{1,0:T(8,128)S(1)}, f32[64,64]{1,0:T(8,128)S(1)}, u32[]{:S(2)}, u32[]{:S(2)}) collective-permute-start(f32[64,64]{1,0:T(8,128)S(1)} %convolution_add_fusion.3.after.own), channel_id=1, source_target_pairs={{0,6},{1,7},{2,4},{3,5},{4,2},{5,3},{6,0},{7,1},{8,14},{9,15},{10,... | collective-permute-start | bytes 49160 | tf_op jit(solution)/shard_map/ppermute | solution.py:603
  13.4 5.5 %collective-permute-start.2 = (f32[64,64]{1,0:T(8,128)S(1)}, f32[64,64]{1,0:T(8,128)S(1)}, u32[]{:S(2)}, u32[]{:S(2)}) collective-permute-start(f32[64,64]{1,0:T(8,128)S(1)} %convolution_add_fusion.3.after.own), channel_id=1, source_target_pairs={{0,4},{1,5},{2,6},{3,7},{4,0},{5,1},{6,2},{7,3},{8,12},{9,13},{10,... | collective-permute-start | bytes 49160 | tf_op jit(solution)/shard_map/ppermute | solution.py:603
  14.2 4.7 %collective-permute-start.1 = (f32[64,64]{1,0:T(8,128)S(1)}, f32[64,64]{1,0:T(8,128)S(1)}, u32[]{:S(2)}, u32[]{:S(2)}) collective-permute-start(f32[64,64]{1,0:T(8,128)S(1)} %convolution_add_fusion.3.after.own), channel_id=1, source_target_pairs={{0,2},{1,3},{2,0},{3,1},{4,6},{5,7},{6,4},{7,5},{8,10},{9,11},{10,... | collective-permute-start | bytes 49160 | tf_op jit(solution)/shard_map/ppermute | solution.py:603
  15.7 1.6 %copy-start.6 = (bf16[64,64,252]{2,1,0:T(8,128)(2,1)S(1)}, bf16[64,64,252]{2,1,0:T(8,128)(2,1)}, u32[]{:S(2)}) copy-start(bf16[64,64,252]{2,1,0:T(8,128)(2,1)} %get-tuple-element.30.transfer) | copy-start | bytes 6193156
  17.3 3.8 %copy-start.3 = (bf16[255,64,64]{0,2,1:T(8,128)(2,1)S(1)}, bf16[255,64,64]{0,2,1:T(8,128)(2,1)}, u32[]{:S(2)}) copy-start(bf16[255,64,64]{0,2,1:T(8,128)(2,1)} %param.13) | copy-start | bytes 6266884
  19.1 4.7 %collective-permute-start.4 = (f32[64,64]{1,0:T(8,128)S(1)}, f32[64,64]{1,0:T(8,128)S(1)}, u32[]{:S(2)}, u32[]{:S(2)}) collective-permute-start(f32[64,64]{1,0:T(8,128)S(1)} %get-tuple-element.32.after), channel_id=1, source_target_pairs={{0,8},{1,9},{2,10},{3,11},{4,12},{5,13},{6,14},{7,15},{8,0},{9,1},... | collective-permute-start | bytes 49160 | tf_op jit(solution)/shard_map/ppermute | solution.py:603
  22.8 5.0 %copy-start = (bf16[64,256,128]{2,1,0:T(8,128)(2,1)S(1)}, bf16[64,256,128]{2,1,0:T(8,128)(2,1)}, u32[]{:S(2)}) copy-start(bf16[64,256,128]{2,1,0:T(8,128)(2,1)} %get-tuple-element.37.quads) | copy-start | bytes 12582916
  22.8 5.0 %copy-start.2 = (bf16[1,31,64,64]{3,2,1,0:T(8,128)(2,1)S(1)}, bf16[1,31,64,64]{3,2,1,0:T(8,128)(2,1)}, u32[]{:S(2)}) copy-start(bf16[1,31,64,64]{3,2,1,0:T(8,128)(2,1)} %param.11) | copy-start | bytes 761860
  24.3 6.5 %collective-permute-start.5 = (f32[64,64]{1,0:T(8,128)S(1)}, f32[64,64]{1,0:T(8,128)S(1)}, u32[]{:S(2)}, u32[]{:S(2)}) collective-permute-start(f32[64,64]{1,0:T(8,128)S(1)} %convolution_add_fusion.2.after), channel_id=1, source_target_pairs={{0,16},{1,17},{2,18},{3,19},{4,20},{5,21},{6,22},{7,23},{8,24},{9,... | collective-permute-start | bytes 49160 | tf_op jit(solution)/shard_map/ppermute | solution.py:603
  27.8 1.6 %copy-start.1 = (bf16[64,128,128]{2,1,0:T(8,128)(2,1)S(1)}, bf16[64,128,128]{2,1,0:T(8,128)(2,1)}, u32[]{:S(2)}) copy-start(bf16[64,128,128]{2,1,0:T(8,128)(2,1)} %get-tuple-element.38.pairs) | copy-start | bytes 6291460
  31.1 6.6 %collective-permute-start.6 = (f32[64,64]{1,0:T(8,128)S(1)}, f32[64,64]{1,0:T(8,128)S(1)}, u32[]{:S(2)}, u32[]{:S(2)}) collective-permute-start(f32[64,64]{1,0:T(8,128)S(1)} %convolution_add_fusion.1.after), channel_id=1, source_target_pairs={{0,48},{1,49},{2,50},{3,51},{4,52},{5,53},{6,54},{7,55},{8,56},{9,... | collective-permute-start | bytes 49160 | tf_op jit(solution)/shard_map/ppermute | solution.py:603
  37.9 7.2 %collective-permute-start.9 = (f32[64,64]{1,0:T(8,128)S(1)}, f32[64,64]{1,0:T(8,128)S(1)}, u32[]{:S(2)}, u32[]{:S(2)}) collective-permute-start(f32[64,64]{1,0:T(8,128)S(1)} %convolution_add_fusion.after), channel_id=1, source_target_pairs={{0,192},{1,193},{2,194},{3,195},{4,196},{5,197},{6,198},{7,199},{8... | collective-permute-start | bytes 49160 | tf_op jit(solution)/shard_map/ppermute | solution.py:603
  38.2 6.9 %collective-permute-start.8 = (f32[64,64]{1,0:T(8,128)S(1)}, f32[64,64]{1,0:T(8,128)S(1)}, u32[]{:S(2)}, u32[]{:S(2)}) collective-permute-start(f32[64,64]{1,0:T(8,128)S(1)} %convolution_add_fusion.after), channel_id=1, source_target_pairs={{0,128},{1,129},{2,130},{3,131},{4,132},{5,133},{6,134},{7,135},{8... | collective-permute-start | bytes 49160 | tf_op jit(solution)/shard_map/ppermute | solution.py:603
  40.8 4.3 %collective-permute-start.7 = (f32[64,64]{1,0:T(8,128)S(1)}, f32[64,64]{1,0:T(8,128)S(1)}, u32[]{:S(2)}, u32[]{:S(2)}) collective-permute-start(f32[64,64]{1,0:T(8,128)S(1)} %convolution_add_fusion.after), channel_id=1, source_target_pairs={{0,64},{1,65},{2,66},{3,67},{4,68},{5,69},{6,70},{7,71},{8,72},{9,... | collective-permute-start | bytes 49160 | tf_op jit(solution)/shard_map/ppermute | solution.py:603

commit v4 on v3

--- a/solution.py
+++ b/solution.py
@@ -11,7 +11,6 @@
 BF16 = jnp.bfloat16
 VMEM = pltpu.VMEM
 AXES = ("leaf", "sub")
-HIGH = lax.Precision.HIGHEST
 
 STEP = 136
 NN = (((1,), (0,)), ((), ()))
@@ -59,8 +58,8 @@
 
 def up_kernel(
     device, bases_h, vectors_h, transfer_h, top_transfer_h,
-    own_out, table0, table1, levels_h, pairs_h, quads_h,
-    bases, vectors, transfer, slab0, slab1, slab2, leaf_coef, levels, pairs, quads, sems, out_sems,
+    own_out, own0_out, sib0_out, levels, quads_top, pairs_h, quads_h,
+    bases, vectors, transfer, slab0, slab1, slab2, leaf_coef, level1, pairs, quads, table0, picks, sems, out_sems,
 ):
     loads = []
     for k in range(4):
@@ -69,13 +68,9 @@
     loads.append(pltpu.make_async_copy(vectors_h, vectors, sems.at[4]))
     loads.append(pltpu.make_async_copy(transfer_h, transfer, sems.at[5]))
     lane0 = pl.multiple_of(128 * (device[0] >> 7), 128)
-    tables = [
-        (top_transfer_h.at[:, :, pl.ds(lane0, 128)], table0),
-        (top_transfer_h.at[:, :, pl.ds(256, 252)], table1),
-    ]
-    loads += [
-        pltpu.make_async_copy(src, dst, sems.at[6 + n]) for n, (src, dst) in enumerate(tables)
-    ]
+    loads.append(
+        pltpu.make_async_copy(top_transfer_h.at[:, :, pl.ds(lane0, 128)], table0, sems.at[6])
+    )
     for copy in loads:
         copy.start()
     stores = []
@@ -112,6 +107,11 @@
     for k in range(len(steps) + UP_DEPTH):
         if k < 16:
             spread(transfer, 126, 128, slab2, [2 * k, 2 * k + 1])
+        if k == 47:
+            loads[6].wait()
+            first_pick = transfer_pick(device[0], [0], lane0, 128)
+        if 47 <= k < 63:
+            pick_row(table0, first_pick, picks, k - 47)
         if k < len(steps):
             level, q = steps[k]
             first = NODE_AT[level] + 4 * q
@@ -119,36 +119,39 @@
             quad = jnp.concatenate(
                 [box_matrix(slab, (first + u) % 128, u >= 2, low) for u in range(4)], 0
             ).astype(BF16)
-            quads[first // 4] = quad
+            if level < 3:
+                quads[first // 4] = quad
+                if q == (32 >> level) - 1:
+                    part = pl.ds(NODE_AT[level] // 4, 32 >> level)
+                    store(quads.at[part], quads_h.at[part])
+            else:
+                quads_top[first // 4 - 56] = quad
             held.append(quad)
         if k >= UP_DEPTH:
             level, q = steps[k - UP_DEPTH]
-            count = 128 >> level
             if level == 0:
                 coef = leaf_coef[:, 256 * q : 256 * q + 256]
+            elif level == 1:
+                coef = level1[:, 256 * q : 256 * q + 256]
             else:
-                at = LEVEL_AT[level] + 256 * q
+                at = LEVEL_AT[level] - 4096 + 256 * q
                 coef = levels[:, at : at + 256]
-            at = LEVEL_AT[level + 1] + 128 * q
-            levels[:, at : at + 128] = fold(mxu(split(coef), held[k - UP_DEPTH], NN))
-            if level < 2 and q == count // 4 - 1:
-                part = pl.ds(NODE_AT[level] // 4, count // 4)
-                store(quads.at[part], quads_h.at[part])
-                if level == 1:
-                    part = pl.ds(LEVEL_AT[2], 2048)
-                    store(levels.at[:, part], levels_h.at[:, pl.ds(0, 2048)])
+            coef = fold(mxu(split(coef), held[k - UP_DEPTH], NN))
+            if level == 0:
+                level1[:, 128 * q : 128 * q + 128] = coef
+            else:
+                at = LEVEL_AT[level + 1] - 4096 + 128 * q
+                levels[:, at : at + 128] = coef
     last = jnp.concatenate(
         [box_matrix(slab2, 124, False, low), box_matrix(slab2, 125, False, low)], 0
     ).astype(BF16)
-    quads[63, :128, :] = last
-    quads[63, 128:, :] = jnp.zeros((128, 128), BF16)
-    part = pl.ds(48, 16)
-    store(quads.at[part], quads_h.at[part])
-    part = pl.ds(LEVEL_AT[3], 1920)
-    store(levels.at[:, part], levels_h.at[:, pl.ds(2048, 1920)])
-    at = LEVEL_AT[6]
+    quads_top[7, :128, :] = last
+    quads_top[7, 128:, :] = jnp.zeros((128, 128), BF16)
+    at = LEVEL_AT[6] - 4096
     own_out[...] = fold(mxu(split(levels[:, at : at + 128]), last, NN))[:, :64]
-    for copy in loads[6:] + stores:
+    own0_out[...] = picked(picks, 0)
+    sib0_out[...] = picked(picks, 8)
+    for copy in stores:
         copy.wait()
 
 
@@ -174,14 +177,15 @@
         up_kernel,
         out_shape=[
             jax.ShapeDtypeStruct((64, 64), F32),
-            jax.ShapeDtypeStruct((64, 64, 128), BF16),
-            jax.ShapeDtypeStruct((64, 64, 252), BF16),
+            jax.ShapeDtypeStruct((64, 64), F32),
+            jax.ShapeDtypeStruct((64, 64), F32),
             jax.ShapeDtypeStruct((64, 3968), F32),
+            jax.ShapeDtypeStruct((8, 256, 128), BF16),
             jax.ShapeDtypeStruct((64, 128, 128), BF16),
-            jax.ShapeDtypeStruct((64, 256, 128), BF16),
+            jax.ShapeDtypeStruct((56, 256, 128), BF16),
         ],
         in_specs=[IN_SMEM] + [IN_HBM] * 4,
-        out_specs=[IN_VMEM] * 3 + [IN_HBM] * 3,
+        out_specs=[IN_VMEM] * 5 + [IN_HBM] * 2,
         scratch_shapes=[
             VMEM((64, 64, 128), BF16),
             VMEM((64, 8192), BF16),
@@ -190,11 +194,13 @@
             VMEM((32 * STEP, 128), F32),
             VMEM((32 * STEP, 128), F32),
             VMEM((64, 8192), F32),
-            VMEM((64, 8064), F32),
+            VMEM((64, 4096), F32),
             VMEM((64, 128, 128), BF16),
-            VMEM((64, 256, 128), BF16),
-            pltpu.SemaphoreType.DMA((8,)),
+            VMEM((56, 256, 128), BF16),
+            VMEM((64, 64, 128), BF16),
+            VMEM((32 * 24, 128), F32),
             pltpu.SemaphoreType.DMA((7,)),
+            pltpu.SemaphoreType.DMA((4,)),
         ],
         compiler_params=params(UP_MIB),
         cost_estimate=cost(8),
@@ -202,14 +208,18 @@
     )(device, bases, vectors, transfer, top_transfer)
 
 
+def pick_row(table, pick, slab, i):
+    rows = jnp.concatenate(
+        [table[2 * i], table[2 * i + 32], table[2 * i + 1], table[2 * i + 33]], 0
+    )
+    out = mxu(pick, rows, NT)
+    slab[pl.ds(48 * i, 16), :] = out[:, :128]
+    slab[pl.ds(48 * i + 24, 16), :] = out[:, 128:]
+
+
 def pick_rows(table, pick, slab):
     for i in range(16):
-        rows = jnp.concatenate(
-            [table[2 * i], table[2 * i + 32], table[2 * i + 1], table[2 * i + 33]], 0
-        )
-        out = mxu(pick, rows, NT)
-        slab[pl.ds(48 * i, 16), :] = out[:, :128]
-        slab[pl.ds(48 * i + 24, 16), :] = out[:, 128:]
+        pick_row(table, pick, slab, i)
 
 
 def picked(slab, row):
@@ -288,30 +298,11 @@
 ]
 
 
-def first_kernel(after, device, transfer, own_out, sib_out, slab):
-    dev = device[0]
-    lane0 = pl.multiple_of(128 * (dev >> 7), 128)
-    pick_rows(transfer, transfer_pick(dev, [0], lane0, 128), slab)
-    own_out[...] = picked(slab, 0)
-    sib_out[...] = picked(slab, 8)
-
-
-def first_pick(after, device, transfer):
-    return pl.pallas_call(
-        first_kernel,
-        out_shape=[jax.ShapeDtypeStruct((64, 64), F32)] * 2,
-        in_specs=[IN_VMEM, IN_SMEM, IN_VMEM],
-        out_specs=[IN_VMEM] * 2,
-        scratch_shapes=[VMEM((32 * 24, 128), F32)],
-        compiler_params=params(WINDOW_MIB),
-        cost_estimate=cost(1),
-        name="first_pick",
-    )(after, device, transfer)
-
-
 def second_kernel(after, device, transfer, own_out, sib_out, quad_out, slab):
     dev = device[0]
-    pick_rows(transfer, transfer_pick(dev, range(1, 7), 256, 252), slab)
+    pick_rows(
+        transfer.at[:, :, pl.ds(256, 252)], transfer_pick(dev, range(1, 7), 256, 252), slab
+    )
     rows = [picked(slab, n) for n in range(16)]
     for n in range(6):
         own_out[n] = rows[n]
@@ -462,11 +453,11 @@
         1.0,
         0.0,
     ).astype(BF16)
-    state = jnp.concatenate([field(6, 0), mxu(unit, quads[63, :128, :64], NT)], 0)
+    state = jnp.concatenate([field(6, 0), mxu(unit, quads[7, :128, :64], NT)], 0)
     for level in range(5, 2, -1):
         below = []
         for q in range((128 >> level) // 4):
-            s = descend(state[:, 128 * q : 128 * q + 128], quads[NODE_AT[level] // 4 + q])
+            s = descend(state[:, 128 * q : 128 * q + 128], quads[NODE_AT[level] // 4 - 56 + q])
             below.append(with_fields(s, [field(level, 2 * q), field(level, 2 * q + 1)]))
         state = jnp.concatenate(below, 1)
     state_out[...] = state
@@ -578,9 +569,14 @@
             out[:, 2048 * piece + at : 2048 * piece + at + 256] = (
                 fold(mxu(g, tops[piece][:, at : at + 256], NN)) + bases[piece][:, at : at + 256]
             )
-        part = pl.ds(2048 * piece, 2048)
-        copies.append(pltpu.make_async_copy(out.at[:, part], out_h.at[:, part], sems.at[piece]))
-        copies[-1].start()
+            if q % 4 == 3:
+                part = pl.ds(2048 * piece + at - 768, 1024)
+                copies.append(
+                    pltpu.make_async_copy(
+                        out.at[:, part], out_h.at[:, part], sems.at[len(copies)]
+                    )
+                )
+                copies[-1].start()
     for copy in copies:
         copy.wait()
 
@@ -591,32 +587,48 @@
         out_shape=jax.ShapeDtypeStruct((64, 8192), F32),
         in_specs=[IN_VMEM] * 13,
         out_specs=IN_HBM,
-        scratch_shapes=[VMEM((64, 8192), F32), pltpu.SemaphoreType.DMA((4,))],
+        scratch_shapes=[VMEM((64, 8192), F32), pltpu.SemaphoreType.DMA((8,))],
         compiler_params=params(16),
         cost_estimate=cost(2),
         name="final",
     )(lift, partial, *partners, *bases, *tops)
 
 
+def climb_kernel(row, own, sib, mine, other, out):
+    a, b = (own[...], sib[...]) if row is None else (own[row], sib[row])
+    out[...] = fold(
+        mxu(split(mine[...]), a.astype(BF16), NN) + mxu(split(other[...]), b.astype(BF16), NN)
+    )
+
+
+def climb(row, own, sib, mine, other):
+    return pl.pallas_call(
+        functools.partial(climb_kernel, row),
+        out_shape=jax.ShapeDtypeStruct((64, 64), F32),
+        in_specs=[IN_VMEM] * 4,
+        out_specs=IN_VMEM,
+        compiler_params=params(WINDOW_MIB),
+        cost_estimate=cost(0.2),
+        name="climb",
+    )(own, sib, mine, other)
+
+
 def exchanged(value, mask):
     devices = lax.axis_size(AXES)
     return lax.ppermute(value, AXES, [(s, s ^ mask) for s in range(devices)])
 
 
-def dot(a, b):
-    return jnp.dot(a, b, precision=HIGH)
-
-
 def on_device(coords, vectors, bases, transfer, coupling, top_transfer, top_coupling):
     vectors = vectors.T
     device = lax.axis_index(AXES).astype(jnp.int32).reshape(1)
-    climbing, table0, table1, levels, pairs, quads = upward(
+    climbing, own0, sib0, levels, quads_top, pairs, quads = upward(
         device,
         bases.transpose(1, 2, 0),
         vectors,
         transfer[0].transpose(1, 2, 0),
         top_transfer.transpose(1, 2, 0),
     )
+    top_transfer = top_transfer.transpose(1, 2, 0)
     table2 = top_coupling.transpose(1, 2, 0)
     coupling = coupling[0]
     lows = []
@@ -625,12 +637,11 @@
         lows.append(lower_piece(piece, after, state, near_in, coupling, levels, quads, pairs))
 
     fields = [exchanged(climbing, 1)]
-    own0, sib0 = first_pick(climbing, device, table0)
-    climbing = dot(climbing, own0) + dot(fields[0], sib0)
+    near0 = near(0, climbing, coords, vectors)
+    climbing = climb(None, own0, sib0, climbing, fields[0])
     start = climbing
-    owns, sibs, quad = second_pick(start, device, table1)
+    owns, sibs, quad = second_pick(start, device, top_transfer)
     ring = [exchanged(start, mask) for mask in (2, 4, 6)]
-    near0 = near(0, start, coords, vectors)
     near1 = near(1, start, coords, vectors)
     climbing, sibling = combine(quad, start, *ring)
     fields += [ring[0], sibling]
@@ -639,15 +650,15 @@
         fields.append(exchanged(start, mask))
         if height == 3:
             lift = lifts(start, device, own0, owns, table2)
+        elif height == 4:
+            state = upper(start, coupling, levels, quads_top)
             near2 = near(2, start, coords, vectors)
-        elif height == 4:
-            state = upper(start, coupling, levels, quads)
-            lower_with(start, 0, near0)
         else:
             near3 = near(3, start, coords, vectors)
-            lower_with(start, 1, near1)
-        climbing = dot(start, owns[height - 1]) + dot(fields[-1], sibs[height - 1])
+            lower_with(start, 0, near0)
+        climbing = climb(height - 1, owns, sibs, start, fields[-1])
     ring = [exchanged(climbing, mask) for mask in (64, 128, 192)]
+    lower_with(climbing, 1, near1)
     lower_with(climbing, 2, near2)
     lower_with(climbing, 3, near3)
     partial = partial_field(climbing, lift, fields)

time: 48 us -> 45.2 us (0.942); the launches traced: 47.2 us -> 45 us
  local copies, waits for them, and re-layouts: 2.36 us -> 0.05 us
  waiting for transfers between devices: 0.76 us -> 2.79 us
  Pallas kernels: 24.1 us -> 22.1 us
  starting transfers between devices: 18.3 us -> 19.7 us
  matrix products: 1.31 us -> 0 us
    unnamed x16 -> x14, local copies, waits for them, and re-layouts: 2.36 us -> 0.05 us
    pallas_call x1, Pallas kernels: 8.31 us -> 6.27 us  [upward(): pl.pallas_call(up_kernel, out_shape=[jax.ShapeDtypeStruct((64, 64), F32),...]
    ppermute x10, waiting for transfers between devices: 0.76 us -> 2.79 us  [exchanged(): return lax.ppermute(value, AXES, [(s, s ^ mask) for s in range(devices)])]
    ppermute x10, starting transfers between devices: 18.3 us -> 19.7 us  [exchanged(): return lax.ppermute(value, AXES, [(s, s ^ mask) for s in range(devices)])]
    dot_general x8 -> x0, matrix products: 1.31 us -> none  [dot(): return jnp.dot(a, b, precision=HIGH)]
  transfers between devices with their start and end apart: 10 -> 10, of which waited for: 1 -> 3; matrix products, arithmetic and copies ran while one was open for 0% -> 0% of each run, Pallas kernels for 29% -> 29%
where the time goes in v4:
time: 45.2 us; the launch traced here: 45 us
  Pallas kernels  22.1 us (49%)
  starting transfers between devices  19.7 us (44%)
  waiting for transfers between devices  2.79 us (6%)
    ppermute x10, starting transfers between devices, exchanged(): return lax.ppermute(value, AXES, [(s, s ^ mask) for s in range(devices)])  19.7 us
    pallas_call x1, Pallas kernels, upward(): pl.pallas_call(up_kernel, out_shape=[jax.ShapeDtypeStruct((64, 64), F32),...  6.27 us
    pallas_call x4, Pallas kernels, lower_piece(): pl.pallas_call(functools.partial(lower_kernel, piece), out_shape=[jax.Sha...  5.49 us
    pallas_call x4, Pallas kernels, near(): pl.pallas_call(functools.partial(near_kernel, piece), out_shape=jax.Shape...  3.79 us
    ppermute x10, waiting for transfers between devices, exchanged(): return lax.ppermute(value, AXES, [(s, s ^ mask) for s in range(devices)])  2.79 us
    pallas_call x1, Pallas kernels, final(): pl.pallas_call(final_kernel, out_shape=jax.ShapeDtypeStruct((64, 8192), F...  1.88 us
    pallas_call x1, Pallas kernels, lifts(): pl.pallas_call(lift_kernel, out_shape=jax.ShapeDtypeStruct((9, 64, 64), F...  1.66 us
    pallas_call x1, Pallas kernels, upper(): pl.pallas_call(upper_kernel, out_shape=jax.ShapeDtypeStruct((128, 1024),...  1.18 us
  transfers between devices with their start and end apart: 10, of which 3 were waited for; matrix products, arithmetic and copies ran while one was open for 0% of the time, Pallas kernels for 29%

profile of v4, /device:TPU:24, one launch (start us, length us, event | category | flops | bytes accessed | tf_op | source)
XLA Modules:
  0.0 45.0 jit_solution(13752152509741570190)
XLA Ops:
  0.0 6.3 %upward.1 = (f32[64,64]{1,0:T(8,128)S(1)}, f32[64,64]{1,0:T(8,128)S(1)}, f32[64,64]{1,0:T(8,128)S(1)}, f32[64,3968]{1,0:T(8,128)S(1)}, bf16[8,256,128]{2,1,0:T(8...) custom-call(s32[1]{0:T(128)} %bitcast.device, bf16[64,64,128]{2,1,0:T(8,128)(2,1)} %bitcast.24, ...), custom_call_target="tpu_custom_call" | custom-call | flops 8000000000 | bytes 65536 | tf_op jit(solution)/shard_map/upward/pallas_call | solution.py:176
  6.4 0.9 %near.4.near_in = f32[64,2048]{1,0:T(8,128)S(1)} custom-call(f32[64,64]{1,0:T(8,128)S(1)} %get-tuple-element.27.mine.after, f32[3,8192]{1,0:T(4,128)S(1)} %copy-done.6, bf16[64,8192]{1,0:T(8,128)(2,1)S(1)} %bitcast.19), custom_call_target="tpu_custom_call" | custom-call | flops 1500000000 | bytes 65536 | tf_op jit(solution)/shard_map/near/pallas_call | solution.py:402
  7.7 2.8 %collective-permute-start.3 = (f32[64,64]{1,0:T(8,128)S(1)}, f32[64,64]{1,0:T(8,128)S(1)}, u32[]{:S(2)}, u32[]{:S(2)}) collective-permute-start(f32[64,64]{1,0:T(8,128)S(1)} %climb.4.after.own), channel_id=1, source_target_pairs={{0,6},{1,7},{2,4},{3,5},{4,2},{5,3},{6,0},{7,1},{8,14},{9,15},{10,... | collective-permute-start | bytes 49160 | tf_op jit(solution)/shard_map/ppermute | solution.py:618
  10.6 0.8 %collective-permute-start.2 = (f32[64,64]{1,0:T(8,128)S(1)}, f32[64,64]{1,0:T(8,128)S(1)}, u32[]{:S(2)}, u32[]{:S(2)}) collective-permute-start(f32[64,64]{1,0:T(8,128)S(1)} %climb.4.after.own), channel_id=1, source_target_pairs={{0,4},{1,5},{2,6},{3,7},{4,0},{5,1},{6,2},{7,3},{8,12},{9,13},{10,... | collective-permute-start | bytes 49160 | tf_op jit(solution)/shard_map/ppermute | solution.py:618
  11.4 0.5 %collective-permute-start.1 = (f32[64,64]{1,0:T(8,128)S(1)}, f32[64,64]{1,0:T(8,128)S(1)}, u32[]{:S(2)}, u32[]{:S(2)}) collective-permute-start(f32[64,64]{1,0:T(8,128)S(1)} %climb.4.after.own), channel_id=1, source_target_pairs={{0,2},{1,3},{2,0},{3,1},{4,6},{5,7},{6,4},{7,5},{8,10},{9,11},{10,... | collective-permute-start | bytes 49160 | tf_op jit(solution)/shard_map/ppermute | solution.py:618
  11.9 0.9 %near.5.near_in = f32[64,2048]{1,0:T(8,128)S(1)} custom-call(f32[64,64]{1,0:T(8,128)S(1)} %climb.4.after.own, f32[3,8192]{1,0:T(4,128)S(1)} %copy-done.6, bf16[64,8192]{1,0:T(8,128)(2,1)S(1)} %bitcast.20), custom_call_target="tpu_custom_call" | custom-call | flops 1500000000 | bytes 65536 | tf_op jit(solution)/shard_map/near/pallas_call | solution.py:402
  12.9 0.9 %second_pick.1 = (f32[8,64,64]{2,1,0:T(8,128)S(1)}, f32[6,64,64]{2,1,0:T(8,128)S(1)}, f32[6,64,64]{2,1,0:T(8,128)S(1)}) custom-call(f32[64,64]{1,0:T(8,128)S(1)} %climb.4.after.own, s32[1]{0:T(128)} %bitcast.device, bf16[64,64,508]{2,1,0:T(8,128)(2,1)S(1)} %bitcast.16), custom_call_target="tpu_custom_call" | custom-call | flops 1000000000 | bytes 65536 | tf_op jit(solution)/shard_map/second_pick/pallas_call | solution.py:320
  13.8 2.2 %collective-permute-done.2.b = f32[64,64]{1,0:T(8,128)S(1)} collective-permute-done((f32[64,64]{1,0:T(8,128)S(1)}, f32[64,64]{1,0:T(8,128)S(1)}, u32[]{:S(2)}, u32[]{:S(2)}) %collective-permute-start.2) | collective-permute-done | bytes 16416 | tf_op jit(solution)/shard_map/ppermute | solution.py:618
  16.2 2.0 %collective-permute-start.4 = (f32[64,64]{1,0:T(8,128)S(1)}, f32[64,64]{1,0:T(8,128)S(1)}, u32[]{:S(2)}, u32[]{:S(2)}) collective-permute-start(f32[64,64]{1,0:T(8,128)S(1)} %get-tuple-element.29.after.mine), channel_id=1, source_target_pairs={{0,8},{1,9},{2,10},{3,11},{4,12},{5,13},{6,14},{7,15},{8,0},{9,1},... | collective-permute-start | bytes 49160 | tf_op jit(solution)/shard_map/ppermute | solution.py:618
  18.2 1.7 %lifts.1.lift = f32[9,64,64]{2,1,0:T(8,128)S(1)} custom-call(f32[64,64]{1,0:T(8,128)S(1)} %get-tuple-element.29.after.mine, s32[1]{0:T(128)} %bitcast.device, f32[64,64]{1,0:T(8,128)S(1)} %get-tuple-element.25.own.own0, f32[8,64,64]{2,1,0:T(8,128)S(1)} %get-tuple-element.30.own, bf16[64,64,255]{2,1,0:T(8,128)(2,1)S(1)} %bitcast.17), custom_call_target="tpu_custom_call" | custom-call | flops 2000000000 | bytes 65536 | tf_op jit(solution)/shard_map/lifts/pallas_call | solution.py:385
  19.9 0.3 collective-permute-done.4.other.refs_3_
  20.3 3.4 %collective-permute-start.5 = (f32[64,64]{1,0:T(8,128)S(1)}, f32[64,64]{1,0:T(8,128)S(1)}, u32[]{:S(2)}, u32[]{:S(2)}) collective-permute-start(f32[64,64]{1,0:T(8,128)S(1)} %climb.5.mine.after), channel_id=1, source_target_pairs={{0,16},{1,17},{2,18},{3,19},{4,20},{5,21},{6,22},{7,23},{8,24},{9,... | collective-permute-start | bytes 49160 | tf_op jit(solution)/shard_map/ppermute | solution.py:618
  23.7 0.9 %near.6.near_in = f32[64,2048]{1,0:T(8,128)S(1)} custom-call(f32[64,64]{1,0:T(8,128)S(1)} %climb.5.mine.after, f32[3,8192]{1,0:T(4,128)S(1)} %copy-done.6, bf16[64,8192]{1,0:T(8,128)(2,1)S(1)} %bitcast.21), custom_call_target="tpu_custom_call" | custom-call | flops 1500000000 | bytes 65536 | tf_op jit(solution)/shard_map/near/pallas_call | solution.py:402
  24.7 1.2 %upper.1.state3 = f32[128,1024]{1,0:T(8,128)S(1)} custom-call(f32[64,64]{1,0:T(8,128)S(1)} %climb.5.mine.after, bf16[31,64,64]{2,1,0:T(8,128)(2,1)S(1)} %bitcast.10, f32[64,3968]{1,0:T(8,128)S(1)} %get-tuple-element.33.levels, bf16[8,256,128]{2,1,0:T(8,128)(2,1)S(1)} %get-tuple-element.34.quads), custom_call_target="tpu_custom_call" | custom-call | flops 1500000000 | bytes 65536 | tf_op jit(solution)/shard_map/upper/pallas_call | solution.py:467
  26.0 5.9 %collective-permute-start.6 = (f32[64,64]{1,0:T(8,128)S(1)}, f32[64,64]{1,0:T(8,128)S(1)}, u32[]{:S(2)}, u32[]{:S(2)}) collective-permute-start(f32[64,64]{1,0:T(8,128)S(1)} %climb.6.mine.after), channel_id=1, source_target_pairs={{0,48},{1,49},{2,50},{3,51},{4,52},{5,53},{6,54},{7,55},{8,56},{9,... | collective-permute-start | bytes 49160 | tf_op jit(solution)/shard_map/ppermute | solution.py:618
  32.0 0.9 %near.7.near_in = f32[64,2048]{1,0:T(8,128)S(1)} custom-call(f32[64,64]{1,0:T(8,128)S(1)} %climb.6.mine.after, f32[3,8192]{1,0:T(4,128)S(1)} %copy-done.6, bf16[64,8192]{1,0:T(8,128)(2,1)S(1)} %bitcast.22), custom_call_target="tpu_custom_call" | custom-call | flops 1500000000 | bytes 65536 | tf_op jit(solution)/shard_map/near/pallas_call | solution.py:402
  32.9 1.4 %lower.4 = (f32[64,2048]{1,0:T(8,128)S(1)}, bf16[128,2048]{1,0:T(8,128)(2,1)S(1)}) custom-call(f32[64,64]{1,0:T(8,128)S(1)} %climb.6.mine.after, f32[128,1024]{1,0:T(8,128)S(1)} %upper.1.state3, f32[64,2048]{1,0:T(8,128)S(1)} %near.4.near_in, bf16[31,64,64]{2,1,0:T(8,128)(2,1)S(1)} %bitcast.11, f32[64,3968]{1,0:T(8,128)S(1)} %get-tuple-element.33.levels, ...), custom_call_target="tpu_custom_call" | custom-call | flops 1500000000 | bytes 65536 | tf_op jit(solution)/shard_map/lower/pallas_call | solution.py:516
  34.5 0.3 collective-permute-start.9
  34.7 2.6 %collective-permute-start.8 = (f32[64,64]{1,0:T(8,128)S(1)}, f32[64,64]{1,0:T(8,128)S(1)}, u32[]{:S(2)}, u32[]{:S(2)}) collective-permute-start(f32[64,64]{1,0:T(8,128)S(1)} %climb.7.after), channel_id=1, source_target_pairs={{0,128},{1,129},{2,130},{3,131},{4,132},{5,133},{6,134},{7,135},{8... | collective-permute-start | bytes 49160 | tf_op jit(solution)/shard_map/ppermute | solution.py:618
  37.3 1.3 %collective-permute-start.7 = (f32[64,64]{1,0:T(8,128)S(1)}, f32[64,64]{1,0:T(8,128)S(1)}, u32[]{:S(2)}, u32[]{:S(2)}) collective-permute-start(f32[64,64]{1,0:T(8,128)S(1)} %climb.7.after), channel_id=1, source_target_pairs={{0,64},{1,65},{2,66},{3,67},{4,68},{5,69},{6,70},{7,71},{8,72},{9,... | collective-permute-start | bytes 49160 | tf_op jit(solution)/shard_map/ppermute | solution.py:618
  38.6 1.4 %lower.7 = (f32[64,2048]{1,0:T(8,128)S(1)}, bf16[128,2048]{1,0:T(8,128)(2,1)S(1)}) custom-call(f32[64,64]{1,0:T(8,128)S(1)} %climb.7.after, f32[128,1024]{1,0:T(8,128)S(1)} %upper.1.state3, f32[64,2048]{1,0:T(8,128)S(1)} %near.7.near_in, bf16[31,64,64]{2,1,0:T(8,128)(2,1)S(1)} %bitcast.12, f32[64,3968]{1,0:T(8,128)S(1)} %get-tuple-element.33.levels, ...), custom_call_target="tpu_custom_call" | custom-call | flops 1500000000 | bytes 65536 | tf_op jit(solution)/shard_map/lower/pallas_call | solution.py:516
  40.0 1.4 %lower.6 = (f32[64,2048]{1,0:T(8,128)S(1)}, bf16[128,2048]{1,0:T(8,128)(2,1)S(1)}) custom-call(f32[64,64]{1,0:T(8,128)S(1)} %climb.7.after, f32[128,1024]{1,0:T(8,128)S(1)} %upper.1.state3, f32[64,2048]{1,0:T(8,128)S(1)} %near.6.near_in, bf16[31,64,64]{2,1,0:T(8,128)(2,1)S(1)} %bitcast.13, f32[64,3968]{1,0:T(8,128)S(1)} %get-tuple-element.33.levels, ...), custom_call_target="tpu_custom_call" | custom-call | flops 1500000000 | bytes 65536 | tf_op jit(solution)/shard_map/lower/pallas_call | solution.py:516
  41.4 1.4 %lower.5 = (f32[64,2048]{1,0:T(8,128)S(1)}, bf16[128,2048]{1,0:T(8,128)(2,1)S(1)}) custom-call(f32[64,64]{1,0:T(8,128)S(1)} %climb.7.after, f32[128,1024]{1,0:T(8,128)S(1)} %upper.1.state3, f32[64,2048]{1,0:T(8,128)S(1)} %near.5.near_in, bf16[31,64,64]{2,1,0:T(8,128)(2,1)S(1)} %bitcast.14, f32[64,3968]{1,0:T(8,128)S(1)} %get-tuple-element.33.levels, ...), custom_call_target="tpu_custom_call" | custom-call | flops 1500000000 | bytes 65536 | tf_op jit(solution)/shard_map/lower/pallas_call | solution.py:516
  43.0 1.9 %final.1 = f32[64,8192]{1,0:T(8,128)} custom-call(f32[9,64,64]{2,1,0:T(8,128)S(1)} %lifts.1.lift, f32[64,64]{1,0:T(8,128)S(1)} %partial_field.1.partial, f32[64,64]{1,0:T(8,128)S(1)} %collective-permute-done.7.refs_0_, f32[64,64]{1,0:T(8,128)S(1)} %collective-permute-done.8.refs_1_, f32[64,64]{1,0:T(8,128)S(1)} %collective-permute-done.9.refs_2_, ...), custom_call_target="tpu_custom_call" | custom-call | flops 2000000000 | bytes 65536 | tf_op jit(solution)/shard_map/final/pallas_call | solution.py:585
  (29 shorter events, 1.3 us)
Async XLA Ops:
  0.0 6.4 %copy-start.5 = (bf16[8192,64]{0,1:T(8,128)(2,1)S(1)}, bf16[8192,64]{0,1:T(8,128)(2,1)}, u32[]{:S(2)}) copy-start(bf16[8192,64]{0,1:T(8,128)(2,1)} %param.8) | copy-start | bytes 3145732
  0.0 6.4 %copy-start.6 = (f32[3,8192]{1,0:T(4,128)S(1)}, f32[3,8192]{1,0:T(4,128)}, u32[]{:S(2)}) copy-start(f32[3,8192]{1,0:T(4,128)} %coords.7) | copy-start | bytes 294916
  6.3 1.3 %collective-permute-start = (f32[64,64]{1,0:T(8,128)S(1)}, f32[64,64]{1,0:T(8,128)S(1)}, u32[]{:S(2)}, u32[]{:S(2)}) collective-permute-start(f32[64,64]{1,0:T(8,128)S(1)} %get-tuple-element.27.mine.after), channel_id=1, source_target_pairs={{0,1},{1,0},{2,3},{3,2},{4,5},{5,4},{6,7},{7,6},{8,9},{9,8},{10,11... | collective-permute-start | bytes 49160 | tf_op jit(solution)/shard_map/ppermute | solution.py:618
  7.7 5.2 %copy-start.3 = (bf16[508,64,64]{0,2,1:T(8,128)(2,1)S(1)}, bf16[508,64,64]{0,2,1:T(8,128)(2,1)}, u32[]{:S(2)}) copy-start(bf16[508,64,64]{0,2,1:T(8,128)(2,1)} %param.12) | copy-start | bytes 12484612
  7.7 6.0 %collective-permute-start.3 = (f32[64,64]{1,0:T(8,128)S(1)}, f32[64,64]{1,0:T(8,128)S(1)}, u32[]{:S(2)}, u32[]{:S(2)}) collective-permute-start(f32[64,64]{1,0:T(8,128)S(1)} %climb.4.after.own), channel_id=1, source_target_pairs={{0,6},{1,7},{2,4},{3,5},{4,2},{5,3},{6,0},{7,1},{8,14},{9,15},{10,... | collective-permute-start | bytes 49160 | tf_op jit(solution)/shard_map/ppermute | solution.py:618
  10.6 5.4 %collective-permute-start.2 = (f32[64,64]{1,0:T(8,128)S(1)}, f32[64,64]{1,0:T(8,128)S(1)}, u32[]{:S(2)}, u32[]{:S(2)}) collective-permute-start(f32[64,64]{1,0:T(8,128)S(1)} %climb.4.after.own), channel_id=1, source_target_pairs={{0,4},{1,5},{2,6},{3,7},{4,0},{5,1},{6,2},{7,3},{8,12},{9,13},{10,... | collective-permute-start | bytes 49160 | tf_op jit(solution)/shard_map/ppermute | solution.py:618
  11.4 4.6 %collective-permute-start.1 = (f32[64,64]{1,0:T(8,128)S(1)}, f32[64,64]{1,0:T(8,128)S(1)}, u32[]{:S(2)}, u32[]{:S(2)}) collective-permute-start(f32[64,64]{1,0:T(8,128)S(1)} %climb.4.after.own), channel_id=1, source_target_pairs={{0,2},{1,3},{2,0},{3,1},{4,6},{5,7},{6,4},{7,5},{8,10},{9,11},{10,... | collective-permute-start | bytes 49160 | tf_op jit(solution)/shard_map/ppermute | solution.py:618
  12.9 5.3 %copy-start.4 = (bf16[255,64,64]{0,2,1:T(8,128)(2,1)S(1)}, bf16[255,64,64]{0,2,1:T(8,128)(2,1)}, u32[]{:S(2)}) copy-start(bf16[255,64,64]{0,2,1:T(8,128)(2,1)} %param.13) | copy-start | bytes 6266884
  16.2 4.0 %collective-permute-start.4 = (f32[64,64]{1,0:T(8,128)S(1)}, f32[64,64]{1,0:T(8,128)S(1)}, u32[]{:S(2)}, u32[]{:S(2)}) collective-permute-start(f32[64,64]{1,0:T(8,128)S(1)} %get-tuple-element.29.after.mine), channel_id=1, source_target_pairs={{0,8},{1,9},{2,10},{3,11},{4,12},{5,13},{6,14},{7,15},{8,0},{9,1},... | collective-permute-start | bytes 49160 | tf_op jit(solution)/shard_map/ppermute | solution.py:618
  20.3 4.3 %copy-start.2 = (bf16[1,31,64,64]{3,2,1,0:T(8,128)(2,1)S(1)}, bf16[1,31,64,64]{3,2,1,0:T(8,128)(2,1)}, u32[]{:S(2)}) copy-start(bf16[1,31,64,64]{3,2,1,0:T(8,128)(2,1)} %param.11) | copy-start | bytes 761860
  20.3 5.5 %collective-permute-start.5 = (f32[64,64]{1,0:T(8,128)S(1)}, f32[64,64]{1,0:T(8,128)S(1)}, u32[]{:S(2)}, u32[]{:S(2)}) collective-permute-start(f32[64,64]{1,0:T(8,128)S(1)} %climb.5.mine.after), channel_id=1, source_target_pairs={{0,16},{1,17},{2,18},{3,19},{4,20},{5,21},{6,22},{7,23},{8,24},{9,... | collective-permute-start | bytes 49160 | tf_op jit(solution)/shard_map/ppermute | solution.py:618
  25.9 7.1 %copy-start.1 = (bf16[64,128,128]{2,1,0:T(8,128)(2,1)S(1)}, bf16[64,128,128]{2,1,0:T(8,128)(2,1)}, u32[]{:S(2)}) copy-start(bf16[64,128,128]{2,1,0:T(8,128)(2,1)} %get-tuple-element.36.pairs) | copy-start | bytes 6291460
  26.0 6.9 %copy-start = (bf16[56,256,128]{2,1,0:T(8,128)(2,1)S(1)}, bf16[56,256,128]{2,1,0:T(8,128)(2,1)}, u32[]{:S(2)}) copy-start(bf16[56,256,128]{2,1,0:T(8,128)(2,1)} %get-tuple-element.35.quads) | copy-start | bytes 11010052
  26.0 8.3 %collective-permute-start.6 = (f32[64,64]{1,0:T(8,128)S(1)}, f32[64,64]{1,0:T(8,128)S(1)}, u32[]{:S(2)}, u32[]{:S(2)}) collective-permute-start(f32[64,64]{1,0:T(8,128)S(1)} %climb.6.mine.after), channel_id=1, source_target_pairs={{0,48},{1,49},{2,50},{3,51},{4,52},{5,53},{6,54},{7,55},{8,56},{9,... | collective-permute-start | bytes 49160 | tf_op jit(solution)/shard_map/ppermute | solution.py:618
  34.5 8.5 %collective-permute-start.9 = (f32[64,64]{1,0:T(8,128)S(1)}, f32[64,64]{1,0:T(8,128)S(1)}, u32[]{:S(2)}, u32[]{:S(2)}) collective-permute-start(f32[64,64]{1,0:T(8,128)S(1)} %climb.7.after), channel_id=1, source_target_pairs={{0,192},{1,193},{2,194},{3,195},{4,196},{5,197},{6,198},{7,199},{8... | collective-permute-start | bytes 49160 | tf_op jit(solution)/shard_map/ppermute | solution.py:618
  34.7 8.3 %collective-permute-start.8 = (f32[64,64]{1,0:T(8,128)S(1)}, f32[64,64]{1,0:T(8,128)S(1)}, u32[]{:S(2)}, u32[]{:S(2)}) collective-permute-start(f32[64,64]{1,0:T(8,128)S(1)} %climb.7.after), channel_id=1, source_target_pairs={{0,128},{1,129},{2,130},{3,131},{4,132},{5,133},{6,134},{7,135},{8... | collective-permute-start | bytes 49160 | tf_op jit(solution)/shard_map/ppermute | solution.py:618
  37.3 5.7 %collective-permute-start.7 = (f32[64,64]{1,0:T(8,128)S(1)}, f32[64,64]{1,0:T(8,128)S(1)}, u32[]{:S(2)}, u32[]{:S(2)}) collective-permute-start(f32[64,64]{1,0:T(8,128)S(1)} %climb.7.after), channel_id=1, source_target_pairs={{0,64},{1,65},{2,66},{3,67},{4,68},{5,69},{6,70},{7,71},{8,72},{9,... | collective-permute-start | bytes 49160 | tf_op jit(solution)/shard_map/ppermute | solution.py:618

commit v5 on v4

--- a/solution.py
+++ b/solution.py
@@ -107,11 +107,11 @@
     for k in range(len(steps) + UP_DEPTH):
         if k < 16:
             spread(transfer, 126, 128, slab2, [2 * k, 2 * k + 1])
-        if k == 47:
+        if k == 51:
             loads[6].wait()
             first_pick = transfer_pick(device[0], [0], lane0, 128)
-        if 47 <= k < 63:
-            pick_row(table0, first_pick, picks, k - 47)
+        if 51 <= k < 67:
+            pick_row(table0, first_pick, picks, k - 51)
         if k < len(steps):
             level, q = steps[k]
             first = NODE_AT[level] + 4 * q
@@ -165,8 +165,8 @@
 
 UP_MIB = 52
 WINDOW_MIB = 12
-UP_DEPTH = 4
-DEPTH = 2
+UP_DEPTH = 8
+DEPTH = 3
 IN_VMEM = pl.BlockSpec(memory_space=VMEM)
 IN_HBM = pl.BlockSpec(memory_space=pl.ANY)
 IN_SMEM = pl.BlockSpec(memory_space=pltpu.SMEM)

time: 45.2 us -> 44.9 us (level)
  no operation moved by 1% of the time
where the time goes in v5:
time: 44.9 us; the launch traced here: 44.8 us
  Pallas kernels  21.7 us (48%)
  starting transfers between devices  19.8 us (44%)
  waiting for transfers between devices  2.87 us (6%)
    ppermute x10, starting transfers between devices, exchanged(): return lax.ppermute(value, AXES, [(s, s ^ mask) for s in range(devices)])  19.8 us
    pallas_call x1, Pallas kernels, upward(): pl.pallas_call(up_kernel, out_shape=[jax.ShapeDtypeStruct((64, 64), F32),...  6.23 us
    pallas_call x4, Pallas kernels, lower_piece(): pl.pallas_call(functools.partial(lower_kernel, piece), out_shape=[jax.Sha...  5.32 us
    pallas_call x4, Pallas kernels, near(): pl.pallas_call(functools.partial(near_kernel, piece), out_shape=jax.Shape...  3.63 us
    ppermute x10, waiting for transfers between devices, exchanged(): return lax.ppermute(value, AXES, [(s, s ^ mask) for s in range(devices)])  2.87 us
    pallas_call x1, Pallas kernels, final(): pl.pallas_call(final_kernel, out_shape=jax.ShapeDtypeStruct((64, 8192), F...  1.89 us
    pallas_call x1, Pallas kernels, lifts(): pl.pallas_call(lift_kernel, out_shape=jax.ShapeDtypeStruct((9, 64, 64), F...  1.66 us
    pallas_call x1, Pallas kernels, upper(): pl.pallas_call(upper_kernel, out_shape=jax.ShapeDtypeStruct((128, 1024),...  1.18 us
  transfers between devices with their start and end apart: 10, of which 3 were waited for; matrix products, arithmetic and copies ran while one was open for 0% of the time, Pallas kernels for 29%

profile of v5, /device:TPU:24, one launch (start us, length us, event | category | flops | bytes accessed | tf_op | source)
XLA Modules:
  0.0 44.8 jit_solution(12829612027931622692)
XLA Ops:
  0.0 6.2 %upward.1 = (f32[64,64]{1,0:T(8,128)S(1)}, f32[64,64]{1,0:T(8,128)S(1)}, f32[64,64]{1,0:T(8,128)S(1)}, f32[64,3968]{1,0:T(8,128)S(1)}, bf16[8,256,128]{2,1,0:T(8...) custom-call(s32[1]{0:T(128)} %bitcast.device, bf16[64,64,128]{2,1,0:T(8,128)(2,1)} %bitcast.24, ...), custom_call_target="tpu_custom_call" | custom-call | flops 8000000000 | bytes 65536 | tf_op jit(solution)/shard_map/upward/pallas_call | solution.py:176
  6.4 0.9 %near.4.near_in = f32[64,2048]{1,0:T(8,128)S(1)} custom-call(f32[64,64]{1,0:T(8,128)S(1)} %get-tuple-element.27.mine.after, f32[3,8192]{1,0:T(4,128)S(1)} %copy-done.6, bf16[64,8192]{1,0:T(8,128)(2,1)S(1)} %bitcast.19), custom_call_target="tpu_custom_call" | custom-call | flops 1500000000 | bytes 65536 | tf_op jit(solution)/shard_map/near/pallas_call | solution.py:402
  7.3 0.3 collective-permute-done.other.refs_0_
  7.7 2.8 %collective-permute-start.3 = (f32[64,64]{1,0:T(8,128)S(1)}, f32[64,64]{1,0:T(8,128)S(1)}, u32[]{:S(2)}, u32[]{:S(2)}) collective-permute-start(f32[64,64]{1,0:T(8,128)S(1)} %climb.4.after.own), channel_id=1, source_target_pairs={{0,6},{1,7},{2,4},{3,5},{4,2},{5,3},{6,0},{7,1},{8,14},{9,15},{10,... | collective-permute-start | bytes 49160 | tf_op jit(solution)/shard_map/ppermute | solution.py:618
  10.5 0.8 %collective-permute-start.2 = (f32[64,64]{1,0:T(8,128)S(1)}, f32[64,64]{1,0:T(8,128)S(1)}, u32[]{:S(2)}, u32[]{:S(2)}) collective-permute-start(f32[64,64]{1,0:T(8,128)S(1)} %climb.4.after.own), channel_id=1, source_target_pairs={{0,4},{1,5},{2,6},{3,7},{4,0},{5,1},{6,2},{7,3},{8,12},{9,13},{10,... | collective-permute-start | bytes 49160 | tf_op jit(solution)/shard_map/ppermute | solution.py:618
  11.3 0.5 %collective-permute-start.1 = (f32[64,64]{1,0:T(8,128)S(1)}, f32[64,64]{1,0:T(8,128)S(1)}, u32[]{:S(2)}, u32[]{:S(2)}) collective-permute-start(f32[64,64]{1,0:T(8,128)S(1)} %climb.4.after.own), channel_id=1, source_target_pairs={{0,2},{1,3},{2,0},{3,1},{4,6},{5,7},{6,4},{7,5},{8,10},{9,11},{10,... | collective-permute-start | bytes 49160 | tf_op jit(solution)/shard_map/ppermute | solution.py:618
  11.9 0.9 %near.5.near_in = f32[64,2048]{1,0:T(8,128)S(1)} custom-call(f32[64,64]{1,0:T(8,128)S(1)} %climb.4.after.own, f32[3,8192]{1,0:T(4,128)S(1)} %copy-done.6, bf16[64,8192]{1,0:T(8,128)(2,1)S(1)} %bitcast.20), custom_call_target="tpu_custom_call" | custom-call | flops 1500000000 | bytes 65536 | tf_op jit(solution)/shard_map/near/pallas_call | solution.py:402
  12.8 0.9 %second_pick.1 = (f32[8,64,64]{2,1,0:T(8,128)S(1)}, f32[6,64,64]{2,1,0:T(8,128)S(1)}, f32[6,64,64]{2,1,0:T(8,128)S(1)}) custom-call(f32[64,64]{1,0:T(8,128)S(1)} %climb.4.after.own, s32[1]{0:T(128)} %bitcast.device, bf16[64,64,508]{2,1,0:T(8,128)(2,1)S(1)} %bitcast.16), custom_call_target="tpu_custom_call" | custom-call | flops 1000000000 | bytes 65536 | tf_op jit(solution)/shard_map/second_pick/pallas_call | solution.py:320
  13.7 2.3 %collective-permute-done.2.b = f32[64,64]{1,0:T(8,128)S(1)} collective-permute-done((f32[64,64]{1,0:T(8,128)S(1)}, f32[64,64]{1,0:T(8,128)S(1)}, u32[]{:S(2)}, u32[]{:S(2)}) %collective-permute-start.2) | collective-permute-done | bytes 16416 | tf_op jit(solution)/shard_map/ppermute | solution.py:618
  16.1 2.0 %collective-permute-start.4 = (f32[64,64]{1,0:T(8,128)S(1)}, f32[64,64]{1,0:T(8,128)S(1)}, u32[]{:S(2)}, u32[]{:S(2)}) collective-permute-start(f32[64,64]{1,0:T(8,128)S(1)} %get-tuple-element.29.after.mine), channel_id=1, source_target_pairs={{0,8},{1,9},{2,10},{3,11},{4,12},{5,13},{6,14},{7,15},{8,0},{9,1},... | collective-permute-start | bytes 49160 | tf_op jit(solution)/shard_map/ppermute | solution.py:618
  18.2 1.7 %lifts.1.lift = f32[9,64,64]{2,1,0:T(8,128)S(1)} custom-call(f32[64,64]{1,0:T(8,128)S(1)} %get-tuple-element.29.after.mine, s32[1]{0:T(128)} %bitcast.device, f32[64,64]{1,0:T(8,128)S(1)} %get-tuple-element.25.own.own0, f32[8,64,64]{2,1,0:T(8,128)S(1)} %get-tuple-element.30.own, bf16[64,64,255]{2,1,0:T(8,128)(2,1)S(1)} %bitcast.17), custom_call_target="tpu_custom_call" | custom-call | flops 2000000000 | bytes 65536 | tf_op jit(solution)/shard_map/lifts/pallas_call | solution.py:385
  19.8 0.3 collective-permute-done.4.other.refs_3_
  20.3 3.4 %collective-permute-start.5 = (f32[64,64]{1,0:T(8,128)S(1)}, f32[64,64]{1,0:T(8,128)S(1)}, u32[]{:S(2)}, u32[]{:S(2)}) collective-permute-start(f32[64,64]{1,0:T(8,128)S(1)} %climb.5.mine.after), channel_id=1, source_target_pairs={{0,16},{1,17},{2,18},{3,19},{4,20},{5,21},{6,22},{7,23},{8,24},{9,... | collective-permute-start | bytes 49160 | tf_op jit(solution)/shard_map/ppermute | solution.py:618
  23.7 0.9 %near.6.near_in = f32[64,2048]{1,0:T(8,128)S(1)} custom-call(f32[64,64]{1,0:T(8,128)S(1)} %climb.5.mine.after, f32[3,8192]{1,0:T(4,128)S(1)} %copy-done.6, bf16[64,8192]{1,0:T(8,128)(2,1)S(1)} %bitcast.21), custom_call_target="tpu_custom_call" | custom-call | flops 1500000000 | bytes 65536 | tf_op jit(solution)/shard_map/near/pallas_call | solution.py:402
  24.6 1.2 %upper.1.state3 = f32[128,1024]{1,0:T(8,128)S(1)} custom-call(f32[64,64]{1,0:T(8,128)S(1)} %climb.5.mine.after, bf16[31,64,64]{2,1,0:T(8,128)(2,1)S(1)} %bitcast.10, f32[64,3968]{1,0:T(8,128)S(1)} %get-tuple-element.33.levels, bf16[8,256,128]{2,1,0:T(8,128)(2,1)S(1)} %get-tuple-element.34.quads), custom_call_target="tpu_custom_call" | custom-call | flops 1500000000 | bytes 65536 | tf_op jit(solution)/shard_map/upper/pallas_call | solution.py:467
  25.9 6.0 %collective-permute-start.6 = (f32[64,64]{1,0:T(8,128)S(1)}, f32[64,64]{1,0:T(8,128)S(1)}, u32[]{:S(2)}, u32[]{:S(2)}) collective-permute-start(f32[64,64]{1,0:T(8,128)S(1)} %climb.6.mine.after), channel_id=1, source_target_pairs={{0,48},{1,49},{2,50},{3,51},{4,52},{5,53},{6,54},{7,55},{8,56},{9,... | collective-permute-start | bytes 49160 | tf_op jit(solution)/shard_map/ppermute | solution.py:618
  31.9 0.9 %near.7.near_in = f32[64,2048]{1,0:T(8,128)S(1)} custom-call(f32[64,64]{1,0:T(8,128)S(1)} %climb.6.mine.after, f32[3,8192]{1,0:T(4,128)S(1)} %copy-done.6, bf16[64,8192]{1,0:T(8,128)(2,1)S(1)} %bitcast.22), custom_call_target="tpu_custom_call" | custom-call | flops 1500000000 | bytes 65536 | tf_op jit(solution)/shard_map/near/pallas_call | solution.py:402
  32.9 1.3 %lower.4 = (f32[64,2048]{1,0:T(8,128)S(1)}, bf16[128,2048]{1,0:T(8,128)(2,1)S(1)}) custom-call(f32[64,64]{1,0:T(8,128)S(1)} %climb.6.mine.after, f32[128,1024]{1,0:T(8,128)S(1)} %upper.1.state3, f32[64,2048]{1,0:T(8,128)S(1)} %near.4.near_in, bf16[31,64,64]{2,1,0:T(8,128)(2,1)S(1)} %bitcast.11, f32[64,3968]{1,0:T(8,128)S(1)} %get-tuple-element.33.levels, ...), custom_call_target="tpu_custom_call" | custom-call | flops 1500000000 | bytes 65536 | tf_op jit(solution)/shard_map/lower/pallas_call | solution.py:516
  34.6 2.6 %collective-permute-start.8 = (f32[64,64]{1,0:T(8,128)S(1)}, f32[64,64]{1,0:T(8,128)S(1)}, u32[]{:S(2)}, u32[]{:S(2)}) collective-permute-start(f32[64,64]{1,0:T(8,128)S(1)} %climb.7.after), channel_id=1, source_target_pairs={{0,128},{1,129},{2,130},{3,131},{4,132},{5,133},{6,134},{7,135},{8... | collective-permute-start | bytes 49160 | tf_op jit(solution)/shard_map/ppermute | solution.py:618
  37.2 1.3 %collective-permute-start.7 = (f32[64,64]{1,0:T(8,128)S(1)}, f32[64,64]{1,0:T(8,128)S(1)}, u32[]{:S(2)}, u32[]{:S(2)}) collective-permute-start(f32[64,64]{1,0:T(8,128)S(1)} %climb.7.after), channel_id=1, source_target_pairs={{0,64},{1,65},{2,66},{3,67},{4,68},{5,69},{6,70},{7,71},{8,72},{9,... | collective-permute-start | bytes 49160 | tf_op jit(solution)/shard_map/ppermute | solution.py:618
  38.5 1.3 %lower.7 = (f32[64,2048]{1,0:T(8,128)S(1)}, bf16[128,2048]{1,0:T(8,128)(2,1)S(1)}) custom-call(f32[64,64]{1,0:T(8,128)S(1)} %climb.7.after, f32[128,1024]{1,0:T(8,128)S(1)} %upper.1.state3, f32[64,2048]{1,0:T(8,128)S(1)} %near.7.near_in, bf16[31,64,64]{2,1,0:T(8,128)(2,1)S(1)} %bitcast.12, f32[64,3968]{1,0:T(8,128)S(1)} %get-tuple-element.33.levels, ...), custom_call_target="tpu_custom_call" | custom-call | flops 1500000000 | bytes 65536 | tf_op jit(solution)/shard_map/lower/pallas_call | solution.py:516
  39.8 1.3 %lower.6 = (f32[64,2048]{1,0:T(8,128)S(1)}, bf16[128,2048]{1,0:T(8,128)(2,1)S(1)}) custom-call(f32[64,64]{1,0:T(8,128)S(1)} %climb.7.after, f32[128,1024]{1,0:T(8,128)S(1)} %upper.1.state3, f32[64,2048]{1,0:T(8,128)S(1)} %near.6.near_in, bf16[31,64,64]{2,1,0:T(8,128)(2,1)S(1)} %bitcast.13, f32[64,3968]{1,0:T(8,128)S(1)} %get-tuple-element.33.levels, ...), custom_call_target="tpu_custom_call" | custom-call | flops 1500000000 | bytes 65536 | tf_op jit(solution)/shard_map/lower/pallas_call | solution.py:516
  41.1 1.3 %lower.5 = (f32[64,2048]{1,0:T(8,128)S(1)}, bf16[128,2048]{1,0:T(8,128)(2,1)S(1)}) custom-call(f32[64,64]{1,0:T(8,128)S(1)} %climb.7.after, f32[128,1024]{1,0:T(8,128)S(1)} %upper.1.state3, f32[64,2048]{1,0:T(8,128)S(1)} %near.5.near_in, bf16[31,64,64]{2,1,0:T(8,128)(2,1)S(1)} %bitcast.14, f32[64,3968]{1,0:T(8,128)S(1)} %get-tuple-element.33.levels, ...), custom_call_target="tpu_custom_call" | custom-call | flops 1500000000 | bytes 65536 | tf_op jit(solution)/shard_map/lower/pallas_call | solution.py:516
  42.8 1.9 %final.1 = f32[64,8192]{1,0:T(8,128)} custom-call(f32[9,64,64]{2,1,0:T(8,128)S(1)} %lifts.1.lift, f32[64,64]{1,0:T(8,128)S(1)} %partial_field.1.partial, f32[64,64]{1,0:T(8,128)S(1)} %collective-permute-done.7.refs_0_, f32[64,64]{1,0:T(8,128)S(1)} %collective-permute-done.8.refs_1_, f32[64,64]{1,0:T(8,128)S(1)} %collective-permute-done.9.refs_2_, ...), custom_call_target="tpu_custom_call" | custom-call | flops 2000000000 | bytes 65536 | tf_op jit(solution)/shard_map/final/pallas_call | solution.py:585
  (29 shorter events, 1.4 us)
Async XLA Ops:
  0.0 6.3 %copy-start.5 = (bf16[8192,64]{0,1:T(8,128)(2,1)S(1)}, bf16[8192,64]{0,1:T(8,128)(2,1)}, u32[]{:S(2)}) copy-start(bf16[8192,64]{0,1:T(8,128)(2,1)} %param.8) | copy-start | bytes 3145732
  0.0 6.3 %copy-start.6 = (f32[3,8192]{1,0:T(4,128)S(1)}, f32[3,8192]{1,0:T(4,128)}, u32[]{:S(2)}) copy-start(f32[3,8192]{1,0:T(4,128)} %coords.7) | copy-start | bytes 294916
  6.2 1.3 %collective-permute-start = (f32[64,64]{1,0:T(8,128)S(1)}, f32[64,64]{1,0:T(8,128)S(1)}, u32[]{:S(2)}, u32[]{:S(2)}) collective-permute-start(f32[64,64]{1,0:T(8,128)S(1)} %get-tuple-element.27.mine.after), channel_id=1, source_target_pairs={{0,1},{1,0},{2,3},{3,2},{4,5},{5,4},{6,7},{7,6},{8,9},{9,8},{10,11... | collective-permute-start | bytes 49160 | tf_op jit(solution)/shard_map/ppermute | solution.py:618
  7.7 5.1 %copy-start.3 = (bf16[508,64,64]{0,2,1:T(8,128)(2,1)S(1)}, bf16[508,64,64]{0,2,1:T(8,128)(2,1)}, u32[]{:S(2)}) copy-start(bf16[508,64,64]{0,2,1:T(8,128)(2,1)} %param.12) | copy-start | bytes 12484612
  7.7 6.0 %collective-permute-start.3 = (f32[64,64]{1,0:T(8,128)S(1)}, f32[64,64]{1,0:T(8,128)S(1)}, u32[]{:S(2)}, u32[]{:S(2)}) collective-permute-start(f32[64,64]{1,0:T(8,128)S(1)} %climb.4.after.own), channel_id=1, source_target_pairs={{0,6},{1,7},{2,4},{3,5},{4,2},{5,3},{6,0},{7,1},{8,14},{9,15},{10,... | collective-permute-start | bytes 49160 | tf_op jit(solution)/shard_map/ppermute | solution.py:618
  10.5 5.4 %collective-permute-start.2 = (f32[64,64]{1,0:T(8,128)S(1)}, f32[64,64]{1,0:T(8,128)S(1)}, u32[]{:S(2)}, u32[]{:S(2)}) collective-permute-start(f32[64,64]{1,0:T(8,128)S(1)} %climb.4.after.own), channel_id=1, source_target_pairs={{0,4},{1,5},{2,6},{3,7},{4,0},{5,1},{6,2},{7,3},{8,12},{9,13},{10,... | collective-permute-start | bytes 49160 | tf_op jit(solution)/shard_map/ppermute | solution.py:618
  11.3 4.6 %collective-permute-start.1 = (f32[64,64]{1,0:T(8,128)S(1)}, f32[64,64]{1,0:T(8,128)S(1)}, u32[]{:S(2)}, u32[]{:S(2)}) collective-permute-start(f32[64,64]{1,0:T(8,128)S(1)} %climb.4.after.own), channel_id=1, source_target_pairs={{0,2},{1,3},{2,0},{3,1},{4,6},{5,7},{6,4},{7,5},{8,10},{9,11},{10,... | collective-permute-start | bytes 49160 | tf_op jit(solution)/shard_map/ppermute | solution.py:618
  12.8 5.4 %copy-start.4 = (bf16[255,64,64]{0,2,1:T(8,128)(2,1)S(1)}, bf16[255,64,64]{0,2,1:T(8,128)(2,1)}, u32[]{:S(2)}) copy-start(bf16[255,64,64]{0,2,1:T(8,128)(2,1)} %param.13) | copy-start | bytes 6266884
  16.1 4.0 %collective-permute-start.4 = (f32[64,64]{1,0:T(8,128)S(1)}, f32[64,64]{1,0:T(8,128)S(1)}, u32[]{:S(2)}, u32[]{:S(2)}) collective-permute-start(f32[64,64]{1,0:T(8,128)S(1)} %get-tuple-element.29.after.mine), channel_id=1, source_target_pairs={{0,8},{1,9},{2,10},{3,11},{4,12},{5,13},{6,14},{7,15},{8,0},{9,1},... | collective-permute-start | bytes 49160 | tf_op jit(solution)/shard_map/ppermute | solution.py:618
  20.3 4.3 %copy-start.2 = (bf16[1,31,64,64]{3,2,1,0:T(8,128)(2,1)S(1)}, bf16[1,31,64,64]{3,2,1,0:T(8,128)(2,1)}, u32[]{:S(2)}) copy-start(bf16[1,31,64,64]{3,2,1,0:T(8,128)(2,1)} %param.11) | copy-start | bytes 761860
  20.3 5.5 %collective-permute-start.5 = (f32[64,64]{1,0:T(8,128)S(1)}, f32[64,64]{1,0:T(8,128)S(1)}, u32[]{:S(2)}, u32[]{:S(2)}) collective-permute-start(f32[64,64]{1,0:T(8,128)S(1)} %climb.5.mine.after), channel_id=1, source_target_pairs={{0,16},{1,17},{2,18},{3,19},{4,20},{5,21},{6,22},{7,23},{8,24},{9,... | collective-permute-start | bytes 49160 | tf_op jit(solution)/shard_map/ppermute | solution.py:618
  25.8 7.1 %copy-start.1 = (bf16[64,128,128]{2,1,0:T(8,128)(2,1)S(1)}, bf16[64,128,128]{2,1,0:T(8,128)(2,1)}, u32[]{:S(2)}) copy-start(bf16[64,128,128]{2,1,0:T(8,128)(2,1)} %get-tuple-element.36.pairs) | copy-start | bytes 6291460
  25.9 6.9 %copy-start = (bf16[56,256,128]{2,1,0:T(8,128)(2,1)S(1)}, bf16[56,256,128]{2,1,0:T(8,128)(2,1)}, u32[]{:S(2)}) copy-start(bf16[56,256,128]{2,1,0:T(8,128)(2,1)} %get-tuple-element.35.quads) | copy-start | bytes 11010052
  25.9 8.3 %collective-permute-start.6 = (f32[64,64]{1,0:T(8,128)S(1)}, f32[64,64]{1,0:T(8,128)S(1)}, u32[]{:S(2)}, u32[]{:S(2)}) collective-permute-start(f32[64,64]{1,0:T(8,128)S(1)} %climb.6.mine.after), channel_id=1, source_target_pairs={{0,48},{1,49},{2,50},{3,51},{4,52},{5,53},{6,54},{7,55},{8,56},{9,... | collective-permute-start | bytes 49160 | tf_op jit(solution)/shard_map/ppermute | solution.py:618
  34.3 8.4 %collective-permute-start.9 = (f32[64,64]{1,0:T(8,128)S(1)}, f32[64,64]{1,0:T(8,128)S(1)}, u32[]{:S(2)}, u32[]{:S(2)}) collective-permute-start(f32[64,64]{1,0:T(8,128)S(1)} %climb.7.after), channel_id=1, source_target_pairs={{0,192},{1,193},{2,194},{3,195},{4,196},{5,197},{6,198},{7,199},{8... | collective-permute-start | bytes 49160 | tf_op jit(solution)/shard_map/ppermute | solution.py:618
  34.6 8.1 %collective-permute-start.8 = (f32[64,64]{1,0:T(8,128)S(1)}, f32[64,64]{1,0:T(8,128)S(1)}, u32[]{:S(2)}, u32[]{:S(2)}) collective-permute-start(f32[64,64]{1,0:T(8,128)S(1)} %climb.7.after), channel_id=1, source_target_pairs={{0,128},{1,129},{2,130},{3,131},{4,132},{5,133},{6,134},{7,135},{8... | collective-permute-start | bytes 49160 | tf_op jit(solution)/shard_map/ppermute | solution.py:618
  37.2 5.6 %collective-permute-start.7 = (f32[64,64]{1,0:T(8,128)S(1)}, f32[64,64]{1,0:T(8,128)S(1)}, u32[]{:S(2)}, u32[]{:S(2)}) collective-permute-start(f32[64,64]{1,0:T(8,128)S(1)} %climb.7.after), channel_id=1, source_target_pairs={{0,64},{1,65},{2,66},{3,67},{4,68},{5,69},{6,70},{7,71},{8,72},{9,... | collective-permute-start | bytes 49160 | tf_op jit(solution)/shard_map/ppermute | solution.py:618
